TPU v7x, 512 devices: a whole 4x8x8 slice. The times are simulated.
512 devices in a mesh: outer: 16 (over y_lo, x), inner: 32 (over z, y_hi, core).
Axes of the slice: x: 4, y: 8 (y_hi: 2, y_lo: 4; y = y_hi * 4 + y_lo), z: 8, core: 2. Of those that a mesh axis runs over, the one named last changes fastest.
Arguments:
- queries: bfloat16 [32768, 1024], P(('outer', 'inner')), may hold values from -8 to 8
- key_rows: bfloat16 [32768, 1024], P(('outer', 'inner')), may hold values from -8 to 8
- value_rows: bfloat16 [32768, 1024], P(('outer', 'inner')), may hold values from -6 to 6
Outputs:
- attended: float32 [32768, 1024], P(('outer', 'inner'))
All inputs are finite; a program needn't handle non-finite values.
Results may differ from a plain program's by a relative error of at most 0.0021.
Values may be sent and summed in bfloat16 or wider, within the bound.
No kernel may reach another device: no remote copies, remote signals or barrier semaphores. Data moves between devices by JAX's collectives and lax.ppermute only.
A program may use at most 64 MiB of HBM per device.

v0:
```python
from functools import reduce

import jax
import jax.numpy as jnp
import numpy as np
from jax import lax
from jax.sharding import PartitionSpec as P

HEADS = 16


FLOOR_SCORE = -1e30


def side_by_side(arrays, axis, dim, along):
    ends, at = ([], 0)
    for a in arrays[:-1]:
        at += a.shape[along]
        ends.append(at)
    both = jnp.concatenate(arrays, axis=along)
    return tuple(jnp.split(lax.all_gather(both, axis, axis=dim, tiled=True), ends, axis=along))


def in_one_piece(arrays, axis, split_dim, concat_dim, along):
    widths = [a.shape[along] for a in arrays]
    both = jnp.concatenate(arrays, axis=along)
    filled = lax.all_to_all(both, axis, split_axis=split_dim, concat_axis=concat_dim, tiled=True)
    return tuple(jnp.split(filled, [sum(widths[:k]) for k in range(1, len(widths))], axis=along))


def side_by_side_2(arrays, axis, split_dim, concat_dim, along):
    columns = [a.reshape(*a.shape[:along], -1) for a in arrays]
    both = jnp.concatenate(columns, axis=along)
    filled, at, done = (
        lax.all_to_all(both, axis, split_axis=split_dim, concat_axis=concat_dim, tiled=True),
        0,
        [],
    )
    for a, column in zip(arrays, columns):
        section = filled[..., at : at + column.shape[along]]
        done.append(section.reshape(*section.shape[:along], *a.shape[along:]))
        at += column.shape[along]
    return tuple(done)


def divisor_block(length, limit):
    extent = min(length, limit)
    while length % extent:
        extent -= 1
    return extent


def fresh_state(count, rows, width):
    return (
        jnp.full((count, rows), FLOOR_SCORE, jnp.float32),
        jnp.zeros((count, rows), jnp.float32),
        jnp.zeros((count, rows, width), jnp.float32),
    )


def finish_state(state):
    row_max, denominator, summed = state
    return (summed / denominator[..., None], row_max + jnp.log(denominator))


def online_step(state, query_rows, query_rank, key_rows, value_rows, key_rank):
    row_max, denominator, summed = state
    scale = query_rows.shape[-1] ** (-0.5)
    scores = (
        jnp.einsum("inh,ibh->inb", query_rows, key_rows, preferred_element_type=jnp.float32) * scale
    )
    scores = jnp.where(key_rank[None, None, :] <= query_rank[None, :, None], scores, FLOOR_SCORE)
    new_max = jnp.maximum(row_max, jnp.max(scores, axis=2))
    weights = jnp.exp(scores - new_max[..., None])
    rescale = jnp.exp(row_max - new_max)
    denominator = denominator * rescale + jnp.sum(weights, axis=2)
    summed = summed * rescale[..., None] + jnp.einsum(
        "inb,ibh->inh", weights.astype(jnp.bfloat16), value_rows, preferred_element_type=jnp.float32
    )
    return (new_max, denominator, summed)


def attend_keys(state, query_rows, query_rank, key_rows, value_rows, key_rank, stop=None):
    length = key_rows.shape[1]
    block = divisor_block(length, 512)

    def advance(index, carry):
        start = index * block
        piece_keys = lax.dynamic_slice_in_dim(key_rows, start, block, 1)
        piece_values = lax.dynamic_slice_in_dim(value_rows, start, block, 1)
        piece_rank = lax.dynamic_slice_in_dim(key_rank, start, block, 0)
        return online_step(carry, query_rows, query_rank, piece_keys, piece_values, piece_rank)

    upper = length // block if stop is None else stop
    return lax.fori_loop(0, upper, advance, state)


def attend(query_rows, query_rank, key_rows, value_rows, key_rank):
    count, length, width = query_rows.shape
    block = divisor_block(length, 512)
    steps = length // block
    query_split = query_rows.reshape(count, steps, block, width).swapaxes(0, 1)
    rank_split = query_rank.reshape(steps, block)

    def one_block(pieces):
        state = attend_keys(
            fresh_state(count, block, width),
            pieces[0],
            pieces[1],
            key_rows,
            value_rows,
            key_rank,
            pieces[2] + 1,
        )
        return finish_state(state)

    outputs, lses = lax.map(
        one_block, (query_split, rank_split, jnp.arange(steps, dtype=jnp.int32))
    )
    return (
        outputs.swapaxes(0, 1).reshape(count, length, width),
        lses.swapaxes(0, 1).reshape(count, length),
    )


def merge_levels(parts):
    row_max = reduce(jnp.maximum, [lse for _, lse in parts])
    weights = [jnp.exp(lse - row_max) for _, lse in parts]
    denominator = reduce(jnp.add, weights)
    summed = reduce(
        jnp.add, [weight[..., None] * output for weight, (output, _) in zip(weights, parts)]
    )
    return (summed / denominator[..., None], row_max + jnp.log(denominator))


def on_device(queries, key_rows, value_rows):
    tokens, features = queries.shape
    heads = HEADS
    width = features // heads
    outer_count = lax.axis_size("outer")
    inner_count = lax.axis_size("inner")
    outer_index = lax.axis_index("outer")
    inner_index = lax.axis_index("inner")
    per_device = 4 * heads // inner_count
    quarter = tokens // 4
    sixteenth = tokens // 16
    class_len = quarter * inner_count
    far_len = sixteenth * inner_count

    def to_items(array):
        return (
            array.reshape(quarter, 4, heads, width)
            .transpose(2, 1, 0, 3)
            .reshape(4 * heads, quarter, width)
        )

    local_ranks = jnp.arange(tokens, dtype=jnp.int32)
    head_major = [
        a.reshape(tokens, heads, width).transpose(1, 0, 2) for a in (queries, key_rows, value_rows)
    ]
    near_out, near_lse = attend(
        head_major[0], local_ranks, head_major[1], head_major[2], local_ranks
    )
    near_out = near_out.transpose(1, 0, 2)
    near_lse = near_lse.T
    item_index = inner_index * per_device + jnp.arange(per_device, dtype=jnp.int32)
    band = item_index // 16
    far_query_rank = outer_index * far_len + jnp.arange(far_len, dtype=jnp.int32)
    pick = np.array(
        [head * 16 + head // 4 * 4 + residue for head in range(heads) for residue in range(4)],
        np.int32,
    )

    def to_sixteen(array):
        spread = (
            array.reshape(sixteenth, 16, heads, width)
            .transpose(2, 1, 0, 3)
            .reshape(16 * heads, sixteenth, width)
        )
        return jnp.take(spread, pick, axis=0)

    gathered_k, gathered_v = side_by_side(
        (to_sixteen(key_rows), to_sixteen(value_rows)), "outer", 1, 0
    )
    mid_q, mid_k, mid_v, far_k, far_v = (
        *in_one_piece(
            (to_items(queries), to_items(key_rows), to_items(value_rows)), "inner", 0, 1, 2
        ),
        *in_one_piece((gathered_k, gathered_v), "inner", 0, 1, 2),
    )
    split = mid_q.reshape(per_device, far_len, 4, width)
    picker = jnp.broadcast_to(band[:, None, None, None], (per_device, far_len, 1, width))
    far_q = jnp.take_along_axis(split, picker, axis=2)[:, :, 0, :]
    position = jnp.arange(far_k.shape[1], dtype=jnp.int32)
    far_key_rank = (
        position // sixteenth % outer_count * far_len
        + position // (outer_count * sixteenth) * sixteenth
        + position % sixteenth
    )
    far_state = attend_keys(
        fresh_state(per_device, far_len, width), far_q, far_query_rank, far_k, far_v, far_key_rank
    )
    far_out, far_lse = finish_state(far_state)
    class_ranks = jnp.arange(class_len, dtype=jnp.int32)
    mid_out, mid_lse = attend(mid_q, class_ranks, mid_k, mid_v, class_ranks)
    back_mid, back_mid_lse, back_far, back_far_lse = (
        *side_by_side_2((mid_out, mid_lse), "inner", 1, 0, 2),
        *side_by_side_2((far_out, far_lse), "inner", 1, 0, 2),
    )
    selector = np.array(
        [[band_index == head // 4 for band_index in range(4)] for head in range(heads)]
    )
    spread_out = jnp.where(
        selector[:, :, None, None, None], back_far.reshape(heads, 1, 4, sixteenth, width), 0.0
    )
    spread_lse = jnp.where(
        selector[:, :, None, None], back_far_lse.reshape(heads, 1, 4, sixteenth), FLOOR_SCORE
    )
    far_placed = (
        spread_out.reshape(heads, 16, sixteenth, width)
        .transpose(2, 1, 0, 3)
        .reshape(tokens, heads, width)
    )
    far_placed_lse = (
        spread_lse.reshape(heads, 16, sixteenth).transpose(2, 1, 0).reshape(tokens, heads)
    )
    placed = (
        back_mid.reshape(heads, 4, quarter, width)
        .transpose(2, 1, 0, 3)
        .reshape(tokens, heads, width)
    )
    placed_lse = back_mid_lse.reshape(heads, 4, quarter).transpose(2, 1, 0).reshape(tokens, heads)
    combined, _ = merge_levels(
        [(near_out, near_lse), (placed, placed_lse), (far_placed, far_placed_lse)]
    )
    return combined.reshape(tokens, features)


def solution(mesh):
    placed = (P(("outer", "inner"), None), P(("outer", "inner"), None), P(("outer", "inner"), None))
    return jax.shard_map(
        on_device,
        mesh=mesh,
        in_specs=placed,
        out_specs=P(("outer", "inner"), None),
        check_vma=False,
    )
```

profile of v0, /device:TPU:1, one launch (start us, length us, event | category | flops | bytes accessed | tf_op | source)
XLA Modules:
  0.0 356.0 jit_solution(15529801843470175704)
XLA Ops:
  6.5 1.1 reshape.245
  7.9 1.2 reshape.247
  9.2 1.1 reshape.249
  10.5 1.1 pad_maximum_fusion.1
  11.6 17.4 %all-to-all-start = ((bf16[64,16,192]{2,1,0:T(8,128)(2,1)}), bf16[64,16,192]{2,1,0:T(8,128)(2,1)S(1)}, u32[]{:S(2)}, u32[]{:S(2)}) async-start(bf16[64,16,192]{2,1,0:T(8,128)(2,1)} %pad_maximum_fusion.1), calls=%async_computation | async-start | bytes 1048576 | tf_op jit(solution)/shard_map/all_to_all | solution.py:27
  32.3 13.9 %all-to-all-done = bf16[64,16,192]{2,1,0:T(8,128)(2,1)S(1)} async-done(((bf16[64,16,192]{2,1,0:T(8,128)(2,1)}), bf16[64,16,192]{2,1,0:T(8,128)(2,1)S(1)}, u32[]{:S(2)}, u32[]{:S(2)}) %all-to-all-start) | async-done | bytes 393248 | tf_op jit(solution)/shard_map/all_to_all | solution.py:27
  48.2 1.0 copy.100
  49.2 7.9 %all-to-all-start.1 = ((f32[2,512,65]{2,0,1:T(2,128)}), f32[2,512,65]{2,0,1:T(2,128)}, u32[]{:S(2)}, u32[]{:S(2)}) async-start(f32[2,512,65]{2,0,1:T(2,128)} %copy.100), calls=%async_computation.1 | async-start | bytes 1048576 | tf_op jit(solution)/shard_map/all_to_all | solution.py:35
  57.1 52.0 %all-gather.2.cloned.1.call-done = bf16[128,64,64]{0,2,1:T(8,128)(2,1)} async-done(((bf16[128,4,64]{0,2,1:T(8,128)(2,1)}), bf16[128,64,64]{0,2,1:T(8,128)(2,1)}) %all-gather.2.cloned.1.call-update) | async-done | bytes 1048592 | tf_op jit(solution)/shard_map/all_gather | solution.py:21
  109.1 2.0 fusion.75
  111.1 1.6 copy.139
  112.8 1.6 copy.140
  114.5 1.5 pad_maximum_fusion
  116.0 20.6 %all-to-all-start.2 = ((bf16[64,64,128]{2,1,0:T(8,128)(2,1)}), bf16[64,64,128]{2,1,0:T(8,128)(2,1)S(1)}, u32[]{:S(2)}, u32[]{:S(2)}) async-start(bf16[64,64,128]{2,1,0:T(8,128)(2,1)} %pad_maximum_fusion), calls=%async_computation.2 | async-start | bytes 2097152 | tf_op jit(solution)/shard_map/all_to_all | solution.py:27
  136.8 0.9 reshape.244
  137.7 0.9 reshape.259
  140.1 173.5 %gather_fusion = bf16[16384]{0:T(1024)(128)(2,1)S(1)} fusion(bf16[2,128,4,64]{3,2,1,0:T(4,128)(2,1)S(1)} %bitcast.106, s32[16384]{0:T(1024)S(1)} %reshape.282), kind=kCustom, calls=%fused_computation.2 | custom fusion | bytes 327680 | tf_op jit(solution)/shard_map/jit(take_along_axis)/gather | solution.py:193
  313.8 1.1 copy.101
  316.1 3.7 %while.38 = (s32[]{:T(128)}, f32[2,128]{1,0:T(2,128)S(1)}, f32[2,128]{1,0:T(2,128)S(1)}, f32[2,128,64]{1,2,0:T(8,128)S(1)}, s32[2048]{0:T(1024)S(1)}, /*index=5*...) while((s32[]{:T(128)}, f32[2,128]{1,0:T(2,128)S(1)}, ...), condition=%wide.region_7.9_spmd.clone, body=%wide.region_4.0_spmd.clone.sunk | while | flops 34588036 | bytes 2153671 | solution.py:95
  320.1 0.9 pad_maximum_fusion.4
  321.0 12.2 %all-to-all-start.3 = ((f32[2,128,65]{2,0,1:T(2,128)}), f32[2,128,65]{2,0,1:T(2,128)S(1)}, u32[]{:S(2)}, u32[]{:S(2)}) async-start(f32[2,128,65]{2,0,1:T(2,128)} %pad_maximum_fusion.4), calls=%async_computation.3 | async-start | bytes 262144 | tf_op jit(solution)/shard_map/all_to_all | solution.py:35
  333.9 11.6 %all-to-all-done.3 = f32[2,128,65]{2,0,1:T(2,128)S(1)} async-done(((f32[2,128,65]{2,0,1:T(2,128)}), f32[2,128,65]{2,0,1:T(2,128)S(1)}, u32[]{:S(2)}, u32[]{:S(2)}) %all-to-all-start.3) | async-done | bytes 66592 | tf_op jit(solution)/shard_map/all_to_all | solution.py:35
  346.6 1.3 fusion.22
  348.3 0.9 reshape.263
  (137 shorter events, 14.4 us)
Async XLA Ops:
  7.8 21.2 %copy-start = (bf16[64,1024]{1,0:T(8,128)(2,1)S(1)}, bf16[64,1024]{1,0:T(8,128)(2,1)}, u32[]{:S(2)}) copy-start(bf16[64,1024]{1,0:T(8,128)(2,1)} %param.11) | copy-start | bytes 393220
  9.0 20.2 %copy-start.1 = (bf16[64,1024]{1,0:T(8,128)(2,1)S(1)}, bf16[64,1024]{1,0:T(8,128)(2,1)}, u32[]{:S(2)}) copy-start(bf16[64,1024]{1,0:T(8,128)(2,1)} %param.12) | copy-start | bytes 393220
  11.6 18.4 %copy-start.10 = (s32[64]{0:T(128)S(1)}, s32[64]{0:T(128)}, u32[]{:S(2)}) copy-start(s32[64]{0:T(128)} %constant.317) | copy-start | bytes 772
  11.6 34.6 %all-to-all-start = ((bf16[64,16,192]{2,1,0:T(8,128)(2,1)}), bf16[64,16,192]{2,1,0:T(8,128)(2,1)S(1)}, u32[]{:S(2)}, u32[]{:S(2)}) async-start(bf16[64,16,192]{2,1,0:T(8,128)(2,1)} %pad_maximum_fusion.1), calls=%async_computation | async-start | bytes 1048576 | tf_op jit(solution)/shard_map/all_to_all | solution.py:27
  29.0 80.1 %all-gather.2.cloned.1.call-start = ((), (), s32[]{:S(2)}) async-start(), calls=%async_computation.4 | async-start | bytes 1114112 | tf_op jit(solution)/shard_map/all_gather | solution.py:21
  46.2 1.2 copy-start.2
  49.2 66.8 %all-to-all-start.1 = ((f32[2,512,65]{2,0,1:T(2,128)}), f32[2,512,65]{2,0,1:T(2,128)}, u32[]{:S(2)}, u32[]{:S(2)}) async-start(f32[2,512,65]{2,0,1:T(2,128)} %copy.100), calls=%async_computation.1 | async-start | bytes 1048576 | tf_op jit(solution)/shard_map/all_to_all | solution.py:35
  114.5 22.2 %copy-start.4 = (bf16[64,1024]{1,0:T(8,128)(2,1)S(1)}, bf16[64,1024]{1,0:T(8,128)(2,1)}, u32[]{:S(2)}) copy-start(bf16[64,1024]{1,0:T(8,128)(2,1)} %param.10) | copy-start | bytes 393220
  116.0 199.0 %all-to-all-start.2 = ((bf16[64,64,128]{2,1,0:T(8,128)(2,1)}), bf16[64,64,128]{2,1,0:T(8,128)(2,1)S(1)}, u32[]{:S(2)}, u32[]{:S(2)}) async-start(bf16[64,64,128]{2,1,0:T(8,128)(2,1)} %pad_maximum_fusion), calls=%async_computation.2 | async-start | bytes 2097152 | tf_op jit(solution)/shard_map/all_to_all | solution.py:27
  136.6 2.5 copy-start.9
  138.6 0.9 copy-start.8
  138.6 1.4 copy-start.3
  139.9 173.7 %copy-start.5 = (f32[16,64,64]{1,2,0:T(8,128)}, f32[16,64,64]{1,2,0:T(8,128)S(1)}, u32[]{:S(2)}) copy-start(f32[16,64,64]{1,2,0:T(8,128)S(1)} %get-tuple-element.496) | copy-start | bytes 786436
  321.0 24.6 %all-to-all-start.3 = ((f32[2,128,65]{2,0,1:T(2,128)}), f32[2,128,65]{2,0,1:T(2,128)S(1)}, u32[]{:S(2)}, u32[]{:S(2)}) async-start(f32[2,128,65]{2,0,1:T(2,128)} %pad_maximum_fusion.4), calls=%async_computation.3 | async-start | bytes 262144 | tf_op jit(solution)/shard_map/all_to_all | solution.py:35
  333.9 12.7 %copy-start.6 = (f32[16,64,64]{1,2,0:T(8,128)S(1)}, f32[16,64,64]{1,2,0:T(8,128)}, u32[]{:S(2)}) copy-start(f32[16,64,64]{1,2,0:T(8,128)} %copy-done.5) | copy-start | bytes 786436
  333.9 12.7 %copy-start.7 = (bf16[64,16,64]{2,1,0:T(8,128)(2,1)S(1)}, bf16[64,16,64]{2,1,0:T(8,128)(2,1)}, u32[]{:S(2)}) copy-start(bf16[64,16,64]{2,1,0:T(8,128)(2,1)} %reshape.259) | copy-start | bytes 393220
Sparse Core Ops, SparseCore 0:
  32.3 76.7 all-gather.1
where the time goes:
time: 357 us; the launch traced here: 356 us
  local copies, waits for them, and re-layouts  195 us (55%)
  waiting for transfers between devices  77.5 us (22%)
  starting transfers between devices  58.1 us (16%)
  between operations  14.1 us (4%)
  other arithmetic  6.08 us (2%)
  matrix products  5.03 us (1%)
    gather x3, local copies, waits for them, and re-layouts, on_device(): far_q = jnp.take_along_axis(split, picker, axis=2)[:, :, 0, :]  174 us
    all_gather x1, waiting for transfers between devices, side_by_side(): lax.all_gather(both, axis, axis=dim, tiled=True)  52 us
    all_to_all x2, starting transfers between devices, in_one_piece(): lax.all_to_all(both, axis, split_axis=split_dim, concat_axis=concat_dim,...  37.9 us
    all_to_all x2, starting transfers between devices, side_by_side_2(): lax.all_to_all(both, axis, split_axis=split_dim, concat_axis=concat_dim,...  20.1 us
    all_to_all x2, waiting for transfers between devices, in_one_piece(): lax.all_to_all(both, axis, split_axis=split_dim, concat_axis=concat_dim,...  13.9 us
    all_to_all x2, waiting for transfers between devices, side_by_side_2(): lax.all_to_all(both, axis, split_axis=split_dim, concat_axis=concat_dim,...  11.6 us
  transfers between devices with their start and end apart: 5, of which 3 were waited for; matrix products, arithmetic and copies ran while one was open for 54% of the time, Pallas kernels for 0%

commit v1 on v0

v1 whole, which is shorter than its diff:
```python
import functools

import jax
import jax.numpy as jnp
from jax import lax
from jax.experimental import pallas as pl
from jax.experimental.pallas import tpu as pltpu
from jax.sharding import PartitionSpec as P

TOK = 64
WIDTH = 64
LANES = 2 * WIDTH
PAIRS = 8
RES = 4
ROWS = TOK // RES
INNER = PAIRS * RES
OUTER = 16
CLASS = ROWS * INNER
FAR = CLASS // 4
FLOOR = -1e30
F32 = jnp.float32
BF16 = jnp.bfloat16


def dot(a, b):
    return jnp.dot(a, b, preferred_element_type=F32)


def dot_t(a, b):
    return lax.dot_general(a, b, (((1,), (1,)), ((), ())), preferred_element_type=F32)


def iota(shape, dim):
    return lax.broadcasted_iota(jnp.int32, shape, dim)


def one_hot(shape, row_of, col_of, dtype=BF16):
    return (row_of(iota(shape, 0)) == col_of(iota(shape, 1))).astype(F32).astype(dtype)


def by_class(r):
    return RES * (r % ROWS) + r // ROWS


def first_head(rows):
    return iota((rows, LANES), 1) < WIDTH


def stack_heads(q):
    left = first_head(q.shape[0])
    zero = jnp.zeros_like(q)
    return jnp.concatenate([jnp.where(left, q, zero), jnp.where(left, zero, q)], axis=0)


def side_heads(x):
    half = x.shape[0] // 2
    return jnp.where(
        first_head(half),
        jnp.broadcast_to(x[:half], (half, LANES)),
        jnp.broadcast_to(x[half:], (half, LANES)),
    )


def softmax_out(scores, values):
    top = jnp.max(scores, axis=1, keepdims=True)
    weights = jnp.exp(scores - top)
    total = jnp.sum(weights, axis=1, keepdims=True)
    summed = dot(weights.astype(BF16), values)
    return side_heads(summed / total), side_heads(top + jnp.log(total))


def pack_kernel(q_ref, k_ref, v_ref, out_ref):
    order = one_hot((TOK, TOK), by_class, lambda c: c)
    for at, ref in enumerate((q_ref, k_ref, v_ref)):
        rows = dot(order, ref[...]).astype(BF16)
        for pair in range(PAIRS):
            part = rows[:, pair * LANES : (pair + 1) * LANES]
            out_ref[pair * RES : (pair + 1) * RES, at * ROWS : (at + 1) * ROWS, :] = part.reshape(
                RES, ROWS, LANES
            )


def near_kernel(q_ref, k_ref, v_ref, out_ref, lse_ref):
    allowed = iota((2 * TOK, TOK), 1) <= iota((2 * TOK, TOK), 0) % TOK
    for pair in range(PAIRS):
        cols = slice(pair * LANES, (pair + 1) * LANES)
        q = stack_heads(q_ref[:, cols] * BF16(WIDTH**-0.5))
        scores = jnp.where(allowed, dot_t(q, k_ref[:, cols]), FLOOR)
        out_ref[:, cols], lse_ref[:, cols] = softmax_out(scores, v_ref[:, cols])


def section(ref, at):
    return ref[:, at * ROWS : (at + 1) * ROWS, :].reshape(CLASS, LANES)


def pick_kernel(place_ref, got_ref, q_ref, kv_ref):
    band = place_ref[0]
    pick = one_hot((FAR, CLASS), lambda r: 4 * r + band, lambda c: c)
    q_ref[...] = dot(pick, section(got_ref, 0)).astype(BF16)
    k = dot(pick, section(got_ref, 1)).astype(BF16)
    v = dot(pick, section(got_ref, 2)).astype(BF16)
    for to in range(OUTER):
        kv_ref[to, :FAR, :] = k
        kv_ref[to, FAR:, :] = v


def mid_kernel(got_ref, out_ref, lse_ref):
    q = section(got_ref, 0) * BF16(WIDTH**-0.5)
    k = section(got_ref, 1)
    v = section(got_ref, 2)
    block = 128
    for start in range(0, CLASS, block):
        end = start + block
        rows = stack_heads(q[start:end])
        shape = (2 * block, end)
        allowed = iota(shape, 1) <= start + iota(shape, 0) % block
        scores = jnp.where(allowed, dot_t(rows, k[:end]), FLOOR)
        out_ref[start:end, :], lse_ref[start:end, :] = softmax_out(scores, v[:end])


def far_kernel(place_ref, q_ref, kv_ref, mid_out_ref, mid_lse_ref, back_ref):
    band, group = place_ref[0], place_ref[1]
    q = stack_heads(q_ref[...] * BF16(WIDTH**-0.5))
    k = kv_ref[:, :FAR, :].reshape(OUTER * FAR, LANES)
    v = kv_ref[:, FAR:, :].reshape(OUTER * FAR, LANES)
    shape = (2 * FAR, OUTER * FAR)
    allowed = iota(shape, 1) <= group * FAR + iota(shape, 0) % FAR
    far_out, far_lse = softmax_out(jnp.where(allowed, dot_t(q, k), FLOOR), v)
    spread = one_hot((CLASS, FAR), lambda r: r, lambda c: 4 * c + band, F32)
    exact = functools.partial(
        jnp.dot, precision=lax.Precision.HIGHEST, preferred_element_type=F32
    )
    present = iota((CLASS, LANES), 0) % 4 == band
    far_out = exact(spread, far_out)
    far_lse = jnp.where(present, exact(spread, far_lse), FLOOR)
    mid_lse = mid_lse_ref[...]
    top = jnp.maximum(mid_lse, far_lse)
    mid_w, far_w = jnp.exp(mid_lse - top), jnp.exp(far_lse - top)
    total = mid_w + far_w
    out = (mid_w * mid_out_ref[...] + far_w * far_out) / total
    lse = top + jnp.log(total)
    high = lse.astype(BF16).astype(F32)
    middle = (lse - high).astype(BF16).astype(F32)
    low = lse - high - middle
    which = iota((CLASS, LANES), 1) % WIDTH // 16
    parts = jnp.where(
        which == 0, high, jnp.where(which == 1, middle, jnp.where(which == 2, low, 0.0))
    )
    back_ref[:, :ROWS, :] = out.astype(BF16).reshape(INNER, ROWS, LANES)
    back_ref[:, ROWS:, :] = parts.astype(BF16).reshape(INNER, ROWS, LANES)


def home_kernel(got_ref, near_out_ref, near_lse_ref, out_ref):
    order = one_hot((TOK, TOK), lambda r: r, by_class)
    shape = (LANES, LANES)
    row, col = iota(shape, 0), iota(shape, 1)
    gather = (row // WIDTH == col // WIDTH) & (row % 16 == 0)
    gather = gather.astype(F32).astype(BF16)
    for pair in range(PAIRS):
        cols = slice(pair * LANES, (pair + 1) * LANES)
        mine = got_ref[pair * RES : (pair + 1) * RES, :, :]
        out = dot(order, mine[:, :ROWS, :].reshape(TOK, LANES))
        parts = dot(order, mine[:, ROWS:, :].reshape(TOK, LANES)).astype(BF16)
        lse = dot(parts, gather)
        near_lse = near_lse_ref[:, cols]
        top = jnp.maximum(lse, near_lse)
        w, near_w = jnp.exp(lse - top), jnp.exp(near_lse - top)
        out_ref[:, cols] = (w * out + near_w * near_out_ref[:, cols]) / (w + near_w)


def call(kernel, outs, args, scalars=0, flops=0, exps=0):
    vmem = pl.BlockSpec(memory_space=pltpu.VMEM)
    specs = [pl.BlockSpec(memory_space=pltpu.SMEM)] * scalars + [vmem] * (len(args) - scalars)
    shapes = [jax.ShapeDtypeStruct(s, t) for s, t in outs]
    moved = sum(a.size * a.dtype.itemsize for a in args)
    moved += sum(s.size * s.dtype.itemsize for s in shapes)
    return pl.pallas_call(
        kernel,
        out_shape=shapes,
        in_specs=specs,
        out_specs=[vmem] * len(shapes),
        compiler_params=pltpu.CompilerParams(vmem_limit_bytes=40 * 2**20),
        cost_estimate=pl.CostEstimate(flops=flops, bytes_accessed=moved, transcendentals=exps),
    )(*args)


def on_device(queries, key_rows, value_rows):
    group = lax.axis_index("outer")
    place = jnp.stack([lax.axis_index("inner") // 8, group]).astype(jnp.int32)
    full = (TOK, PAIRS * LANES)
    (packed,) = call(
        pack_kernel, [((INNER, 3 * ROWS, LANES), BF16)], (queries, key_rows, value_rows)
    )
    got = lax.all_to_all(packed, "inner", 0, 0, tiled=True)
    near_out, near_lse = call(
        near_kernel,
        [(full, F32), (full, F32)],
        (queries, key_rows, value_rows),
        flops=2 * 16 * 64 * 64 * 128 * 2,
        exps=16 * 64 * 64,
    )
    far_q, far_kv = call(
        pick_kernel,
        [((FAR, LANES), BF16), ((OUTER, 2 * FAR, LANES), BF16)],
        (place, got),
        scalars=1,
    )
    all_kv = lax.all_to_all(far_kv, "outer", 0, 0, tiled=True)
    mid_out, mid_lse = call(
        mid_kernel,
        [((CLASS, LANES), F32), ((CLASS, LANES), F32)],
        (got,),
        flops=4 * 2 * 512 * 512 * 128,
        exps=2 * 512 * 512,
    )
    (back,) = call(
        far_kernel,
        [((INNER, 2 * ROWS, LANES), BF16)],
        (place, far_q, all_kv, mid_out, mid_lse),
        scalars=1,
        flops=4 * 2 * 128 * 2048 * 128,
        exps=2 * 128 * 2048,
    )
    home = lax.all_to_all(back, "inner", 0, 0, tiled=True)
    (out,) = call(home_kernel, [(full, F32)], (home, near_out, near_lse))
    return out


def solution(mesh):
    rows = P(("outer", "inner"), None)
    return jax.shard_map(
        on_device, mesh=mesh, in_specs=(rows,) * 3, out_specs=rows, check_vma=False
    )
```

time: 357 us -> 96.6 us (0.27)
  the two profiles are of different devices: /device:TPU:1 before, /device:TPU:8 now
where the time goes in v1:
time: 96.6 us; the launch traced here: 96.2 us
  waiting for transfers between devices  59.5 us (62%)
  starting transfers between devices  24.8 us (26%)
  Pallas kernels  8.98 us (9%)
  local copies, waits for them, and re-layouts  2.72 us (3%)
    all_to_all x1, waiting for transfers between devices, on_device(): all_kv = lax.all_to_all(far_kv, 'outer', 0, 0, tiled=True)  23.9 us
    all_to_all x1, waiting for transfers between devices, on_device(): got = lax.all_to_all(packed, 'inner', 0, 0, tiled=True)  19.7 us
    all_to_all x1, waiting for transfers between devices, on_device(): home = lax.all_to_all(back, 'inner', 0, 0, tiled=True)  15.9 us
    all_to_all x1, starting transfers between devices, on_device(): got = lax.all_to_all(packed, 'inner', 0, 0, tiled=True)  15.1 us
    pallas_call x6, Pallas kernels, call(): pl.pallas_call(kernel, out_shape=shapes, in_specs=specs, out_specs=[vmem]...  8.98 us
    all_to_all x1, starting transfers between devices, on_device(): all_kv = lax.all_to_all(far_kv, 'outer', 0, 0, tiled=True)  5.78 us
    all_to_all x1, starting transfers between devices, on_device(): home = lax.all_to_all(back, 'inner', 0, 0, tiled=True)  4 us
    unnamed x12, local copies, waits for them, and re-layouts  2.72 us
  transfers between devices with their start and end apart: 3, of which 3 were waited for; matrix products, arithmetic and copies ran while one was open for 0% of the time, Pallas kernels for 2%

profile of v1, /device:TPU:8, one launch (start us, length us, event | category | flops | bytes accessed | tf_op | source)
XLA Modules:
  0.0 96.2 jit_solution(5627850356229035712)
XLA Ops:
  0.0 0.0 copy-start
  0.0 0.9 copy-done
  0.9 0.0 copy-start.2
  0.9 0.9 copy-done.2
  1.8 0.0 copy-start.4
  1.8 0.9 copy-done.4
  2.7 1.0 %shard_map.37 = bf16[32,48,128]{2,1,0:T(8,128)(2,1)} custom-call(bf16[64,1024]{1,0:T(8,128)(2,1)S(1)} %copy-done, bf16[64,1024]{1,0:T(8,128)(2,1)S(1)} %copy-done.2, bf16[64,1024]{1,0:T(8,128)(2,1)S(1)} %copy-done.4), custom_call_target="tpu_custom_call" | custom-call | bytes 786432 | tf_op jit(solution)/shard_map/pallas_call | solution.py:177
  3.7 15.1 %all-to-all-start = ((bf16[32,48,128]{2,1,0:T(8,128)(2,1)}), bf16[32,48,128]{2,1,0:T(8,128)(2,1)S(1)}, u32[]{:S(2)}, u32[]{:S(2)}) async-start(bf16[32,48,128]{2,1,0:T(8,128)(2,1)} %shard_map.37), calls=%async_computation | async-start | bytes 786432 | tf_op jit(solution)/shard_map/all_to_all | solution.py:194
  18.8 0.1 pad_add_fusion.place_ref
  18.9 19.7 %all-to-all-done.got_ref = bf16[32,48,128]{2,1,0:T(8,128)(2,1)S(1)} async-done(((bf16[32,48,128]{2,1,0:T(8,128)(2,1)}), bf16[32,48,128]{2,1,0:T(8,128)(2,1)S(1)}, u32[]{:S(2)}, u32[]{:S(2)}) %all-to-all-start) | async-done | bytes 393248 | tf_op jit(solution)/shard_map/all_to_all | solution.py:194
  38.6 1.8 %shard_map.38 = (bf16[128,128]{1,0:T(8,128)(2,1)S(1)}, bf16[16,256,128]{2,1,0:T(8,128)(2,1)}) custom-call(s32[2]{0:T(128)S(1)} %pad_add_fusion.place_ref, bf16[32,48,128]{2,1,0:T(8,128)(2,1)S(1)} %all-to-all-done.got_ref), custom_call_target="tpu_custom_call" | custom-call | bytes 1474568 | tf_op jit(solution)/shard_map/pallas_call | solution.py:177
  40.4 5.8 %all-to-all-start.1 = ((bf16[16,256,128]{2,1,0:T(8,128)(2,1)}), bf16[16,256,128]{2,1,0:T(8,128)(2,1)S(1)}, u32[]{:S(2)}, u32[]{:S(2)}) async-start(bf16[16,256,128]{2,1,0:T(8,128)(2,1)} %get-tuple-element.12), calls=%async_computation.1 | async-start | bytes 2097152 | tf_op jit(solution)/shard_map/all_to_all | solution.py:208
  46.2 1.3 %shard_map.39 = (f32[512,128]{1,0:T(8,128)S(1)}, f32[512,128]{1,0:T(8,128)S(1)}) custom-call(bf16[32,48,128]{2,1,0:T(8,128)(2,1)S(1)} %all-to-all-done.got_ref), custom_call_target="tpu_custom_call" | custom-call | flops 268435456 | bytes 917504 | tf_op jit(solution)/shard_map/pallas_call | solution.py:177
  47.4 23.9 %all-to-all-done.1.kv_ref = bf16[16,256,128]{2,1,0:T(8,128)(2,1)S(1)} async-done(((bf16[16,256,128]{2,1,0:T(8,128)(2,1)}), bf16[16,256,128]{2,1,0:T(8,128)(2,1)S(1)}, u32[]{:S(2)}, u32[]{:S(2)}) %all-to-all-start.1) | async-done | bytes 1048608 | tf_op jit(solution)/shard_map/all_to_all | solution.py:208
  71.3 3.1 %shard_map.40 = bf16[32,32,128]{2,1,0:T(8,128)(2,1)} custom-call(s32[2]{0:T(128)S(1)} %pad_add_fusion.place_ref, bf16[128,128]{1,0:T(8,128)(2,1)S(1)} %get-tuple-element.11.q_ref, bf16[16,256,128]{2,1,0:T(8,128)(2,1)S(1)} %all-to-all-done.1.kv_ref, f32[512,128]{1,0:T(8,128)S(1)} %get-tuple-element.13.mid_out_ref, f32[512,128]{1,0:T(8,128)S(1)} %get-tuple-element.14.mid_lse_ref), custom_call_target="tpu_custom_call" | custom-call | flops 268435456 | bytes 1867784 | tf_op jit(solution)/shard_map/pallas_call | solution.py:177
  74.4 0.0 copy-start.1
  74.4 0.0 copy-start.3
  74.5 4.0 %all-to-all-start.2 = ((bf16[32,32,128]{2,1,0:T(8,128)(2,1)}), bf16[32,32,128]{2,1,0:T(8,128)(2,1)S(1)}, u32[]{:S(2)}, u32[]{:S(2)}) async-start(bf16[32,32,128]{2,1,0:T(8,128)(2,1)} %shard_map.40), calls=%async_computation.2 | async-start | bytes 524288 | tf_op jit(solution)/shard_map/all_to_all | solution.py:224
  78.5 0.0 copy-done.1
  78.5 0.0 copy-done.3
  78.5 0.0 copy-done.5
  78.5 0.7 shard_map.41
  79.2 15.9 %all-to-all-done.2.got_ref = bf16[32,32,128]{2,1,0:T(8,128)(2,1)S(1)} async-done(((bf16[32,32,128]{2,1,0:T(8,128)(2,1)}), bf16[32,32,128]{2,1,0:T(8,128)(2,1)S(1)}, u32[]{:S(2)}, u32[]{:S(2)}) %all-to-all-start.2) | async-done | bytes 262176 | tf_op jit(solution)/shard_map/all_to_all | solution.py:224
  95.1 1.1 %shard_map.42 = f32[64,1024]{1,0:T(8,128)} custom-call(bf16[32,32,128]{2,1,0:T(8,128)(2,1)S(1)} %all-to-all-done.2.got_ref, f32[64,1024]{1,0:T(8,128)S(1)} %get-tuple-element.15.near_out_ref, f32[64,1024]{1,0:T(8,128)S(1)} %get-tuple-element.16.near_lse_ref), custom_call_target="tpu_custom_call" | custom-call | bytes 1048576 | tf_op jit(solution)/shard_map/pallas_call | solution.py:177
  (1 shorter events, 0.0 us)
Async XLA Ops:
  0.0 0.9 copy-start
  0.9 0.9 copy-start.2
  1.8 0.9 copy-start.4
  3.7 34.9 %all-to-all-start = ((bf16[32,48,128]{2,1,0:T(8,128)(2,1)}), bf16[32,48,128]{2,1,0:T(8,128)(2,1)S(1)}, u32[]{:S(2)}, u32[]{:S(2)}) async-start(bf16[32,48,128]{2,1,0:T(8,128)(2,1)} %shard_map.37), calls=%async_computation | async-start | bytes 786432 | tf_op jit(solution)/shard_map/all_to_all | solution.py:194
  40.4 30.9 %all-to-all-start.1 = ((bf16[16,256,128]{2,1,0:T(8,128)(2,1)}), bf16[16,256,128]{2,1,0:T(8,128)(2,1)S(1)}, u32[]{:S(2)}, u32[]{:S(2)}) async-start(bf16[16,256,128]{2,1,0:T(8,128)(2,1)} %get-tuple-element.12), calls=%async_computation.1 | async-start | bytes 2097152 | tf_op jit(solution)/shard_map/all_to_all | solution.py:208
  74.4 4.0 %copy-start.1 = (bf16[64,1024]{1,0:T(8,128)(2,1)S(1)}, bf16[64,1024]{1,0:T(8,128)(2,1)}, u32[]{:S(2)}) copy-start(bf16[64,1024]{1,0:T(8,128)(2,1)} %q_ref.3) | copy-start | bytes 393220
  74.4 4.0 %copy-start.3 = (bf16[64,1024]{1,0:T(8,128)(2,1)S(1)}, bf16[64,1024]{1,0:T(8,128)(2,1)}, u32[]{:S(2)}) copy-start(bf16[64,1024]{1,0:T(8,128)(2,1)} %k_ref.3) | copy-start | bytes 393220
  74.5 4.0 %copy-start.5 = (bf16[64,1024]{1,0:T(8,128)(2,1)S(1)}, bf16[64,1024]{1,0:T(8,128)(2,1)}, u32[]{:S(2)}) copy-start(bf16[64,1024]{1,0:T(8,128)(2,1)} %v_ref.3) | copy-start | bytes 393220
  74.5 20.7 %all-to-all-start.2 = ((bf16[32,32,128]{2,1,0:T(8,128)(2,1)}), bf16[32,32,128]{2,1,0:T(8,128)(2,1)S(1)}, u32[]{:S(2)}, u32[]{:S(2)}) async-start(bf16[32,32,128]{2,1,0:T(8,128)(2,1)} %shard_map.40), calls=%async_computation.2 | async-start | bytes 524288 | tf_op jit(solution)/shard_map/all_to_all | solution.py:224

commit v2 on v1

--- a/solution.py
+++ b/solution.py
@@ -14,7 +14,7 @@
 RES = 4
 ROWS = TOK // RES
 INNER = PAIRS * RES
-OUTER = 16
+HALF = 8
 CLASS = ROWS * INNER
 FAR = CLASS // 4
 FLOOR = -1e30
@@ -69,10 +69,17 @@
     return side_heads(summed / total), side_heads(top + jnp.log(total))
 
 
-def pack_kernel(q_ref, k_ref, v_ref, out_ref):
+def pack_kernel(q_ref, k_ref, v_ref, out_ref, held, sems):
+    copies = [
+        pltpu.make_async_copy(ref, held.at[at], sems.at[at])
+        for at, ref in enumerate((q_ref, k_ref, v_ref))
+    ]
+    for copy in copies:
+        copy.start()
     order = one_hot((TOK, TOK), by_class, lambda c: c)
-    for at, ref in enumerate((q_ref, k_ref, v_ref)):
-        rows = dot(order, ref[...]).astype(BF16)
+    for at, copy in enumerate(copies):
+        copy.wait()
+        rows = dot(order, held[at]).astype(BF16)
         for pair in range(PAIRS):
             part = rows[:, pair * LANES : (pair + 1) * LANES]
             out_ref[pair * RES : (pair + 1) * RES, at * ROWS : (at + 1) * ROWS, :] = part.reshape(
@@ -99,7 +106,7 @@
     q_ref[...] = dot(pick, section(got_ref, 0)).astype(BF16)
     k = dot(pick, section(got_ref, 1)).astype(BF16)
     v = dot(pick, section(got_ref, 2)).astype(BF16)
-    for to in range(OUTER):
+    for to in range(HALF):
         kv_ref[to, :FAR, :] = k
         kv_ref[to, FAR:, :] = v
 
@@ -118,34 +125,95 @@
         out_ref[start:end, :], lse_ref[start:end, :] = softmax_out(scores, v[:end])
 
 
-def far_kernel(place_ref, q_ref, kv_ref, mid_out_ref, mid_lse_ref, back_ref):
-    band, group = place_ref[0], place_ref[1]
-    q = stack_heads(q_ref[...] * BF16(WIDTH**-0.5))
-    k = kv_ref[:, :FAR, :].reshape(OUTER * FAR, LANES)
-    v = kv_ref[:, FAR:, :].reshape(OUTER * FAR, LANES)
-    shape = (2 * FAR, OUTER * FAR)
-    allowed = iota(shape, 1) <= group * FAR + iota(shape, 0) % FAR
-    far_out, far_lse = softmax_out(jnp.where(allowed, dot_t(q, k), FLOOR), v)
-    spread = one_hot((CLASS, FAR), lambda r: r, lambda c: 4 * c + band, F32)
-    exact = functools.partial(
-        jnp.dot, precision=lax.Precision.HIGHEST, preferred_element_type=F32
-    )
-    present = iota((CLASS, LANES), 0) % 4 == band
-    far_out = exact(spread, far_out)
-    far_lse = jnp.where(present, exact(spread, far_lse), FLOOR)
-    mid_lse = mid_lse_ref[...]
-    top = jnp.maximum(mid_lse, far_lse)
-    mid_w, far_w = jnp.exp(mid_lse - top), jnp.exp(far_lse - top)
-    total = mid_w + far_w
-    out = (mid_w * mid_out_ref[...] + far_w * far_out) / total
-    lse = top + jnp.log(total)
+def far_keys(kv_ref):
+    keys = kv_ref[:, :FAR, :].reshape(HALF * FAR, LANES)
+    return keys, kv_ref[:, FAR:, :].reshape(HALF * FAR, LANES)
+
+
+def lse_part(lse, which):
     high = lse.astype(BF16).astype(F32)
     middle = (lse - high).astype(BF16).astype(F32)
     low = lse - high - middle
-    which = iota((CLASS, LANES), 1) % WIDTH // 16
-    parts = jnp.where(
+    return jnp.where(
         which == 0, high, jnp.where(which == 1, middle, jnp.where(which == 2, low, 0.0))
     )
+
+
+def serve_kernel(q_ref, kv_ref, part_ref):
+    k, v = far_keys(kv_ref)
+    q = stack_heads(q_ref[...] * BF16(WIDTH**-0.5))
+    scores = dot_t(q, k)
+    top = jnp.max(scores, axis=1, keepdims=True)
+    weights = jnp.exp(scores - top)
+    total = jnp.sum(weights, axis=1, keepdims=True)
+    part_ref[:FAR, :] = side_heads(dot(weights.astype(BF16), v) / total).astype(BF16)
+    lse = top + jnp.log(total)
+    lane = iota((FAR, LANES), 1)
+    shape = (FAR, LANES)
+    mine = jnp.where(
+        lane % 16 < 8, jnp.broadcast_to(lse[:FAR], shape), jnp.broadcast_to(lse[FAR:], shape)
+    )
+    parts = lse_part(mine, lane % 8)
+    lane = lane[:16]
+    packed = parts[:16]
+    for b in range(1, FAR // 16):
+        packed = jnp.where(lane // 16 == b, parts[16 * b : 16 * b + 16], packed)
+    part_ref[FAR:, :] = packed.astype(BF16)
+
+
+def merge(out, lse, other_out, other_lse):
+    top = jnp.maximum(lse, other_lse)
+    w, other_w = jnp.exp(lse - top), jnp.exp(other_lse - top)
+    total = w + other_w
+    return (w * out + other_w * other_out) / total, top + jnp.log(total)
+
+
+def spread_rows(band, dtype):
+    return one_hot((CLASS, FAR), lambda r: r, lambda c: 4 * c + band, dtype)
+
+
+def far_present(band):
+    return iota((CLASS, LANES), 0) % 4 == band
+
+
+def far_kernel(place_ref, q_ref, kv_ref, mid_out_ref, mid_lse_ref, out_ref, lse_ref):
+    band, group = place_ref[0], place_ref[1]
+    k, v = far_keys(kv_ref)
+    q = stack_heads(q_ref[...] * BF16(WIDTH**-0.5))
+    shape = (2 * FAR, HALF * FAR)
+    allowed = iota(shape, 1) <= group % HALF * FAR + iota(shape, 0) % FAR
+    far_out, far_lse = softmax_out(jnp.where(allowed, dot_t(q, k), FLOOR), v)
+    exact = functools.partial(
+        jnp.dot, precision=lax.Precision.HIGHEST, preferred_element_type=F32
+    )
+    spread = spread_rows(band, F32)
+    far_lse = jnp.where(far_present(band), exact(spread, far_lse), FLOOR)
+    out_ref[...], lse_ref[...] = merge(
+        mid_out_ref[...], mid_lse_ref[...], exact(spread, far_out), far_lse
+    )
+
+
+def join_kernel(place_ref, part_ref, mid_out_ref, mid_lse_ref, back_ref):
+    band, group = place_ref[0], place_ref[1]
+    shape = (LANES, FAR // 16 * LANES)
+    row, col = iota(shape, 0), iota(shape, 1)
+    same = (row // 16 == col // LANES) & (row % 16 // 8 == col % LANES // WIDTH)
+    gather = (same & (row % 8 < 3)).astype(F32).astype(BF16)
+    wide = dot(part_ref[FAR:, :], gather)
+    part_lse = jnp.concatenate(
+        [wide[:, b * LANES : (b + 1) * LANES] for b in range(FAR // 16)], axis=0
+    )
+    high = part_lse.astype(BF16)
+    middle = (part_lse - high.astype(F32)).astype(BF16)
+    low = (part_lse - high.astype(F32) - middle.astype(F32)).astype(BF16)
+    spread = spread_rows(band, BF16)
+    present = far_present(band) & (group >= HALF)
+    part_lse = dot(spread, high) + dot(spread, middle) + dot(spread, low)
+    part_lse = jnp.where(present, part_lse, FLOOR)
+    out, lse = merge(
+        mid_out_ref[...], mid_lse_ref[...], dot(spread, part_ref[:FAR, :]), part_lse
+    )
+    parts = lse_part(lse, iota((CLASS, LANES), 1) % WIDTH // 16)
     back_ref[:, :ROWS, :] = out.astype(BF16).reshape(INNER, ROWS, LANES)
     back_ref[:, ROWS:, :] = parts.astype(BF16).reshape(INNER, ROWS, LANES)
 
@@ -162,15 +230,13 @@
         out = dot(order, mine[:, :ROWS, :].reshape(TOK, LANES))
         parts = dot(order, mine[:, ROWS:, :].reshape(TOK, LANES)).astype(BF16)
         lse = dot(parts, gather)
-        near_lse = near_lse_ref[:, cols]
-        top = jnp.maximum(lse, near_lse)
-        w, near_w = jnp.exp(lse - top), jnp.exp(near_lse - top)
-        out_ref[:, cols] = (w * out + near_w * near_out_ref[:, cols]) / (w + near_w)
-
-
-def call(kernel, outs, args, scalars=0, flops=0, exps=0):
+        out_ref[:, cols] = merge(out, lse, near_out_ref[:, cols], near_lse_ref[:, cols])[0]
+
+
+def call(kernel, outs, args, scalars=0, flops=0, exps=0, scratch=(), inside=pltpu.VMEM):
     vmem = pl.BlockSpec(memory_space=pltpu.VMEM)
-    specs = [pl.BlockSpec(memory_space=pltpu.SMEM)] * scalars + [vmem] * (len(args) - scalars)
+    specs = [pl.BlockSpec(memory_space=pltpu.SMEM)] * scalars
+    specs += [pl.BlockSpec(memory_space=inside)] * (len(args) - scalars)
     shapes = [jax.ShapeDtypeStruct(s, t) for s, t in outs]
     moved = sum(a.size * a.dtype.itemsize for a in args)
     moved += sum(s.size * s.dtype.itemsize for s in shapes)
@@ -179,6 +245,7 @@
         out_shape=shapes,
         in_specs=specs,
         out_specs=[vmem] * len(shapes),
+        scratch_shapes=scratch,
         compiler_params=pltpu.CompilerParams(vmem_limit_bytes=40 * 2**20),
         cost_estimate=pl.CostEstimate(flops=flops, bytes_accessed=moved, transcendentals=exps),
     )(*args)
@@ -188,8 +255,13 @@
     group = lax.axis_index("outer")
     place = jnp.stack([lax.axis_index("inner") // 8, group]).astype(jnp.int32)
     full = (TOK, PAIRS * LANES)
+    class_wide = ((CLASS, LANES), F32)
     (packed,) = call(
-        pack_kernel, [((INNER, 3 * ROWS, LANES), BF16)], (queries, key_rows, value_rows)
+        pack_kernel,
+        [((INNER, 3 * ROWS, LANES), BF16)],
+        (queries, key_rows, value_rows),
+        scratch=[pltpu.VMEM((3, *full), BF16), pltpu.SemaphoreType.DMA((3,))],
+        inside=pltpu.HBM,
     )
     got = lax.all_to_all(packed, "inner", 0, 0, tiled=True)
     near_out, near_lse = call(
@@ -201,25 +273,43 @@
     )
     far_q, far_kv = call(
         pick_kernel,
-        [((FAR, LANES), BF16), ((OUTER, 2 * FAR, LANES), BF16)],
+        [((FAR, LANES), BF16), ((HALF, 2 * FAR, LANES), BF16)],
         (place, got),
         scalars=1,
     )
-    all_kv = lax.all_to_all(far_kv, "outer", 0, 0, tiled=True)
+    halves = [list(range(HALF)), list(range(HALF, 2 * HALF))]
+    half_kv = lax.all_to_all(
+        far_kv, "outer", 0, 0, tiled=True, axis_index_groups=halves
+    )
+    their_q = lax.ppermute(far_q, "outer", [(g + HALF, g) for g in range(HALF)])
     mid_out, mid_lse = call(
         mid_kernel,
-        [((CLASS, LANES), F32), ((CLASS, LANES), F32)],
+        [class_wide, class_wide],
         (got,),
         flops=4 * 2 * 512 * 512 * 128,
         exps=2 * 512 * 512,
     )
+    (part,) = call(
+        serve_kernel,
+        [((FAR + 16, LANES), BF16)],
+        (their_q, half_kv),
+        flops=4 * 2 * 128 * 1024 * 128,
+        exps=2 * 128 * 1024,
+    )
+    part = lax.ppermute(part, "outer", [(g, g + HALF) for g in range(HALF)])
+    mid_out, mid_lse = call(
+        far_kernel,
+        [class_wide, class_wide],
+        (place, far_q, half_kv, mid_out, mid_lse),
+        scalars=1,
+        flops=4 * 2 * 128 * 1024 * 128,
+        exps=2 * 128 * 1024,
+    )
     (back,) = call(
-        far_kernel,
+        join_kernel,
         [((INNER, 2 * ROWS, LANES), BF16)],
-        (place, far_q, all_kv, mid_out, mid_lse),
+        (place, part, mid_out, mid_lse),
         scalars=1,
-        flops=4 * 2 * 128 * 2048 * 128,
-        exps=2 * 128 * 2048,
     )
     home = lax.all_to_all(back, "inner", 0, 0, tiled=True)
     (out,) = call(home_kernel, [(full, F32)], (home, near_out, near_lse))

time: 96.6 us -> 84.8 us (0.88)
  the two profiles are of different devices: /device:TPU:8 before, /device:TPU:1 now
where the time goes in v2:
time: 84.8 us; the launch traced here: 83.4 us
  starting transfers between devices  36 us (42%)
  waiting for transfers between devices  33.7 us (40%)
  Pallas kernels  10.8 us (13%)
  local copies, waits for them, and re-layouts  2.72 us (3%)
    all_to_all x1, starting transfers between devices, on_device(): got = lax.all_to_all(packed, 'inner', 0, 0, tiled=True)  17.3 us
    all_to_all x1, waiting for transfers between devices, on_device(): got = lax.all_to_all(packed, 'inner', 0, 0, tiled=True)  14.8 us
    all_to_all x1, waiting for transfers between devices, on_device(): home = lax.all_to_all(back, 'inner', 0, 0, tiled=True)  12.9 us
    pallas_call x8, Pallas kernels, call(): pl.pallas_call(kernel, out_shape=shapes, in_specs=specs, out_specs=[vmem]...  10.8 us
    all_to_all x1, starting transfers between devices, on_device(): lax.all_to_all(far_kv, 'outer', 0, 0, tiled=True, axis_index_groups=halves)  8.01 us
    all_to_all x1, starting transfers between devices, on_device(): home = lax.all_to_all(back, 'inner', 0, 0, tiled=True)  7.51 us
    ppermute x1, waiting for transfers between devices, on_device(): their_q = lax.ppermute(far_q, 'outer', [(g + HALF, g) for g in range(HALF)])  4.36 us
    unnamed x12, local copies, waits for them, and re-layouts  2.72 us
  transfers between devices with their start and end apart: 5, of which 4 were waited for; matrix products, arithmetic and copies ran while one was open for 0% of the time, Pallas kernels for 5%

profile of v2, /device:TPU:1, one launch (start us, length us, event | category | flops | bytes accessed | tf_op | source)
XLA Modules:
  0.0 83.4 jit_solution(5879731863959758119)
XLA Ops:
  0.0 0.9 %copy-done = bf16[64,1024]{1,0:T(8,128)(2,1)S(1)} copy-done((bf16[64,1024]{1,0:T(8,128)(2,1)S(1)}, bf16[64,1024]{1,0:T(8,128)(2,1)}, u32[]{:S(2)}) %copy-start) | copy-done | bytes 131096
  0.9 0.9 %copy-done.2 = bf16[64,1024]{1,0:T(8,128)(2,1)S(1)} copy-done((bf16[64,1024]{1,0:T(8,128)(2,1)S(1)}, bf16[64,1024]{1,0:T(8,128)(2,1)}, u32[]{:S(2)}) %copy-start.2) | copy-done | bytes 131096
  1.8 0.9 %copy-done.4 = bf16[64,1024]{1,0:T(8,128)(2,1)S(1)} copy-done((bf16[64,1024]{1,0:T(8,128)(2,1)S(1)}, bf16[64,1024]{1,0:T(8,128)(2,1)}, u32[]{:S(2)}) %copy-start.4) | copy-done | bytes 131096
  2.7 1.8 %shard_map.37 = bf16[32,48,128]{2,1,0:T(8,128)(2,1)} custom-call(bf16[64,1024]{1,0:T(8,128)(2,1)S(1)} %copy-done, bf16[64,1024]{1,0:T(8,128)(2,1)S(1)} %copy-done.2, bf16[64,1024]{1,0:T(8,128)(2,1)S(1)} %copy-done.4), custom_call_target="tpu_custom_call" | custom-call | bytes 786432 | tf_op jit(solution)/shard_map/pallas_call | solution.py:243
  4.5 17.3 %all-to-all-start = ((bf16[32,48,128]{2,1,0:T(8,128)(2,1)}), bf16[32,48,128]{2,1,0:T(8,128)(2,1)S(1)}, u32[]{:S(2)}, u32[]{:S(2)}) async-start(bf16[32,48,128]{2,1,0:T(8,128)(2,1)} %shard_map.37), calls=%async_computation | async-start | bytes 786432 | tf_op jit(solution)/shard_map/all_to_all | solution.py:266
  21.8 0.1 pad_add_fusion.place_ref
  21.8 14.8 %all-to-all-done.got_ref = bf16[32,48,128]{2,1,0:T(8,128)(2,1)S(1)} async-done(((bf16[32,48,128]{2,1,0:T(8,128)(2,1)}), bf16[32,48,128]{2,1,0:T(8,128)(2,1)S(1)}, u32[]{:S(2)}, u32[]{:S(2)}) %all-to-all-start) | async-done | bytes 393248 | tf_op jit(solution)/shard_map/all_to_all | solution.py:266
  36.6 1.6 %shard_map.38 = (bf16[128,128]{1,0:T(8,128)(2,1)S(1)}, bf16[8,256,128]{2,1,0:T(8,128)(2,1)}) custom-call(s32[2]{0:T(128)S(1)} %pad_add_fusion.place_ref, bf16[32,48,128]{2,1,0:T(8,128)(2,1)S(1)} %all-to-all-done.got_ref), custom_call_target="tpu_custom_call" | custom-call | bytes 950280 | tf_op jit(solution)/shard_map/pallas_call | solution.py:243
  38.2 8.0 %all-to-all-start.1 = ((bf16[8,256,128]{2,1,0:T(8,128)(2,1)}), bf16[8,256,128]{2,1,0:T(8,128)(2,1)S(1)}, u32[]{:S(2)}, u32[]{:S(2)}) async-start(bf16[8,256,128]{2,1,0:T(8,128)(2,1)} %get-tuple-element.14), calls=%async_computation.1 | async-start | bytes 1048576 | tf_op jit(solution)/shard_map/all_to_all | solution.py:281
  46.2 1.3 %collective-permute-start = (bf16[128,128]{1,0:T(8,128)(2,1)S(1)}, bf16[128,128]{1,0:T(8,128)(2,1)S(1)}, u32[]{:S(2)}, u32[]{:S(2)}) collective-permute-start(bf16[128,128]{1,0:T(8,128)(2,1)S(1)} %get-tuple-element.13.q_ref), channel_id=1, source_target_pairs={{256,0},{288,32},{320,64},{352,96},{384,128},{416,160},{448,192},{... | collective-permute-start | bytes 98312 | tf_op jit(solution)/shard_map/ppermute | solution.py:284
  47.5 4.4 %collective-permute-done.q_ref = bf16[128,128]{1,0:T(8,128)(2,1)S(1)} collective-permute-done((bf16[128,128]{1,0:T(8,128)(2,1)S(1)}, bf16[128,128]{1,0:T(8,128)(2,1)S(1)}, u32[]{:S(2)}, u32[]{:S(2)}) %collective-permute-start) | collective-permute-done | bytes 32800 | tf_op jit(solution)/shard_map/ppermute | solution.py:284
  51.9 1.6 %all-to-all-done.1.kv_ref = bf16[8,256,128]{2,1,0:T(8,128)(2,1)S(1)} async-done(((bf16[8,256,128]{2,1,0:T(8,128)(2,1)}), bf16[8,256,128]{2,1,0:T(8,128)(2,1)S(1)}, u32[]{:S(2)}, u32[]{:S(2)}) %all-to-all-start.1) | async-done | bytes 524320 | tf_op jit(solution)/shard_map/all_to_all | solution.py:281
  53.5 0.6 shard_map.39
  54.1 2.0 %collective-permute-start.1 = (bf16[144,128]{1,0:T(8,128)(2,1)S(1)}, bf16[144,128]{1,0:T(8,128)(2,1)S(1)}, u32[]{:S(2)}, u32[]{:S(2)}) collective-permute-start(bf16[144,128]{1,0:T(8,128)(2,1)S(1)} %shard_map.39), channel_id=1, source_target_pairs={{0,256},{32,288},{64,320},{96,352},{128,384},{160,416},{192,448},{... | collective-permute-start | bytes 110600 | tf_op jit(solution)/shard_map/ppermute | solution.py:299
  56.1 1.3 %shard_map.40 = (f32[512,128]{1,0:T(8,128)S(1)}, f32[512,128]{1,0:T(8,128)S(1)}) custom-call(bf16[32,48,128]{2,1,0:T(8,128)(2,1)S(1)} %all-to-all-done.got_ref), custom_call_target="tpu_custom_call" | custom-call | flops 268435456 | bytes 917504 | tf_op jit(solution)/shard_map/pallas_call | solution.py:243
  57.4 1.8 %shard_map.41 = (f32[512,128]{1,0:T(8,128)S(1)}, f32[512,128]{1,0:T(8,128)S(1)}) custom-call(s32[2]{0:T(128)S(1)} %pad_add_fusion.place_ref, bf16[128,128]{1,0:T(8,128)(2,1)S(1)} %get-tuple-element.13.q_ref, bf16[8,256,128]{2,1,0:T(8,128)(2,1)S(1)} %all-to-all-done.1.kv_ref, f32[512,128]{1,0:T(8,128)S(1)} %get-tuple-element.15.mid_out_ref, ...), custom_call_target="tpu_custom_call" | custom-call | flops 134217728 | bytes 1605640 | tf_op jit(solution)/shard_map/pallas_call | solution.py:243
  59.3 0.0 collective-permute-done.1.part_ref
  59.3 1.9 %shard_map.42 = bf16[32,32,128]{2,1,0:T(8,128)(2,1)} custom-call(s32[2]{0:T(128)S(1)} %pad_add_fusion.place_ref, bf16[144,128]{1,0:T(8,128)(2,1)S(1)} %collective-permute-done.1.part_ref, f32[512,128]{1,0:T(8,128)S(1)} %get-tuple-element.17.mid_out_ref, f32[512,128]{1,0:T(8,128)S(1)} %get-tuple-element.18.mid_lse_ref), custom_call_target="tpu_custom_call" | custom-call | bytes 823304 | tf_op jit(solution)/shard_map/pallas_call | solution.py:243
  61.2 7.5 %all-to-all-start.2 = ((bf16[32,32,128]{2,1,0:T(8,128)(2,1)}), bf16[32,32,128]{2,1,0:T(8,128)(2,1)S(1)}, u32[]{:S(2)}, u32[]{:S(2)}) async-start(bf16[32,32,128]{2,1,0:T(8,128)(2,1)} %shard_map.42), calls=%async_computation.2 | async-start | bytes 524288 | tf_op jit(solution)/shard_map/all_to_all | solution.py:314
  68.7 0.0 copy-done.1
  68.7 0.0 copy-done.3
  68.7 0.7 shard_map.43
  69.4 12.9 %all-to-all-done.2.got_ref = bf16[32,32,128]{2,1,0:T(8,128)(2,1)S(1)} async-done(((bf16[32,32,128]{2,1,0:T(8,128)(2,1)}), bf16[32,32,128]{2,1,0:T(8,128)(2,1)S(1)}, u32[]{:S(2)}, u32[]{:S(2)}) %all-to-all-start.2) | async-done | bytes 262176 | tf_op jit(solution)/shard_map/all_to_all | solution.py:314
  82.3 1.1 %shard_map.44 = f32[64,1024]{1,0:T(8,128)} custom-call(bf16[32,32,128]{2,1,0:T(8,128)(2,1)S(1)} %all-to-all-done.2.got_ref, f32[64,1024]{1,0:T(8,128)S(1)} %get-tuple-element.19.near_out_ref, f32[64,1024]{1,0:T(8,128)S(1)} %get-tuple-element.20.near_lse_ref), custom_call_target="tpu_custom_call" | custom-call | bytes 1048576 | tf_op jit(solution)/shard_map/pallas_call | solution.py:243
  (7 shorter events, 0.0 us)
Async XLA Ops:
  0.0 0.9 %copy-start = (bf16[64,1024]{1,0:T(8,128)(2,1)S(1)}, bf16[64,1024]{1,0:T(8,128)(2,1)}, u32[]{:S(2)}) copy-start(bf16[64,1024]{1,0:T(8,128)(2,1)} %q_ref.3) | copy-start | bytes 393220
  0.9 0.9 %copy-start.2 = (bf16[64,1024]{1,0:T(8,128)(2,1)S(1)}, bf16[64,1024]{1,0:T(8,128)(2,1)}, u32[]{:S(2)}) copy-start(bf16[64,1024]{1,0:T(8,128)(2,1)} %k_ref.3) | copy-start | bytes 393220
  1.8 0.9 %copy-start.4 = (bf16[64,1024]{1,0:T(8,128)(2,1)S(1)}, bf16[64,1024]{1,0:T(8,128)(2,1)}, u32[]{:S(2)}) copy-start(bf16[64,1024]{1,0:T(8,128)(2,1)} %v_ref.3) | copy-start | bytes 393220
  4.5 32.1 %all-to-all-start = ((bf16[32,48,128]{2,1,0:T(8,128)(2,1)}), bf16[32,48,128]{2,1,0:T(8,128)(2,1)S(1)}, u32[]{:S(2)}, u32[]{:S(2)}) async-start(bf16[32,48,128]{2,1,0:T(8,128)(2,1)} %shard_map.37), calls=%async_computation | async-start | bytes 786432 | tf_op jit(solution)/shard_map/all_to_all | solution.py:266
  38.2 15.3 %all-to-all-start.1 = ((bf16[8,256,128]{2,1,0:T(8,128)(2,1)}), bf16[8,256,128]{2,1,0:T(8,128)(2,1)S(1)}, u32[]{:S(2)}, u32[]{:S(2)}) async-start(bf16[8,256,128]{2,1,0:T(8,128)(2,1)} %get-tuple-element.14), calls=%async_computation.1 | async-start | bytes 1048576 | tf_op jit(solution)/shard_map/all_to_all | solution.py:281
  46.2 5.6 %collective-permute-start = (bf16[128,128]{1,0:T(8,128)(2,1)S(1)}, bf16[128,128]{1,0:T(8,128)(2,1)S(1)}, u32[]{:S(2)}, u32[]{:S(2)}) collective-permute-start(bf16[128,128]{1,0:T(8,128)(2,1)S(1)} %get-tuple-element.13.q_ref), channel_id=1, source_target_pairs={{256,0},{288,32},{320,64},{352,96},{384,128},{416,160},{448,192},{... | collective-permute-start | bytes 98312 | tf_op jit(solution)/shard_map/ppermute | solution.py:284
  54.1 5.1 %collective-permute-start.1 = (bf16[144,128]{1,0:T(8,128)(2,1)S(1)}, bf16[144,128]{1,0:T(8,128)(2,1)S(1)}, u32[]{:S(2)}, u32[]{:S(2)}) collective-permute-start(bf16[144,128]{1,0:T(8,128)(2,1)S(1)} %shard_map.39), channel_id=1, source_target_pairs={{0,256},{32,288},{64,320},{96,352},{128,384},{160,416},{192,448},{... | collective-permute-start | bytes 110600 | tf_op jit(solution)/shard_map/ppermute | solution.py:299
  61.2 7.5 %copy-start.1 = (bf16[64,1024]{1,0:T(8,128)(2,1)S(1)}, bf16[64,1024]{1,0:T(8,128)(2,1)}, u32[]{:S(2)}) copy-start(bf16[64,1024]{1,0:T(8,128)(2,1)} %q_ref.3) | copy-start | bytes 393220
  61.2 7.5 %copy-start.3 = (bf16[64,1024]{1,0:T(8,128)(2,1)S(1)}, bf16[64,1024]{1,0:T(8,128)(2,1)}, u32[]{:S(2)}) copy-start(bf16[64,1024]{1,0:T(8,128)(2,1)} %k_ref.3) | copy-start | bytes 393220
  61.2 7.5 %copy-start.5 = (bf16[64,1024]{1,0:T(8,128)(2,1)S(1)}, bf16[64,1024]{1,0:T(8,128)(2,1)}, u32[]{:S(2)}) copy-start(bf16[64,1024]{1,0:T(8,128)(2,1)} %v_ref.3) | copy-start | bytes 393220
  61.2 21.2 %all-to-all-start.2 = ((bf16[32,32,128]{2,1,0:T(8,128)(2,1)}), bf16[32,32,128]{2,1,0:T(8,128)(2,1)S(1)}, u32[]{:S(2)}, u32[]{:S(2)}) async-start(bf16[32,32,128]{2,1,0:T(8,128)(2,1)} %shard_map.42), calls=%async_computation.2 | async-start | bytes 524288 | tf_op jit(solution)/shard_map/all_to_all | solution.py:314

commit v3 on v1

v3 whole, which is shorter than its diff:
```python
import jax
import jax.numpy as jnp
from jax import lax
from jax.experimental import pallas as pl
from jax.experimental.pallas import tpu as pltpu
from jax.sharding import PartitionSpec as P

TOK = 64
WIDTH = 64
LANES = 2 * WIDTH
PAIRS = 8
RES = 4
ROWS = TOK // RES
EIGHT = ROWS // 2
INNER = PAIRS * RES
HALF = 8
FOLD = 2
CHUNK = ROWS + EIGHT
CLASS = ROWS * INNER
FAR = CLASS // 4
FLOOR = -1e30
F32 = jnp.float32
BF16 = jnp.bfloat16


def dot(a, b):
    return jnp.dot(a, b, preferred_element_type=F32)


def dot_t(a, b):
    return lax.dot_general(a, b, (((1,), (1,)), ((), ())), preferred_element_type=F32)


def iota(shape, dim):
    return lax.broadcasted_iota(jnp.int32, shape, dim)


def one_hot(shape, row_of, col_of):
    return (row_of(iota(shape, 0)) == col_of(iota(shape, 1))).astype(F32).astype(BF16)


def by_class(r):
    return RES * (r % ROWS) + r // ROWS


def by_half(r):
    return RES * (r // (TOK // 2) * EIGHT + r % EIGHT) + r // EIGHT % RES


def left(shape):
    return iota(shape, len(shape) - 1) < WIDTH


def swap(x):
    return pltpu.roll(x, WIDTH, x.ndim - 1)


def beside(a, b):
    return jnp.where(left(a.shape), a, swap(b))


def beside_right(a, b):
    return jnp.where(left(a.shape), swap(a), b)


def merge(out, lse, other_out, other_lse):
    top = jnp.maximum(lse, other_lse)
    w, other_w = jnp.exp(lse - top), jnp.exp(other_lse - top)
    total = w + other_w
    return (w * out + other_w * other_out) / total, top + jnp.log(total)


def pack_kernel(q_ref, k_ref, v_ref, out_ref, held, sems):
    copies = [
        pltpu.make_async_copy(ref, held.at[at], sems.at[at])
        for at, ref in enumerate((q_ref, k_ref, v_ref))
    ]
    for copy in copies:
        copy.start()
    order = one_hot((TOK, TOK), by_class, lambda c: c)
    sorted_rows = []
    for at, copy in enumerate(copies):
        copy.wait()
        sorted_rows.append(dot(order, held[at]))
    for pair in range(PAIRS):
        cols = slice(pair * LANES, (pair + 1) * LANES)
        q, k, v = (x[:, cols] for x in sorted_rows)
        q = q.reshape(RES, ROWS, LANES)
        for head, join in enumerate((beside, beside_right)):
            kv = join(k, v).reshape(RES, ROWS, LANES)
            chunk = jnp.concatenate([kv, join(q[:, :EIGHT], q[:, EIGHT:])], axis=1)
            at = head * INNER + pair * RES
            out_ref[at : at + RES, :, :] = chunk.astype(BF16)


def near_kernel(q_ref, k_ref, v_ref, out_ref, lse_ref):
    allowed = iota((2 * TOK, TOK), 1) <= iota((2 * TOK, TOK), 0) % TOK
    mine = left((TOK, LANES))
    for pair in range(PAIRS):
        cols = slice(pair * LANES, (pair + 1) * LANES)
        q = q_ref[:, cols] * BF16(WIDTH**-0.5)
        zero = jnp.zeros_like(q)
        q = jnp.concatenate([jnp.where(mine, q, zero), jnp.where(mine, zero, q)], axis=0)
        scores = jnp.where(allowed, dot_t(q, k_ref[:, cols]), FLOOR)
        out, lse = softmax_out(scores, v_ref[:, cols])
        lse = jnp.broadcast_to(lse, out.shape)
        out_ref[:, cols] = jnp.where(mine, out[:TOK], out[TOK:])
        lse_ref[:, cols] = jnp.where(mine, lse[:TOK], lse[TOK:])


def softmax_out(scores, values):
    top = jnp.max(scores, axis=1, keepdims=True)
    weights = jnp.exp(scores - top)
    total = jnp.sum(weights, axis=1, keepdims=True)
    return dot(weights.astype(BF16), values) / total, top + jnp.log(total)


def lse_beside_out(scores, kv):
    out, lse = softmax_out(scores, kv)
    return jnp.where(left(out.shape), jnp.broadcast_to(lse, out.shape), out)


def unpack(got_ref, group):
    chunk = got_ref[group * INNER : (group + 1) * INNER, :, :].astype(F32)
    kv = chunk[:, :ROWS, :].reshape(CLASS, LANES).astype(BF16)
    packed = chunk[:, ROWS:, :] * WIDTH**-0.5
    q = jnp.concatenate([packed, swap(packed)], axis=1)
    q = jnp.where(left(q.shape), q, 0.0)
    return q.reshape(CLASS, LANES).astype(BF16), kv


def pick_kernel(place_ref, got_ref, q_ref, kv_ref):
    band = place_ref[0]
    pick = one_hot((FAR, CLASS), lambda r: 4 * r + band, lambda c: c)
    for group in range(FOLD):
        q, kv = unpack(got_ref, group)
        rows = slice(group * FAR, (group + 1) * FAR)
        q_ref[rows, :] = dot(pick, q).astype(BF16)
        far_kv = dot(pick, kv).astype(BF16)
        for to in range(HALF):
            kv_ref[to, rows, :] = far_kv


def mid_kernel(got_ref, state_ref):
    block = 128
    for group in range(FOLD):
        q, kv = unpack(got_ref, group)
        for start in range(0, CLASS, block):
            end = start + block
            shape = (block, end)
            allowed = iota(shape, 1) <= start + iota(shape, 0)
            scores = jnp.where(allowed, dot_t(q[start:end], kv[:end]), FLOOR)
            at = group * CLASS + start
            state_ref[at : at + block, :] = lse_beside_out(scores, kv[:end])


def far_kernel(place_ref, q_ref, kv_ref, mid_ref, back_ref):
    band, group = place_ref[0], place_ref[1]
    first = kv_ref[:, :FAR, :].reshape(HALF * FAR, LANES)
    second = kv_ref[:, FAR:, :].reshape(HALF * FAR, LANES)
    shape = (FAR, HALF * FAR)
    allowed = iota(shape, 1) <= group * FAR + iota(shape, 0)
    over_first = dot_t(q_ref[...], first)
    over_second = jnp.where(allowed, dot_t(q_ref[FAR:, :], second), FLOOR)
    early = lse_beside_out(jnp.where(allowed, over_first[:FAR], FLOOR), first)
    late = lse_beside_out(
        jnp.concatenate([over_first[FAR:], over_second], axis=1),
        jnp.concatenate([first, second], axis=0),
    )
    spread = one_hot((CLASS, FAR), lambda r: r, lambda c: 4 * c + band)
    present = iota((CLASS, LANES), 0) % 4 == band
    for at, far in enumerate((early, late)):
        high = far.astype(BF16)
        rest = far - high.astype(F32)
        middle = rest.astype(BF16)
        low = (rest - middle.astype(F32)).astype(BF16)
        far = dot(spread, high) + dot(spread, middle) + dot(spread, low)
        mid = mid_ref[at * CLASS : (at + 1) * CLASS, :]
        far_lse = jnp.where(present, swap(far), FLOOR)
        out, lse = merge(mid, swap(mid), far, far_lse)
        high = lse.astype(BF16).astype(F32)
        middle = (lse - high).astype(BF16).astype(F32)
        which = iota(lse.shape, 1) % WIDTH // 16
        parts = jnp.where(which == 1, middle, jnp.where(which == 2, lse - high - middle, 0.0))
        parts = jnp.where(which == 0, high, parts)
        chunks = []
        for x in (out, parts):
            x = x.reshape(INNER, ROWS, LANES)
            chunks.append(beside_right(x[:, :EIGHT], x[:, EIGHT:]))
        back_ref[at * INNER : (at + 1) * INNER, :, :] = jnp.concatenate(chunks, axis=1).astype(BF16)


def home_kernel(got_ref, near_out_ref, near_lse_ref, out_ref):
    order = one_hot((TOK, TOK), lambda r: r, by_half)
    shape = (LANES, LANES)
    row, col = iota(shape, 0), iota(shape, 1)
    gather = (row // WIDTH == col // WIDTH) & (row % 16 == 0)
    gather = gather.astype(F32).astype(BF16)
    for pair in range(PAIRS):
        cols = slice(pair * LANES, (pair + 1) * LANES)
        rows = slice(pair * RES, (pair + 1) * RES)
        a = got_ref[rows, :, :].astype(F32)
        b = got_ref[INNER + pair * RES : INNER + (pair + 1) * RES, :, :].astype(F32)
        both = jnp.concatenate([beside(a, b), beside_right(a, b)], axis=0).astype(F32)
        tall = (TOK, LANES)
        out = dot(order, both[:, :EIGHT, :].reshape(tall).astype(BF16))
        parts = dot(order, both[:, EIGHT:, :].reshape(tall).astype(BF16)).astype(BF16)
        lse = dot(parts, gather)
        out_ref[:, cols] = merge(out, lse, near_out_ref[:, cols], near_lse_ref[:, cols])[0]


def call(kernel, outs, args, scalars=0, flops=0, exps=0, scratch=(), inside=pltpu.VMEM, mib=40):
    vmem = pl.BlockSpec(memory_space=pltpu.VMEM)
    specs = [pl.BlockSpec(memory_space=pltpu.SMEM)] * scalars
    specs += [pl.BlockSpec(memory_space=inside)] * (len(args) - scalars)
    shapes = [jax.ShapeDtypeStruct(s, t) for s, t in outs]
    moved = sum(a.size * a.dtype.itemsize for a in args)
    moved += sum(s.size * s.dtype.itemsize for s in shapes)
    return pl.pallas_call(
        kernel,
        out_shape=shapes,
        in_specs=specs,
        out_specs=[vmem] * len(shapes),
        scratch_shapes=scratch,
        compiler_params=pltpu.CompilerParams(vmem_limit_bytes=mib * 2**20),
        cost_estimate=pl.CostEstimate(flops=flops, bytes_accessed=moved, transcendentals=exps),
    )(*args)


def on_device(queries, key_rows, value_rows):
    group = lax.axis_index("outer") % HALF
    place = jnp.stack([lax.axis_index("inner") // 8, group]).astype(jnp.int32)
    full = (TOK, PAIRS * LANES)
    folded = [
        [(g + HALF * half) * INNER + i for half in range(FOLD) for i in range(INNER)]
        for g in range(HALF)
    ]
    halves = [list(range(half * HALF, (half + 1) * HALF)) for half in range(FOLD)]
    (packed,) = call(
        pack_kernel,
        [((FOLD * INNER, CHUNK, LANES), BF16)],
        (queries, key_rows, value_rows),
        scratch=[pltpu.VMEM((3, *full), BF16), pltpu.SemaphoreType.DMA((3,))],
        inside=pl.ANY,
        mib=60,
    )
    got = lax.all_to_all(
        packed, ("outer", "inner"), 0, 0, tiled=True, axis_index_groups=folded
    )
    near_out, near_lse = call(
        near_kernel,
        [(full, F32), (full, F32)],
        (queries, key_rows, value_rows),
        flops=2 * 16 * 64 * 64 * 128 * 2,
        exps=16 * 64 * 64,
    )
    far_q, far_kv = call(
        pick_kernel,
        [((FOLD * FAR, LANES), BF16), ((HALF, FOLD * FAR, LANES), BF16)],
        (place, got),
        scalars=1,
    )
    all_kv = lax.all_to_all(far_kv, "outer", 0, 0, tiled=True, axis_index_groups=halves)
    (mid,) = call(
        mid_kernel,
        [((FOLD * CLASS, LANES), F32)],
        (got,),
        flops=4 * 2 * 512 * 512 * 128,
        exps=2 * 512 * 512,
    )
    (back,) = call(
        far_kernel,
        [((FOLD * INNER, ROWS, LANES), BF16)],
        (place, far_q, all_kv, mid),
        scalars=1,
        flops=4 * 3 * 128 * 1024 * 128,
        exps=3 * 128 * 1024,
    )
    home = lax.all_to_all(
        back, ("outer", "inner"), 0, 0, tiled=True, axis_index_groups=folded
    )
    (out,) = call(home_kernel, [(full, F32)], (home, near_out, near_lse))
    return out


def solution(mesh):
    rows = P(("outer", "inner"), None)
    return jax.shard_map(
        on_device, mesh=mesh, in_specs=(rows,) * 3, out_specs=rows, check_vma=False
    )
```

time: 96.6 us -> 78.7 us (0.81)
  the two profiles are of different devices: /device:TPU:8 before, /device:TPU:1 now
where the time goes in v3:
time: 78.7 us; the launch traced here: 78.4 us
  waiting for transfers between devices  38.4 us (49%)
  starting transfers between devices  29 us (37%)
  Pallas kernels  10.8 us (14%)
    all_to_all x1, starting transfers between devices, on_device(): lax.all_to_all(packed, ('outer', 'inner'), 0, 0, tiled=True, axis_index_g...  17.7 us
    all_to_all x1, waiting for transfers between devices, on_device(): lax.all_to_all(packed, ('outer', 'inner'), 0, 0, tiled=True, axis_index_g...  17.4 us
    all_to_all x1, waiting for transfers between devices, on_device(): lax.all_to_all(back, ('outer', 'inner'), 0, 0, tiled=True, axis_index_gro...  14.7 us
    pallas_call x6, Pallas kernels, call(): pl.pallas_call(kernel, out_shape=shapes, in_specs=specs, out_specs=[vmem]...  10.8 us
    all_to_all x1, starting transfers between devices, on_device(): lax.all_to_all(back, ('outer', 'inner'), 0, 0, tiled=True, axis_index_gro...  7.34 us
    all_to_all x1, waiting for transfers between devices, on_device(): lax.all_to_all(far_kv, 'outer', 0, 0, tiled=True, axis_index_groups=halves)  6.27 us
    all_to_all x1, starting transfers between devices, on_device(): lax.all_to_all(far_kv, 'outer', 0, 0, tiled=True, axis_index_groups=halves)  4.02 us
  transfers between devices with their start and end apart: 3, of which 3 were waited for; matrix products, arithmetic and copies ran while one was open for 0% of the time, Pallas kernels for 3%

profile of v3, /device:TPU:1, one launch (start us, length us, event | category | flops | bytes accessed | tf_op | source)
XLA Modules:
  0.0 78.4 jit_solution(18203890804916125667)
XLA Ops:
  0.0 2.3 %shard_map.37 = bf16[64,24,128]{2,1,0:T(8,128)(2,1)} custom-call(bf16[64,1024]{1,0:T(8,128)(2,1)} %q_ref.3, bf16[64,1024]{1,0:T(8,128)(2,1)} %k_ref.3, bf16[64,1024]{1,0:T(8,128)(2,1)} %v_ref.3), custom_call_target="tpu_custom_call" | custom-call | bytes 786432 | tf_op jit(solution)/shard_map/pallas_call | solution.py:219
  2.3 17.7 %all-to-all-start = ((bf16[64,24,128]{2,1,0:T(8,128)(2,1)}), bf16[64,24,128]{2,1,0:T(8,128)(2,1)S(1)}, u32[]{:S(2)}, u32[]{:S(2)}) async-start(bf16[64,24,128]{2,1,0:T(8,128)(2,1)} %shard_map.37), calls=%async_computation | async-start | bytes 786432 | tf_op jit(solution)/shard_map/all_to_all | solution.py:247
  20.0 0.1 pad_add_fusion.place_ref
  20.0 17.4 %all-to-all-done.got_ref = bf16[64,24,128]{2,1,0:T(8,128)(2,1)S(1)} async-done(((bf16[64,24,128]{2,1,0:T(8,128)(2,1)}), bf16[64,24,128]{2,1,0:T(8,128)(2,1)S(1)}, u32[]{:S(2)}, u32[]{:S(2)}) %all-to-all-start) | async-done | bytes 393248 | tf_op jit(solution)/shard_map/all_to_all | solution.py:247
  37.4 1.7 %shard_map.38 = (bf16[256,128]{1,0:T(8,128)(2,1)S(1)}, bf16[8,256,128]{2,1,0:T(8,128)(2,1)}) custom-call(s32[2]{0:T(128)S(1)} %pad_add_fusion.place_ref, bf16[64,24,128]{2,1,0:T(8,128)(2,1)S(1)} %all-to-all-done.got_ref), custom_call_target="tpu_custom_call" | custom-call | bytes 983048 | tf_op jit(solution)/shard_map/pallas_call | solution.py:219
  39.1 4.0 %all-to-all-start.1 = ((bf16[8,256,128]{2,1,0:T(8,128)(2,1)}), bf16[8,256,128]{2,1,0:T(8,128)(2,1)S(1)}, u32[]{:S(2)}, u32[]{:S(2)}) async-start(bf16[8,256,128]{2,1,0:T(8,128)(2,1)} %get-tuple-element.10), calls=%async_computation.1 | async-start | bytes 1048576 | tf_op jit(solution)/shard_map/all_to_all | solution.py:263
  43.1 2.0 %shard_map.39.mid_ref = f32[1024,128]{1,0:T(8,128)S(1)} custom-call(bf16[64,24,128]{2,1,0:T(8,128)(2,1)S(1)} %all-to-all-done.got_ref), custom_call_target="tpu_custom_call" | custom-call | flops 268435456 | bytes 917504 | tf_op jit(solution)/shard_map/pallas_call | solution.py:219
  45.1 6.3 %all-to-all-done.1.kv_ref = bf16[8,256,128]{2,1,0:T(8,128)(2,1)S(1)} async-done(((bf16[8,256,128]{2,1,0:T(8,128)(2,1)}), bf16[8,256,128]{2,1,0:T(8,128)(2,1)S(1)}, u32[]{:S(2)}, u32[]{:S(2)}) %all-to-all-start.1) | async-done | bytes 524320 | tf_op jit(solution)/shard_map/all_to_all | solution.py:263
  51.4 2.9 %shard_map.40 = bf16[64,16,128]{2,1,0:T(8,128)(2,1)} custom-call(s32[2]{0:T(128)S(1)} %pad_add_fusion.place_ref, bf16[256,128]{1,0:T(8,128)(2,1)S(1)} %get-tuple-element.9.q_ref, bf16[8,256,128]{2,1,0:T(8,128)(2,1)S(1)} %all-to-all-done.1.kv_ref, f32[1024,128]{1,0:T(8,128)S(1)} %shard_map.39.mid_ref), custom_call_target="tpu_custom_call" | custom-call | flops 201326592 | bytes 1376264 | tf_op jit(solution)/shard_map/pallas_call | solution.py:219
  54.4 0.0 copy-start
  54.4 0.0 copy-start.1
  54.4 0.0 copy-start.2
  54.4 7.3 %all-to-all-start.2 = ((bf16[64,16,128]{2,1,0:T(8,128)(2,1)}), bf16[64,16,128]{2,1,0:T(8,128)(2,1)S(1)}, u32[]{:S(2)}, u32[]{:S(2)}) async-start(bf16[64,16,128]{2,1,0:T(8,128)(2,1)} %shard_map.40), calls=%async_computation.2 | async-start | bytes 524288 | tf_op jit(solution)/shard_map/all_to_all | solution.py:279
  61.7 0.0 copy-done
  61.7 0.0 copy-done.1
  61.7 0.0 copy-done.2
  61.7 0.7 shard_map.41
  62.4 14.7 %all-to-all-done.2.got_ref = bf16[64,16,128]{2,1,0:T(8,128)(2,1)S(1)} async-done(((bf16[64,16,128]{2,1,0:T(8,128)(2,1)}), bf16[64,16,128]{2,1,0:T(8,128)(2,1)S(1)}, u32[]{:S(2)}, u32[]{:S(2)}) %all-to-all-start.2) | async-done | bytes 262176 | tf_op jit(solution)/shard_map/all_to_all | solution.py:279
  77.2 1.2 %shard_map.42 = f32[64,1024]{1,0:T(8,128)} custom-call(bf16[64,16,128]{2,1,0:T(8,128)(2,1)S(1)} %all-to-all-done.2.got_ref, f32[64,1024]{1,0:T(8,128)S(1)} %get-tuple-element.11.near_out_ref, f32[64,1024]{1,0:T(8,128)S(1)} %get-tuple-element.12.near_lse_ref), custom_call_target="tpu_custom_call" | custom-call | bytes 1048576 | tf_op jit(solution)/shard_map/pallas_call | solution.py:219
Async XLA Ops:
  2.3 35.2 %all-to-all-start = ((bf16[64,24,128]{2,1,0:T(8,128)(2,1)}), bf16[64,24,128]{2,1,0:T(8,128)(2,1)S(1)}, u32[]{:S(2)}, u32[]{:S(2)}) async-start(bf16[64,24,128]{2,1,0:T(8,128)(2,1)} %shard_map.37), calls=%async_computation | async-start | bytes 786432 | tf_op jit(solution)/shard_map/all_to_all | solution.py:247
  39.1 12.3 %all-to-all-start.1 = ((bf16[8,256,128]{2,1,0:T(8,128)(2,1)}), bf16[8,256,128]{2,1,0:T(8,128)(2,1)S(1)}, u32[]{:S(2)}, u32[]{:S(2)}) async-start(bf16[8,256,128]{2,1,0:T(8,128)(2,1)} %get-tuple-element.10), calls=%async_computation.1 | async-start | bytes 1048576 | tf_op jit(solution)/shard_map/all_to_all | solution.py:263
  54.4 7.4 %copy-start = (bf16[64,1024]{1,0:T(8,128)(2,1)S(1)}, bf16[64,1024]{1,0:T(8,128)(2,1)}, u32[]{:S(2)}) copy-start(bf16[64,1024]{1,0:T(8,128)(2,1)} %q_ref.3) | copy-start | bytes 393220
  54.4 7.4 %copy-start.1 = (bf16[64,1024]{1,0:T(8,128)(2,1)S(1)}, bf16[64,1024]{1,0:T(8,128)(2,1)}, u32[]{:S(2)}) copy-start(bf16[64,1024]{1,0:T(8,128)(2,1)} %k_ref.3) | copy-start | bytes 393220
  54.4 7.4 %copy-start.2 = (bf16[64,1024]{1,0:T(8,128)(2,1)S(1)}, bf16[64,1024]{1,0:T(8,128)(2,1)}, u32[]{:S(2)}) copy-start(bf16[64,1024]{1,0:T(8,128)(2,1)} %v_ref.3) | copy-start | bytes 393220
  54.4 22.8 %all-to-all-start.2 = ((bf16[64,16,128]{2,1,0:T(8,128)(2,1)}), bf16[64,16,128]{2,1,0:T(8,128)(2,1)S(1)}, u32[]{:S(2)}, u32[]{:S(2)}) async-start(bf16[64,16,128]{2,1,0:T(8,128)(2,1)} %shard_map.40), calls=%async_computation.2 | async-start | bytes 524288 | tf_op jit(solution)/shard_map/all_to_all | solution.py:279

commit v4 on v3

v4 whole, which is shorter than its diff:
```python
import jax
import jax.numpy as jnp
from jax import lax
from jax.experimental import pallas as pl
from jax.experimental.pallas import tpu as pltpu
from jax.sharding import PartitionSpec as P

TOK = 64
WIDTH = 64
LANES = 2 * WIDTH
PAIRS = 8
RES = 4
ROWS = TOK // RES
EIGHT = ROWS // 2
INNER = PAIRS * RES
HALF = 8
FOLD = 2
CHUNK = ROWS + EIGHT
CLASS = ROWS * INNER
FAR = CLASS // 4
FLOOR = -1e30
F32 = jnp.float32
BF16 = jnp.bfloat16


def dot(a, b):
    return jnp.dot(a, b, preferred_element_type=F32)


def dot_t(a, b):
    return lax.dot_general(a, b, (((1,), (1,)), ((), ())), preferred_element_type=F32)


def iota(shape, dim):
    return lax.broadcasted_iota(jnp.int32, shape, dim)


def one_hot(shape, row_of, col_of):
    return (row_of(iota(shape, 0)) == col_of(iota(shape, 1))).astype(F32).astype(BF16)


def by_class(r):
    return RES * (r % ROWS) + r // ROWS


def by_half(r):
    return RES * (r // (TOK // 2) * EIGHT + r % EIGHT) + r // EIGHT % RES


def left(shape):
    return iota(shape, len(shape) - 1) < WIDTH


def swap(x):
    return pltpu.roll(x, WIDTH, x.ndim - 1)


def beside(a, b):
    return jnp.where(left(a.shape), a, swap(b))


def beside_right(a, b):
    return jnp.where(left(a.shape), swap(a), b)


def merge(out, lse, other_out, other_lse):
    top = jnp.maximum(lse, other_lse)
    w, other_w = jnp.exp(lse - top), jnp.exp(other_lse - top)
    total = w + other_w
    return (w * out + other_w * other_out) / total, top + jnp.log(total)


def pack_kernel(q_ref, k_ref, v_ref, out_ref, held, chunks, in_sems, out_sems):
    copies = [
        pltpu.make_async_copy(ref, held.at[at], in_sems.at[at])
        for at, ref in enumerate((k_ref, v_ref, q_ref))
    ]
    for copy in copies:
        copy.start()
    order = one_hot((TOK, TOK), by_class, lambda c: c)
    sorted_rows = []
    for at, copy in enumerate(copies):
        copy.wait()
        sorted_rows.append(dot(order, held[at]))
    sends = []
    for pair in range(PAIRS):
        cols = slice(pair * LANES, (pair + 1) * LANES)
        k, v, q = (x[:, cols] for x in sorted_rows)
        q = q.reshape(RES, ROWS, LANES)
        for head, join in enumerate((beside, beside_right)):
            kv = join(k, v).reshape(RES, ROWS, LANES)
            chunk = jnp.concatenate([kv, join(q[:, :EIGHT], q[:, EIGHT:])], axis=1)
            rows = pl.ds(head * INNER + pair * RES, RES)
            chunks[rows, :, :] = chunk.astype(BF16)
            sends.append(
                pltpu.make_async_copy(
                    chunks.at[rows], out_ref.at[rows], out_sems.at[len(sends)]
                )
            )
            sends[-1].start()
    for send in sends:
        send.wait()


def near_kernel(q_ref, k_ref, v_ref, out_ref, lse_ref):
    allowed = iota((2 * TOK, TOK), 1) <= iota((2 * TOK, TOK), 0) % TOK
    mine = left((TOK, LANES))
    for pair in range(PAIRS):
        cols = slice(pair * LANES, (pair + 1) * LANES)
        q = q_ref[:, cols] * BF16(WIDTH**-0.5)
        zero = jnp.zeros_like(q)
        q = jnp.concatenate([jnp.where(mine, q, zero), jnp.where(mine, zero, q)], axis=0)
        scores = jnp.where(allowed, dot_t(q, k_ref[:, cols]), FLOOR)
        out, lse = softmax_out(scores, v_ref[:, cols])
        lse = jnp.broadcast_to(lse, out.shape)
        out_ref[:, cols] = jnp.where(mine, out[:TOK], out[TOK:])
        lse_ref[:, cols] = jnp.where(mine, lse[:TOK], lse[TOK:])


def softmax_out(scores, values):
    top = jnp.max(scores, axis=1, keepdims=True)
    weights = jnp.exp(scores - top)
    total = jnp.sum(weights, axis=1, keepdims=True)
    return dot(weights.astype(BF16), values) / total, top + jnp.log(total)


def keys_values(got_ref, group):
    return got_ref[group * INNER : (group + 1) * INNER, :ROWS, :].reshape(CLASS, LANES)


def scaled_queries(got_ref, group):
    packed = got_ref[group * INNER : (group + 1) * INNER, ROWS:, :].astype(F32) * WIDTH**-0.5
    q = jnp.concatenate([packed, swap(packed)], axis=1)
    q = jnp.where(left(q.shape), q, 0.0)
    return q.reshape(CLASS, LANES).astype(BF16)


def far_rows(band):
    return one_hot(
        (FAR, CLASS), lambda r: r % INNER * ROWS + r // INNER * 4 + band, lambda c: c
    )


def far_rank(n):
    return n // FAR * FAR + n % INNER * 4 + n % FAR // INNER


def lse_parts(lse):
    high = lse.astype(BF16).astype(F32)
    middle = (lse - high).astype(BF16).astype(F32)
    which = iota(lse.shape, 1) % WIDTH // 16
    parts = jnp.where(which == 1, middle, jnp.where(which == 2, lse - high - middle, 0.0))
    return jnp.where(which == 0, high, parts)


def pick_kernel(place_ref, got_ref, kv_ref, held, sems):
    pick = far_rows(place_ref[0])
    sends = []
    for group in range(FOLD):
        rows = pl.ds(group * FAR, FAR)
        held[rows, :] = dot(pick, keys_values(got_ref, group)).astype(BF16)
        for to in range(HALF):
            sends.append(
                pltpu.make_async_copy(
                    held.at[rows], kv_ref.at[to, rows], sems.at[len(sends)]
                )
            )
            sends[-1].start()
    for send in sends:
        send.wait()


def mid_kernel(place_ref, got_ref, far_q_ref, state_ref, base_ref):
    pick = far_rows(place_ref[0])
    block = 128
    for group in range(FOLD):
        q, kv = scaled_queries(got_ref, group), keys_values(got_ref, group)
        far_q_ref[group * FAR : (group + 1) * FAR, :] = dot(pick, q).astype(BF16)
        for start in range(0, CLASS, block):
            end = start + block
            shape = (block, end)
            allowed = iota(shape, 1) <= start + iota(shape, 0)
            scores = jnp.where(allowed, dot_t(q[start:end], kv[:end]), FLOOR)
            out, lse = softmax_out(scores, kv[:end])
            lse = jnp.broadcast_to(lse, out.shape)
            at = group * CLASS + start
            state_ref[at : at + block, :] = jnp.where(left(out.shape), lse, out)
            packed = []
            for x in (out, lse_parts(lse)):
                x = x.reshape(block // ROWS, ROWS, LANES)
                packed.append(beside_right(x[:, :EIGHT], x[:, EIGHT:]))
            packed = jnp.concatenate(packed, axis=1)
            base_ref[at : at + block, :] = packed.reshape(block, LANES)


def far_kernel(place_ref, q_ref, kv_ref, state_ref, base_ref, back_ref, fresh):
    band, group = place_ref[0], place_ref[1]
    first = kv_ref[:, :FAR, :].reshape(HALF * FAR, LANES)
    second = kv_ref[:, FAR:, :].reshape(HALF * FAR, LANES)
    shape = (FAR, HALF * FAR)
    allowed = far_rank(iota(shape, 1)) <= group * FAR + far_rank(iota(shape, 0))
    over_first = dot_t(q_ref[...], first)
    over_second = jnp.where(allowed, dot_t(q_ref[FAR:, :], second), FLOOR)
    early = softmax_out(jnp.where(allowed, over_first[:FAR], FLOOR), first)
    late = softmax_out(
        jnp.concatenate([over_first[FAR:], over_second], axis=1),
        jnp.concatenate([first, second], axis=0),
    )
    for at, (far_out, far_lse) in enumerate((early, late)):
        start = at * CLASS + band
        mid = jnp.concatenate(
            [state_ref[pl.ds(start + 4 * lot, INNER, stride=ROWS), :] for lot in range(4)], axis=0
        )
        out, lse = merge(mid, swap(mid), far_out, jnp.broadcast_to(far_lse, far_out.shape))
        for x, down in ((out, 0), (lse_parts(lse), EIGHT)):
            for lot in range(2):
                upper = x[lot * INNER : (lot + 1) * INNER]
                lower = x[(lot + 2) * INNER : (lot + 3) * INNER]
                rows = pl.ds(start + down + 4 * lot, INNER, stride=ROWS)
                fresh[rows, :] = beside_right(upper, lower)
    shape = (FOLD * CLASS, LANES)
    back = jnp.where(iota(shape, 0) % 4 == band, fresh[: FOLD * CLASS, :], base_ref[...])
    back_ref[...] = back.astype(BF16).reshape(FOLD * INNER, ROWS, LANES)


def home_kernel(got_ref, near_out_ref, near_lse_ref, out_ref, held, sems):
    order = one_hot((TOK, TOK), lambda r: r, by_half)
    shape = (LANES, LANES)
    row, col = iota(shape, 0), iota(shape, 1)
    gather = (row // WIDTH == col // WIDTH) & (row % 16 == 0)
    gather = gather.astype(F32).astype(BF16)
    sends = []
    for pair in range(PAIRS):
        cols = slice(pair * LANES, (pair + 1) * LANES)
        rows = slice(pair * RES, (pair + 1) * RES)
        a = got_ref[rows, :, :].astype(F32)
        b = got_ref[INNER + pair * RES : INNER + (pair + 1) * RES, :, :].astype(F32)
        both = jnp.concatenate([beside(a, b), beside_right(a, b)], axis=0)
        tall = (TOK, LANES)
        out = dot(order, both[:, :EIGHT, :].reshape(tall).astype(BF16))
        parts = dot(order, both[:, EIGHT:, :].reshape(tall).astype(BF16)).astype(BF16)
        lse = dot(parts, gather)
        held[:, cols] = merge(out, lse, near_out_ref[:, cols], near_lse_ref[:, cols])[0]
        sends.append(
            pltpu.make_async_copy(held.at[:, cols], out_ref.at[:, cols], sems.at[pair])
        )
        sends[-1].start()
    for send in sends:
        send.wait()


def call(
    kernel, outs, args, scalars=0, flops=0, exps=0, scratch=(), inside=None, outside=None, mib=40
):
    vmem = pltpu.VMEM
    specs = [pl.BlockSpec(memory_space=pltpu.SMEM)] * scalars
    specs += [pl.BlockSpec(memory_space=inside or vmem)] * (len(args) - scalars)
    shapes = [jax.ShapeDtypeStruct(s, t) for s, t in outs]
    moved = sum(a.size * a.dtype.itemsize for a in args)
    moved += sum(s.size * s.dtype.itemsize for s in shapes)
    return pl.pallas_call(
        kernel,
        out_shape=shapes,
        in_specs=specs,
        out_specs=[pl.BlockSpec(memory_space=outside or vmem)] * len(shapes),
        scratch_shapes=scratch,
        compiler_params=pltpu.CompilerParams(vmem_limit_bytes=mib * 2**20),
        cost_estimate=pl.CostEstimate(flops=flops, bytes_accessed=moved, transcendentals=exps),
    )(*args)


def on_device(queries, key_rows, value_rows):
    group = lax.axis_index("outer") % HALF
    place = jnp.stack([lax.axis_index("inner") // 8, group]).astype(jnp.int32)
    full = (TOK, PAIRS * LANES)
    tall = (FOLD * CLASS, LANES)
    spare = (FOLD * CLASS + ROWS, LANES)
    dma = pltpu.SemaphoreType.DMA
    folded = [
        [(g + HALF * half) * INNER + i for half in range(FOLD) for i in range(INNER)]
        for g in range(HALF)
    ]
    halves = [list(range(half * HALF, (half + 1) * HALF)) for half in range(FOLD)]
    chunks = (FOLD * INNER, CHUNK, LANES)
    (packed,) = call(
        pack_kernel,
        [(chunks, BF16)],
        (queries, key_rows, value_rows),
        scratch=[
            pltpu.VMEM((3, *full), BF16),
            pltpu.VMEM(chunks, BF16),
            dma((3,)),
            dma((2 * PAIRS,)),
        ],
        inside=pl.ANY,
        outside=pl.ANY,
        mib=60,
    )
    got = lax.all_to_all(
        packed, ("outer", "inner"), 0, 0, tiled=True, axis_index_groups=folded
    )
    near_out, near_lse = call(
        near_kernel,
        [(full, F32), (full, F32)],
        (queries, key_rows, value_rows),
        flops=2 * 16 * 64 * 64 * 128 * 2,
        exps=16 * 64 * 64,
    )
    (far_kv,) = call(
        pick_kernel,
        [((HALF, FOLD * FAR, LANES), BF16)],
        (place, got),
        scalars=1,
        scratch=[pltpu.VMEM((FOLD * FAR, LANES), BF16), dma((FOLD * HALF,))],
        outside=pl.ANY,
    )
    all_kv = lax.all_to_all(far_kv, "outer", 0, 0, tiled=True, axis_index_groups=halves)
    far_q, state, base = call(
        mid_kernel,
        [((FOLD * FAR, LANES), BF16), (spare, F32), (tall, F32)],
        (place, got),
        scalars=1,
        flops=4 * 2 * 512 * 512 * 128,
        exps=2 * 512 * 512,
    )
    (back,) = call(
        far_kernel,
        [((FOLD * INNER, ROWS, LANES), BF16)],
        (place, far_q, all_kv, state, base),
        scalars=1,
        flops=4 * 3 * 128 * 1024 * 128,
        exps=3 * 128 * 1024,
        scratch=[pltpu.VMEM(spare, F32)],
    )
    home = lax.all_to_all(
        back, ("outer", "inner"), 0, 0, tiled=True, axis_index_groups=folded
    )
    (out,) = call(
        home_kernel,
        [(full, F32)],
        (home, near_out, near_lse),
        scratch=[pltpu.VMEM(full, F32), dma((PAIRS,))],
        outside=pl.ANY,
    )
    return out


def solution(mesh):
    rows = P(("outer", "inner"), None)
    return jax.shard_map(
        on_device, mesh=mesh, in_specs=(rows,) * 3, out_specs=rows, check_vma=False
    )
```

time: 78.7 us -> 78.2 us (level)
  waiting for transfers between devices: 38.4 us -> 37.6 us
    all_to_all x1, waiting for transfers between devices: 6.27 us -> 5.43 us  [on_device(): lax.all_to_all(far_kv, 'outer', 0, 0, tiled=True, axis_index_groups=halves)]
  transfers between devices with their start and end apart: 3 -> 3, of which waited for: 3 -> 3; matrix products, arithmetic and copies ran while one was open for 0% -> 0% of each run, Pallas kernels for 3% -> 5%
where the time goes in v4:
time: 78.2 us; the launch traced here: 77.8 us
  waiting for transfers between devices  37.6 us (48%)
  starting transfers between devices  29 us (37%)
  Pallas kernels  11 us (14%)
    all_to_all x1, starting transfers between devices, on_device(): lax.all_to_all(packed, ('outer', 'inner'), 0, 0, tiled=True, axis_index_g...  17.7 us
    all_to_all x1, waiting for transfers between devices, on_device(): lax.all_to_all(packed, ('outer', 'inner'), 0, 0, tiled=True, axis_index_g...  17.4 us
    all_to_all x1, waiting for transfers between devices, on_device(): lax.all_to_all(back, ('outer', 'inner'), 0, 0, tiled=True, axis_index_gro...  14.8 us
    pallas_call x6, Pallas kernels, call(): pl.pallas_call(kernel, out_shape=shapes, in_specs=specs, out_specs=[pl.Bl...  11 us
    all_to_all x1, starting transfers between devices, on_device(): lax.all_to_all(back, ('outer', 'inner'), 0, 0, tiled=True, axis_index_gro...  7.36 us
    all_to_all x1, waiting for transfers between devices, on_device(): lax.all_to_all(far_kv, 'outer', 0, 0, tiled=True, axis_index_groups=halves)  5.43 us
    all_to_all x1, starting transfers between devices, on_device(): lax.all_to_all(far_kv, 'outer', 0, 0, tiled=True, axis_index_groups=halves)  4.03 us
  transfers between devices with their start and end apart: 3, of which 3 were waited for; matrix products, arithmetic and copies ran while one was open for 0% of the time, Pallas kernels for 5%

profile of v4, /device:TPU:1, one launch (start us, length us, event | category | flops | bytes accessed | tf_op | source)
XLA Modules:
  0.0 77.8 jit_solution(2179103941858361335)
XLA Ops:
  0.0 2.4 %shard_map.37 = bf16[64,24,128]{2,1,0:T(8,128)(2,1)} custom-call(bf16[64,1024]{1,0:T(8,128)(2,1)} %q_ref.3, bf16[64,1024]{1,0:T(8,128)(2,1)} %k_ref.3, bf16[64,1024]{1,0:T(8,128)(2,1)} %v_ref.3), custom_call_target="tpu_custom_call" | custom-call | bytes 786432 | tf_op jit(solution)/shard_map/pallas_call | solution.py:261
  2.4 17.7 %all-to-all-start = ((bf16[64,24,128]{2,1,0:T(8,128)(2,1)}), bf16[64,24,128]{2,1,0:T(8,128)(2,1)S(1)}, u32[]{:S(2)}, u32[]{:S(2)}) async-start(bf16[64,24,128]{2,1,0:T(8,128)(2,1)} %shard_map.37), calls=%async_computation | async-start | bytes 786432 | tf_op jit(solution)/shard_map/all_to_all | solution.py:299
  20.1 0.1 pad_add_fusion.place_ref
  20.2 17.4 %all-to-all-done.got_ref = bf16[64,24,128]{2,1,0:T(8,128)(2,1)S(1)} async-done(((bf16[64,24,128]{2,1,0:T(8,128)(2,1)}), bf16[64,24,128]{2,1,0:T(8,128)(2,1)S(1)}, u32[]{:S(2)}, u32[]{:S(2)}) %all-to-all-start) | async-done | bytes 393248 | tf_op jit(solution)/shard_map/all_to_all | solution.py:299
  37.5 1.7 %shard_map.39 = bf16[8,256,128]{2,1,0:T(8,128)(2,1)} custom-call(s32[2]{0:T(128)S(1)} %pad_add_fusion.place_ref, bf16[64,24,128]{2,1,0:T(8,128)(2,1)S(1)} %all-to-all-done.got_ref), custom_call_target="tpu_custom_call" | custom-call | bytes 917512 | tf_op jit(solution)/shard_map/pallas_call | solution.py:261
  39.2 4.0 %all-to-all-start.1 = ((bf16[8,256,128]{2,1,0:T(8,128)(2,1)}), bf16[8,256,128]{2,1,0:T(8,128)(2,1)S(1)}, u32[]{:S(2)}, u32[]{:S(2)}) async-start(bf16[8,256,128]{2,1,0:T(8,128)(2,1)} %shard_map.39), calls=%async_computation.1 | async-start | bytes 1048576 | tf_op jit(solution)/shard_map/all_to_all | solution.py:317
  43.3 2.8 %shard_map.38 = (bf16[256,128]{1,0:T(8,128)(2,1)S(1)}, f32[1040,128]{1,0:T(8,128)S(1)}, f32[1024,128]{1,0:T(8,128)S(1)}) custom-call(s32[2]{0:T(128)S(1)} %pad_add_fusion.place_ref, bf16[64,24,128]{2,1,0:T(8,128)(2,1)S(1)} %all-to-all-done.got_ref), custom_call_target="tpu_custom_call" | custom-call | flops 268435456 | bytes 1515528 | tf_op jit(solution)/shard_map/pallas_call | solution.py:261
  46.1 5.4 %all-to-all-done.1.kv_ref = bf16[8,256,128]{2,1,0:T(8,128)(2,1)S(1)} async-done(((bf16[8,256,128]{2,1,0:T(8,128)(2,1)}), bf16[8,256,128]{2,1,0:T(8,128)(2,1)S(1)}, u32[]{:S(2)}, u32[]{:S(2)}) %all-to-all-start.1) | async-done | bytes 524320 | tf_op jit(solution)/shard_map/all_to_all | solution.py:317
  51.5 2.3 %shard_map.40 = bf16[64,16,128]{2,1,0:T(8,128)(2,1)} custom-call(s32[2]{0:T(128)S(1)} %pad_add_fusion.place_ref, bf16[256,128]{1,0:T(8,128)(2,1)S(1)} %get-tuple-element.10.q_ref, bf16[8,256,128]{2,1,0:T(8,128)(2,1)S(1)} %all-to-all-done.1.kv_ref, f32[1040,128]{1,0:T(8,128)S(1)} %get-tuple-element.11.state_ref, f32[1024,128]{1,0:T(8,128)S(1)} %get-tuple-element.12.base_ref), custom_call_target="tpu_custom_call" | custom-call | flops 201326592 | bytes 1908744 | tf_op jit(solution)/shard_map/pallas_call | solution.py:261
  53.8 0.0 copy-start
  53.8 0.0 copy-start.1
  53.8 0.0 copy-start.2
  53.8 7.4 %all-to-all-start.2 = ((bf16[64,16,128]{2,1,0:T(8,128)(2,1)}), bf16[64,16,128]{2,1,0:T(8,128)(2,1)S(1)}, u32[]{:S(2)}, u32[]{:S(2)}) async-start(bf16[64,16,128]{2,1,0:T(8,128)(2,1)} %shard_map.40), calls=%async_computation.2 | async-start | bytes 524288 | tf_op jit(solution)/shard_map/all_to_all | solution.py:335
  61.2 0.0 copy-done
  61.2 0.0 copy-done.1
  61.2 0.0 copy-done.2
  61.2 0.7 shard_map.41
  61.9 14.8 %all-to-all-done.2.got_ref = bf16[64,16,128]{2,1,0:T(8,128)(2,1)S(1)} async-done(((bf16[64,16,128]{2,1,0:T(8,128)(2,1)}), bf16[64,16,128]{2,1,0:T(8,128)(2,1)S(1)}, u32[]{:S(2)}, u32[]{:S(2)}) %all-to-all-start.2) | async-done | bytes 262176 | tf_op jit(solution)/shard_map/all_to_all | solution.py:335
  76.7 1.2 %shard_map.42 = f32[64,1024]{1,0:T(8,128)} custom-call(bf16[64,16,128]{2,1,0:T(8,128)(2,1)S(1)} %all-to-all-done.2.got_ref, f32[64,1024]{1,0:T(8,128)S(1)} %get-tuple-element.13.near_out_ref, f32[64,1024]{1,0:T(8,128)S(1)} %get-tuple-element.14.near_lse_ref), custom_call_target="tpu_custom_call" | custom-call | bytes 1048576 | tf_op jit(solution)/shard_map/pallas_call | solution.py:261
Async XLA Ops:
  2.4 35.1 %all-to-all-start = ((bf16[64,24,128]{2,1,0:T(8,128)(2,1)}), bf16[64,24,128]{2,1,0:T(8,128)(2,1)S(1)}, u32[]{:S(2)}, u32[]{:S(2)}) async-start(bf16[64,24,128]{2,1,0:T(8,128)(2,1)} %shard_map.37), calls=%async_computation | async-start | bytes 786432 | tf_op jit(solution)/shard_map/all_to_all | solution.py:299
  39.2 12.3 %all-to-all-start.1 = ((bf16[8,256,128]{2,1,0:T(8,128)(2,1)}), bf16[8,256,128]{2,1,0:T(8,128)(2,1)S(1)}, u32[]{:S(2)}, u32[]{:S(2)}) async-start(bf16[8,256,128]{2,1,0:T(8,128)(2,1)} %shard_map.39), calls=%async_computation.1 | async-start | bytes 1048576 | tf_op jit(solution)/shard_map/all_to_all | solution.py:317
  53.8 7.4 %copy-start = (bf16[64,1024]{1,0:T(8,128)(2,1)S(1)}, bf16[64,1024]{1,0:T(8,128)(2,1)}, u32[]{:S(2)}) copy-start(bf16[64,1024]{1,0:T(8,128)(2,1)} %q_ref.3) | copy-start | bytes 393220
  53.8 7.4 %copy-start.1 = (bf16[64,1024]{1,0:T(8,128)(2,1)S(1)}, bf16[64,1024]{1,0:T(8,128)(2,1)}, u32[]{:S(2)}) copy-start(bf16[64,1024]{1,0:T(8,128)(2,1)} %k_ref.3) | copy-start | bytes 393220
  53.8 7.4 %copy-start.2 = (bf16[64,1024]{1,0:T(8,128)(2,1)S(1)}, bf16[64,1024]{1,0:T(8,128)(2,1)}, u32[]{:S(2)}) copy-start(bf16[64,1024]{1,0:T(8,128)(2,1)} %v_ref.3) | copy-start | bytes 393220
  53.8 22.8 %all-to-all-start.2 = ((bf16[64,16,128]{2,1,0:T(8,128)(2,1)}), bf16[64,16,128]{2,1,0:T(8,128)(2,1)S(1)}, u32[]{:S(2)}, u32[]{:S(2)}) async-start(bf16[64,16,128]{2,1,0:T(8,128)(2,1)} %shard_map.40), calls=%async_computation.2 | async-start | bytes 524288 | tf_op jit(solution)/shard_map/all_to_all | solution.py:335

commit v5 on v4

--- a/solution.py
+++ b/solution.py
@@ -70,19 +70,22 @@
     return (w * out + other_w * other_out) / total, top + jnp.log(total)
 
 
-def pack_kernel(q_ref, k_ref, v_ref, out_ref, held, chunks, in_sems, out_sems):
+def copies_in(refs, held, sems):
     copies = [
-        pltpu.make_async_copy(ref, held.at[at], in_sems.at[at])
-        for at, ref in enumerate((k_ref, v_ref, q_ref))
+        pltpu.make_async_copy(ref, held.at[at], sems.at[at]) for at, ref in enumerate(refs)
     ]
     for copy in copies:
         copy.start()
+    return copies
+
+
+def pack_kernel(place_ref, q_ref, k_ref, v_ref, out_ref, held, sems):
+    copies = copies_in((k_ref, v_ref, q_ref), held, sems)
     order = one_hot((TOK, TOK), by_class, lambda c: c)
     sorted_rows = []
     for at, copy in enumerate(copies):
         copy.wait()
         sorted_rows.append(dot(order, held[at]))
-    sends = []
     for pair in range(PAIRS):
         cols = slice(pair * LANES, (pair + 1) * LANES)
         k, v, q = (x[:, cols] for x in sorted_rows)
@@ -90,19 +93,11 @@
         for head, join in enumerate((beside, beside_right)):
             kv = join(k, v).reshape(RES, ROWS, LANES)
             chunk = jnp.concatenate([kv, join(q[:, :EIGHT], q[:, EIGHT:])], axis=1)
-            rows = pl.ds(head * INNER + pair * RES, RES)
-            chunks[rows, :, :] = chunk.astype(BF16)
-            sends.append(
-                pltpu.make_async_copy(
-                    chunks.at[rows], out_ref.at[rows], out_sems.at[len(sends)]
-                )
-            )
-            sends[-1].start()
-    for send in sends:
-        send.wait()
-
-
-def near_kernel(q_ref, k_ref, v_ref, out_ref, lse_ref):
+            at = head * INNER + pair * RES
+            out_ref[at : at + RES, :, :] = chunk.astype(BF16)
+
+
+def near_level(q_ref, k_ref, v_ref, out_ref, lse_ref):
     allowed = iota((2 * TOK, TOK), 1) <= iota((2 * TOK, TOK), 0) % TOK
     mine = left((TOK, LANES))
     for pair in range(PAIRS):
@@ -170,7 +165,21 @@
         send.wait()
 
 
-def mid_kernel(place_ref, got_ref, far_q_ref, state_ref, base_ref):
+def mid_kernel(
+    place_ref,
+    got_ref,
+    q_ref,
+    k_ref,
+    v_ref,
+    far_q_ref,
+    state_ref,
+    base_ref,
+    near_out_ref,
+    near_lse_ref,
+    held,
+    sems,
+):
+    copies = copies_in((q_ref, k_ref, v_ref), held, sems)
     pick = far_rows(place_ref[0])
     block = 128
     for group in range(FOLD):
@@ -191,6 +200,9 @@
                 packed.append(beside_right(x[:, :EIGHT], x[:, EIGHT:]))
             packed = jnp.concatenate(packed, axis=1)
             base_ref[at : at + block, :] = packed.reshape(block, LANES)
+    for copy in copies:
+        copy.wait()
+    near_level(held.at[0], held.at[1], held.at[2], near_out_ref, near_lse_ref)
 
 
 def far_kernel(place_ref, q_ref, kv_ref, state_ref, base_ref, back_ref, fresh):
@@ -249,20 +261,20 @@
         send.wait()
 
 
-def call(
-    kernel, outs, args, scalars=0, flops=0, exps=0, scratch=(), inside=None, outside=None, mib=40
-):
-    vmem = pltpu.VMEM
-    specs = [pl.BlockSpec(memory_space=pltpu.SMEM)] * scalars
-    specs += [pl.BlockSpec(memory_space=inside or vmem)] * (len(args) - scalars)
-    shapes = [jax.ShapeDtypeStruct(s, t) for s, t in outs]
+HBM = pl.BlockSpec(memory_space=pltpu.HBM)
+VMEM = pl.BlockSpec(memory_space=pltpu.VMEM)
+SMEM = pl.BlockSpec(memory_space=pltpu.SMEM)
+
+
+def call(kernel, ins, outs, flops=0, exps=0, scratch=(), mib=40):
+    args, in_specs = [a for a, _ in ins], [s for _, s in ins]
+    shapes = [space.memory_space(s, t) for s, t, space in outs]
     moved = sum(a.size * a.dtype.itemsize for a in args)
-    moved += sum(s.size * s.dtype.itemsize for s in shapes)
     return pl.pallas_call(
         kernel,
         out_shape=shapes,
-        in_specs=specs,
-        out_specs=[pl.BlockSpec(memory_space=outside or vmem)] * len(shapes),
+        in_specs=in_specs,
+        out_specs=[s for *_, s in outs],
         scratch_shapes=scratch,
         compiler_params=pltpu.CompilerParams(vmem_limit_bytes=mib * 2**20),
         cost_estimate=pl.CostEstimate(flops=flops, bytes_accessed=moved, transcendentals=exps),
@@ -281,53 +293,45 @@
         for g in range(HALF)
     ]
     halves = [list(range(half * HALF, (half + 1) * HALF)) for half in range(FOLD)]
-    chunks = (FOLD * INNER, CHUNK, LANES)
+    own = [
+        (pltpu.with_memory_space_constraint(x, pltpu.HBM), HBM)
+        for x in (queries, key_rows, value_rows)
+    ]
+    held = [pltpu.VMEM((3, *full), BF16), dma((3,))]
     (packed,) = call(
         pack_kernel,
-        [(chunks, BF16)],
-        (queries, key_rows, value_rows),
-        scratch=[
-            pltpu.VMEM((3, *full), BF16),
-            pltpu.VMEM(chunks, BF16),
-            dma((3,)),
-            dma((2 * PAIRS,)),
-        ],
-        inside=pl.ANY,
-        outside=pl.ANY,
-        mib=60,
+        [(place, SMEM), *own],
+        [((FOLD * INNER, CHUNK, LANES), BF16, VMEM)],
+        scratch=held,
     )
     got = lax.all_to_all(
         packed, ("outer", "inner"), 0, 0, tiled=True, axis_index_groups=folded
     )
-    near_out, near_lse = call(
-        near_kernel,
-        [(full, F32), (full, F32)],
-        (queries, key_rows, value_rows),
-        flops=2 * 16 * 64 * 64 * 128 * 2,
-        exps=16 * 64 * 64,
-    )
     (far_kv,) = call(
         pick_kernel,
-        [((HALF, FOLD * FAR, LANES), BF16)],
-        (place, got),
-        scalars=1,
+        [(place, SMEM), (got, VMEM)],
+        [((HALF, FOLD * FAR, LANES), BF16, HBM)],
         scratch=[pltpu.VMEM((FOLD * FAR, LANES), BF16), dma((FOLD * HALF,))],
-        outside=pl.ANY,
     )
     all_kv = lax.all_to_all(far_kv, "outer", 0, 0, tiled=True, axis_index_groups=halves)
-    far_q, state, base = call(
+    far_q, state, base, near_out, near_lse = call(
         mid_kernel,
-        [((FOLD * FAR, LANES), BF16), (spare, F32), (tall, F32)],
-        (place, got),
-        scalars=1,
+        [(place, SMEM), (got, VMEM), *own],
+        [
+            ((FOLD * FAR, LANES), BF16, VMEM),
+            (spare, F32, VMEM),
+            (tall, F32, VMEM),
+            (full, F32, VMEM),
+            (full, F32, VMEM),
+        ],
         flops=4 * 2 * 512 * 512 * 128,
         exps=2 * 512 * 512,
+        scratch=held,
     )
     (back,) = call(
         far_kernel,
-        [((FOLD * INNER, ROWS, LANES), BF16)],
-        (place, far_q, all_kv, state, base),
-        scalars=1,
+        [(place, SMEM), (far_q, VMEM), (all_kv, VMEM), (state, VMEM), (base, VMEM)],
+        [((FOLD * INNER, ROWS, LANES), BF16, VMEM)],
         flops=4 * 3 * 128 * 1024 * 128,
         exps=3 * 128 * 1024,
         scratch=[pltpu.VMEM(spare, F32)],
@@ -337,10 +341,9 @@
     )
     (out,) = call(
         home_kernel,
-        [(full, F32)],
-        (home, near_out, near_lse),
+        [(home, VMEM), (near_out, VMEM), (near_lse, VMEM)],
+        [(full, F32, HBM)],
         scratch=[pltpu.VMEM(full, F32), dma((PAIRS,))],
-        outside=pl.ANY,
     )
     return out
 

time: 78.2 us -> 76.6 us (0.980)
  blocking collectives: 0 us -> 57.4 us
  waiting for transfers between devices: 37.6 us -> 4.91 us
  starting transfers between devices: 29 us -> 4.03 us
  Pallas kernels: 11 us -> 9.86 us
    all_to_all x0 -> x2, blocking collectives: none -> 57.4 us  [the longest x1 34.9 us: on_device(): lax.all_to_all(packed, ('outer', 'inner'), 0, 0, tiled=True, axis_index_g...]
    all_to_all x2 -> x0, waiting for transfers between devices: 32.1 us -> none  [the longest x1 17.4 us: on_device(): lax.all_to_all(packed, ('outer', 'inner'), 0, 0, tiled=True, axis_index_g...]
    all_to_all x2 -> x0, starting transfers between devices: 25 us -> none  [the longest x1 17.7 us: on_device(): lax.all_to_all(packed, ('outer', 'inner'), 0, 0, tiled=True, axis_index_g...]
    pallas_call x6 -> x5, Pallas kernels: 11 us -> 9.86 us  [call(): pl.pallas_call(kernel, out_shape=shapes, in_specs=in_specs, out_specs=[s...]
  transfers between devices with their start and end apart: 3 -> 1, of which waited for: 3 -> 1; matrix products, arithmetic and copies ran while one was open for 0% -> 0% of each run, Pallas kernels for 5% -> 4%
where the time goes in v5:
time: 76.6 us; the launch traced here: 76.3 us
  blocking collectives  57.4 us (75%)
  Pallas kernels  9.86 us (13%)
  waiting for transfers between devices  4.91 us (6%)
  starting transfers between devices  4.03 us (5%)
    all_to_all x1, blocking collectives, on_device(): lax.all_to_all(packed, ('outer', 'inner'), 0, 0, tiled=True, axis_index_g...  34.9 us
    all_to_all x1, blocking collectives, on_device(): lax.all_to_all(back, ('outer', 'inner'), 0, 0, tiled=True, axis_index_gro...  22.5 us
    pallas_call x5, Pallas kernels, call(): pl.pallas_call(kernel, out_shape=shapes, in_specs=in_specs, out_specs=[s...  9.86 us
    all_to_all x1, waiting for transfers between devices, on_device(): lax.all_to_all(far_kv, 'outer', 0, 0, tiled=True, axis_index_groups=halves)  4.91 us
    all_to_all x1, starting transfers between devices, on_device(): lax.all_to_all(far_kv, 'outer', 0, 0, tiled=True, axis_index_groups=halves)  4.03 us
  transfers between devices with their start and end apart: 1, of which 1 were waited for; matrix products, arithmetic and copies ran while one was open for 0% of the time, Pallas kernels for 4%

profile of v5, /device:TPU:1, one launch (start us, length us, event | category | flops | bytes accessed | tf_op | source)
XLA Modules:
  0.0 76.3 jit_solution(6422877355185549142)
XLA Ops:
  0.0 0.1 pad_add_fusion.place_ref
  0.1 2.1 %shard_map.37 = bf16[64,24,128]{2,1,0:T(8,128)(2,1)S(1)} custom-call(s32[2]{0:T(128)S(1)} %pad_add_fusion.place_ref, bf16[64,1024]{1,0:T(8,128)(2,1)} %q_ref.3, bf16[64,1024]{1,0:T(8,128)(2,1)} %k_ref.3, bf16[64,1024]{1,0:T(8,128)(2,1)} %v_ref.3), custom_call_target="tpu_custom_call" | custom-call | bytes 393224 | tf_op jit(solution)/shard_map/pallas_call | solution.py:273
  2.1 34.9 %all_to_all.15.got_ref = bf16[64,24,128]{2,1,0:T(8,128)(2,1)S(1)} all-to-all(bf16[64,24,128]{2,1,0:T(8,128)(2,1)S(1)} %shard_map.37), channel_id=1, replica_groups={{0,1,2,3,4,5,6,7,8,9,10,11,12,13,14,15,16,17,18,19,20,21,22,23,24,25,26..., dimensions={0} | all-to-all | bytes 786432 | tf_op jit(solution)/shard_map/all_to_all | solution.py:307
  37.1 1.7 %shard_map.39 = bf16[8,256,128]{2,1,0:T(8,128)(2,1)} custom-call(s32[2]{0:T(128)S(1)} %pad_add_fusion.place_ref, bf16[64,24,128]{2,1,0:T(8,128)(2,1)S(1)} %all_to_all.15.got_ref), custom_call_target="tpu_custom_call" | custom-call | bytes 393224 | tf_op jit(solution)/shard_map/pallas_call | solution.py:273
  38.8 4.0 %all-to-all-start.1 = ((bf16[8,256,128]{2,1,0:T(8,128)(2,1)}), bf16[8,256,128]{2,1,0:T(8,128)(2,1)S(1)}, u32[]{:S(2)}, u32[]{:S(2)}) async-start(bf16[8,256,128]{2,1,0:T(8,128)(2,1)} %shard_map.39), calls=%async_computation.1 | async-start | bytes 1048576 | tf_op jit(solution)/shard_map/all_to_all | solution.py:316
  42.8 3.4 %shard_map.38 = (bf16[256,128]{1,0:T(8,128)(2,1)S(1)}, f32[1040,128]{1,0:T(8,128)S(1)}, f32[1024,128]{1,0:T(8,128)S(1)}, f32[64,1024]{1,0:T(8,128)S(1)}, f32[64,1024]{1,0:T(8,128)S(1)}) custom-call(s32[2]{0:T(128)S(1)} %pad_add_fusion.place_ref, bf16[64,24,128]{2,1,0:T(8,128)(2,1)S(1)} %all_to_all.15.got_ref, bf16[64,1024]{1,0:T(8,128)(2,1)} %q_ref.3, ...), custom_call_target="tpu_custom_call" | custom-call | flops 268435456 | bytes 786440 | tf_op jit(solution)/shard_map/pallas_call | solution.py:273
  46.2 4.9 %all-to-all-done.1.kv_ref = bf16[8,256,128]{2,1,0:T(8,128)(2,1)S(1)} async-done(((bf16[8,256,128]{2,1,0:T(8,128)(2,1)}), bf16[8,256,128]{2,1,0:T(8,128)(2,1)S(1)}, u32[]{:S(2)}, u32[]{:S(2)}) %all-to-all-start.1) | async-done | bytes 524320 | tf_op jit(solution)/shard_map/all_to_all | solution.py:316
  51.1 1.6 %shard_map.40 = bf16[64,16,128]{2,1,0:T(8,128)(2,1)S(1)} custom-call(s32[2]{0:T(128)S(1)} %pad_add_fusion.place_ref, bf16[256,128]{1,0:T(8,128)(2,1)S(1)} %get-tuple-element.10.q_ref, bf16[8,256,128]{2,1,0:T(8,128)(2,1)S(1)} %all-to-all-done.1.kv_ref, f32[1040,128]{1,0:T(8,128)S(1)} %get-tuple-element.11.state_ref, f32[1024,128]{1,0:T(8,128)S(1)} %get-tuple-element.12.base_ref), custom_call_target="tpu_custom_call" | custom-call | flops 201326592 | bytes 1646600 | tf_op jit(solution)/shard_map/pallas_call | solution.py:273
  52.7 22.5 %all_to_all.16.got_ref = bf16[64,16,128]{2,1,0:T(8,128)(2,1)S(1)} all-to-all(bf16[64,16,128]{2,1,0:T(8,128)(2,1)S(1)} %shard_map.40), channel_id=1, replica_groups={{0,1,2,3,4,5,6,7,8,9,10,11,12,13,14,15,16,17,18,19,20,21,22,23,24,25,26..., dimensions={0} | all-to-all | bytes 524288 | tf_op jit(solution)/shard_map/all_to_all | solution.py:339
  75.2 1.2 %shard_map.41 = f32[64,1024]{1,0:T(8,128)} custom-call(bf16[64,16,128]{2,1,0:T(8,128)(2,1)S(1)} %all_to_all.16.got_ref, f32[64,1024]{1,0:T(8,128)S(1)} %get-tuple-element.13.near_out_ref, f32[64,1024]{1,0:T(8,128)S(1)} %get-tuple-element.14.near_lse_ref), custom_call_target="tpu_custom_call" | custom-call | bytes 786432 | tf_op jit(solution)/shard_map/pallas_call | solution.py:273
Async XLA Ops:
  38.8 12.3 %all-to-all-start.1 = ((bf16[8,256,128]{2,1,0:T(8,128)(2,1)}), bf16[8,256,128]{2,1,0:T(8,128)(2,1)S(1)}, u32[]{:S(2)}, u32[]{:S(2)}) async-start(bf16[8,256,128]{2,1,0:T(8,128)(2,1)} %shard_map.39), calls=%async_computation.1 | async-start | bytes 1048576 | tf_op jit(solution)/shard_map/all_to_all | solution.py:316

commit v6 on v5

--- a/solution.py
+++ b/solution.py
@@ -148,43 +148,28 @@
     return jnp.where(which == 0, high, parts)
 
 
-def pick_kernel(place_ref, got_ref, kv_ref, held, sems):
+def pick_kernel(place_ref, got_ref, q_ref, kv_ref):
     pick = far_rows(place_ref[0])
-    sends = []
     for group in range(FOLD):
-        rows = pl.ds(group * FAR, FAR)
-        held[rows, :] = dot(pick, keys_values(got_ref, group)).astype(BF16)
+        rows = slice(group * FAR, (group + 1) * FAR)
+        kv = dot(pick, keys_values(got_ref, group)).astype(BF16)
         for to in range(HALF):
-            sends.append(
-                pltpu.make_async_copy(
-                    held.at[rows], kv_ref.at[to, rows], sems.at[len(sends)]
-                )
-            )
-            sends[-1].start()
-    for send in sends:
-        send.wait()
-
-
-def mid_kernel(
-    place_ref,
-    got_ref,
-    q_ref,
-    k_ref,
-    v_ref,
-    far_q_ref,
-    state_ref,
-    base_ref,
-    near_out_ref,
-    near_lse_ref,
-    held,
-    sems,
-):
-    copies = copies_in((q_ref, k_ref, v_ref), held, sems)
-    pick = far_rows(place_ref[0])
+            kv_ref[to, rows, :] = kv
+        q_ref[rows, :] = dot(pick, scaled_queries(got_ref, group)).astype(BF16)
+
+
+def chunk_rows(out, lse):
+    packed = []
+    for x in (out, lse_parts(lse)):
+        x = x.reshape(x.shape[0] // ROWS, ROWS, LANES)
+        packed.append(beside_right(x[:, :EIGHT], x[:, EIGHT:]))
+    return jnp.concatenate(packed, axis=1).reshape(out.shape)
+
+
+def mid_level(got_ref, state, back):
     block = 128
     for group in range(FOLD):
         q, kv = scaled_queries(got_ref, group), keys_values(got_ref, group)
-        far_q_ref[group * FAR : (group + 1) * FAR, :] = dot(pick, q).astype(BF16)
         for start in range(0, CLASS, block):
             end = start + block
             shape = (block, end)
@@ -193,20 +178,11 @@
             out, lse = softmax_out(scores, kv[:end])
             lse = jnp.broadcast_to(lse, out.shape)
             at = group * CLASS + start
-            state_ref[at : at + block, :] = jnp.where(left(out.shape), lse, out)
-            packed = []
-            for x in (out, lse_parts(lse)):
-                x = x.reshape(block // ROWS, ROWS, LANES)
-                packed.append(beside_right(x[:, :EIGHT], x[:, EIGHT:]))
-            packed = jnp.concatenate(packed, axis=1)
-            base_ref[at : at + block, :] = packed.reshape(block, LANES)
-    for copy in copies:
-        copy.wait()
-    near_level(held.at[0], held.at[1], held.at[2], near_out_ref, near_lse_ref)
-
-
-def far_kernel(place_ref, q_ref, kv_ref, state_ref, base_ref, back_ref, fresh):
-    band, group = place_ref[0], place_ref[1]
+            state[at : at + block, :] = jnp.where(left(out.shape), lse, out)
+            back[at : at + block, :] = chunk_rows(out, lse)
+
+
+def far_level(band, group, q_ref, kv_ref, state, back):
     first = kv_ref[:, :FAR, :].reshape(HALF * FAR, LANES)
     second = kv_ref[:, FAR:, :].reshape(HALF * FAR, LANES)
     shape = (FAR, HALF * FAR)
@@ -221,7 +197,7 @@
     for at, (far_out, far_lse) in enumerate((early, late)):
         start = at * CLASS + band
         mid = jnp.concatenate(
-            [state_ref[pl.ds(start + 4 * lot, INNER, stride=ROWS), :] for lot in range(4)], axis=0
+            [state[pl.ds(start + 4 * lot, INNER, stride=ROWS), :] for lot in range(4)], axis=0
         )
         out, lse = merge(mid, swap(mid), far_out, jnp.broadcast_to(far_lse, far_out.shape))
         for x, down in ((out, 0), (lse_parts(lse), EIGHT)):
@@ -229,10 +205,33 @@
                 upper = x[lot * INNER : (lot + 1) * INNER]
                 lower = x[(lot + 2) * INNER : (lot + 3) * INNER]
                 rows = pl.ds(start + down + 4 * lot, INNER, stride=ROWS)
-                fresh[rows, :] = beside_right(upper, lower)
-    shape = (FOLD * CLASS, LANES)
-    back = jnp.where(iota(shape, 0) % 4 == band, fresh[: FOLD * CLASS, :], base_ref[...])
-    back_ref[...] = back.astype(BF16).reshape(FOLD * INNER, ROWS, LANES)
+                back[rows, :] = beside_right(upper, lower)
+
+
+def attend_kernel(
+    place_ref,
+    got_ref,
+    far_q_ref,
+    kv_ref,
+    q_ref,
+    k_ref,
+    v_ref,
+    back_ref,
+    near_out_ref,
+    near_lse_ref,
+    held,
+    sems,
+    state,
+    back,
+):
+    copies = copies_in((q_ref, k_ref, v_ref), held, sems)
+    mid_level(got_ref, state, back)
+    far_level(place_ref[0], place_ref[1], far_q_ref, kv_ref, state, back)
+    chunks = back[: FOLD * CLASS, :].astype(BF16)
+    back_ref[...] = chunks.reshape(FOLD * INNER, ROWS, LANES)
+    for copy in copies:
+        copy.wait()
+    near_level(held.at[0], held.at[1], held.at[2], near_out_ref, near_lse_ref)
 
 
 def home_kernel(got_ref, near_out_ref, near_lse_ref, out_ref, held, sems):
@@ -285,7 +284,6 @@
     group = lax.axis_index("outer") % HALF
     place = jnp.stack([lax.axis_index("inner") // 8, group]).astype(jnp.int32)
     full = (TOK, PAIRS * LANES)
-    tall = (FOLD * CLASS, LANES)
     spare = (FOLD * CLASS + ROWS, LANES)
     dma = pltpu.SemaphoreType.DMA
     folded = [
@@ -307,34 +305,21 @@
     got = lax.all_to_all(
         packed, ("outer", "inner"), 0, 0, tiled=True, axis_index_groups=folded
     )
-    (far_kv,) = call(
+    far_q, far_kv = call(
         pick_kernel,
         [(place, SMEM), (got, VMEM)],
-        [((HALF, FOLD * FAR, LANES), BF16, HBM)],
-        scratch=[pltpu.VMEM((FOLD * FAR, LANES), BF16), dma((FOLD * HALF,))],
+        [((FOLD * FAR, LANES), BF16, VMEM), ((HALF, FOLD * FAR, LANES), BF16, VMEM)],
     )
     all_kv = lax.all_to_all(far_kv, "outer", 0, 0, tiled=True, axis_index_groups=halves)
-    far_q, state, base, near_out, near_lse = call(
-        mid_kernel,
-        [(place, SMEM), (got, VMEM), *own],
+    back, near_out, near_lse = call(
+        attend_kernel,
+        [(place, SMEM), (got, VMEM), (far_q, VMEM), (all_kv, VMEM), *own],
         [
-            ((FOLD * FAR, LANES), BF16, VMEM),
-            (spare, F32, VMEM),
-            (tall, F32, VMEM),
+            ((FOLD * INNER, ROWS, LANES), BF16, VMEM),
             (full, F32, VMEM),
             (full, F32, VMEM),
         ],
-        flops=4 * 2 * 512 * 512 * 128,
-        exps=2 * 512 * 512,
-        scratch=held,
-    )
-    (back,) = call(
-        far_kernel,
-        [(place, SMEM), (far_q, VMEM), (all_kv, VMEM), (state, VMEM), (base, VMEM)],
-        [((FOLD * INNER, ROWS, LANES), BF16, VMEM)],
-        flops=4 * 3 * 128 * 1024 * 128,
-        exps=3 * 128 * 1024,
-        scratch=[pltpu.VMEM(spare, F32)],
+        scratch=[*held, pltpu.VMEM(spare, F32), pltpu.VMEM(spare, F32)],
     )
     home = lax.all_to_all(
         back, ("outer", "inner"), 0, 0, tiled=True, axis_index_groups=folded

time: 76.6 us -> 79.2 us (1.034)
  blocking collectives: 57.4 us -> 69.5 us
  waiting for transfers between devices: 4.91 us -> 0 us
  starting transfers between devices: 4.03 us -> 0 us
    all_to_all x0 -> x1, blocking collectives: none -> 12.6 us  [on_device(): lax.all_to_all(far_kv, 'outer', 0, 0, tiled=True, axis_index_groups=halves)]
    all_to_all x1 -> x0, waiting for transfers between devices: 4.91 us -> none  [on_device(): lax.all_to_all(far_kv, 'outer', 0, 0, tiled=True, axis_index_groups=halves)]
    all_to_all x1 -> x0, starting transfers between devices: 4.03 us -> none  [on_device(): lax.all_to_all(far_kv, 'outer', 0, 0, tiled=True, axis_index_groups=halves)]
    pallas_call x5 -> x4, Pallas kernels: 9.86 us -> 9.36 us  [call(): pl.pallas_call(kernel, out_shape=shapes, in_specs=in_specs, out_specs=[s...]
  transfers between devices with their start and end apart: 1 -> 0, of which waited for: 1 -> 0; matrix products, arithmetic and copies ran while one was open for 0% -> 0% of each run, Pallas kernels for 4% -> 0%
where the time goes in v6:
time: 79.2 us; the launch traced here: 79 us
  blocking collectives  69.5 us (88%)
  Pallas kernels  9.36 us (12%)
    all_to_all x1, blocking collectives, on_device(): lax.all_to_all(packed, ('outer', 'inner'), 0, 0, tiled=True, axis_index_g...  34.9 us
    all_to_all x1, blocking collectives, on_device(): lax.all_to_all(back, ('outer', 'inner'), 0, 0, tiled=True, axis_index_gro...  22 us
    all_to_all x1, blocking collectives, on_device(): lax.all_to_all(far_kv, 'outer', 0, 0, tiled=True, axis_index_groups=halves)  12.6 us
    pallas_call x4, Pallas kernels, call(): pl.pallas_call(kernel, out_shape=shapes, in_specs=in_specs, out_specs=[s...  9.36 us

profile of v6, /device:TPU:1, one launch (start us, length us, event | category | flops | bytes accessed | tf_op | source)
XLA Modules:
  0.0 79.0 jit_solution(13657933113688848808)
XLA Ops:
  0.0 0.1 pad_add_fusion.place_ref
  0.1 2.1 %shard_map.37 = bf16[64,24,128]{2,1,0:T(8,128)(2,1)S(1)} custom-call(s32[2]{0:T(128)S(1)} %pad_add_fusion.place_ref, bf16[64,1024]{1,0:T(8,128)(2,1)} %q_ref.3, bf16[64,1024]{1,0:T(8,128)(2,1)} %k_ref.3, bf16[64,1024]{1,0:T(8,128)(2,1)} %v_ref.3), custom_call_target="tpu_custom_call" | custom-call | bytes 393224 | tf_op jit(solution)/shard_map/pallas_call | solution.py:272
  2.1 34.9 %all_to_all.15.got_ref = bf16[64,24,128]{2,1,0:T(8,128)(2,1)S(1)} all-to-all(bf16[64,24,128]{2,1,0:T(8,128)(2,1)S(1)} %shard_map.37), channel_id=1, replica_groups={{0,1,2,3,4,5,6,7,8,9,10,11,12,13,14,15,16,17,18,19,20,21,22,23,24,25,26..., dimensions={0} | all-to-all | bytes 786432 | tf_op jit(solution)/shard_map/all_to_all | solution.py:305
  37.1 0.9 %shard_map.38 = (bf16[256,128]{1,0:T(8,128)(2,1)S(1)}, bf16[8,256,128]{2,1,0:T(8,128)(2,1)S(1)}) custom-call(s32[2]{0:T(128)S(1)} %pad_add_fusion.place_ref, bf16[64,24,128]{2,1,0:T(8,128)(2,1)S(1)} %all_to_all.15.got_ref), custom_call_target="tpu_custom_call" | custom-call | bytes 393224 | tf_op jit(solution)/shard_map/pallas_call | solution.py:272
  38.0 12.6 %all_to_all.16.kv_ref = bf16[8,256,128]{2,1,0:T(8,128)(2,1)S(1)} all-to-all(bf16[8,256,128]{2,1,0:T(8,128)(2,1)S(1)} %get-tuple-element.11), channel_id=1, replica_groups={{0,32,64,96,128,160,192,224},{256,288,320,352,384,416,448,480},{1,33,65..., dimensions={0} | all-to-all | bytes 1048576 | tf_op jit(solution)/shard_map/all_to_all | solution.py:313
  50.5 5.3 %shard_map.39 = (bf16[64,16,128]{2,1,0:T(8,128)(2,1)S(1)}, f32[64,1024]{1,0:T(8,128)S(1)}, f32[64,1024]{1,0:T(8,128)S(1)}) custom-call(s32[2]{0:T(128)S(1)} %pad_add_fusion.place_ref, bf16[64,24,128]{2,1,0:T(8,128)(2,1)S(1)} %all_to_all.15.got_ref, bf16[256,128]{1,0:T(8,128)(2,1)S(1)} %get-tuple-element.10.far_q_ref, ...), custom_call_target="tpu_custom_call" | custom-call | bytes 1376264 | tf_op jit(solution)/shard_map/pallas_call | solution.py:272
  55.8 22.0 %all_to_all.17.got_ref = bf16[64,16,128]{2,1,0:T(8,128)(2,1)S(1)} all-to-all(bf16[64,16,128]{2,1,0:T(8,128)(2,1)S(1)} %get-tuple-element.12), channel_id=1, replica_groups={{0,1,2,3,4,5,6,7,8,9,10,11,12,13,14,15,16,17,18,19,20,21,22,23,24,25,26..., dimensions={0} | all-to-all | bytes 524288 | tf_op jit(solution)/shard_map/all_to_all | solution.py:324
  77.8 1.2 %shard_map.40 = f32[64,1024]{1,0:T(8,128)} custom-call(bf16[64,16,128]{2,1,0:T(8,128)(2,1)S(1)} %all_to_all.17.got_ref, f32[64,1024]{1,0:T(8,128)S(1)} %get-tuple-element.13.near_out_ref, f32[64,1024]{1,0:T(8,128)S(1)} %get-tuple-element.14.near_lse_ref), custom_call_target="tpu_custom_call" | custom-call | bytes 786432 | tf_op jit(solution)/shard_map/pallas_call | solution.py:272

commit v7 on v5

--- a/solution.py
+++ b/solution.py
@@ -79,7 +79,7 @@
     return copies
 
 
-def pack_kernel(place_ref, q_ref, k_ref, v_ref, out_ref, held, sems):
+def pack_kernel(q_ref, k_ref, v_ref, out_ref, held, sems):
     copies = copies_in((k_ref, v_ref, q_ref), held, sems)
     order = one_hot((TOK, TOK), by_class, lambda c: c)
     sorted_rows = []
@@ -130,6 +130,10 @@
     return q.reshape(CLASS, LANES).astype(BF16)
 
 
+def place():
+    return lax.axis_index("inner") // (INNER // 4), lax.axis_index("outer") % HALF
+
+
 def far_rows(band):
     return one_hot(
         (FAR, CLASS), lambda r: r % INNER * ROWS + r // INNER * 4 + band, lambda c: c
@@ -148,8 +152,8 @@
     return jnp.where(which == 0, high, parts)
 
 
-def pick_kernel(place_ref, got_ref, kv_ref, held, sems):
-    pick = far_rows(place_ref[0])
+def pick_kernel(got_ref, kv_ref, held, sems):
+    pick = far_rows(place()[0])
     sends = []
     for group in range(FOLD):
         rows = pl.ds(group * FAR, FAR)
@@ -166,7 +170,6 @@
 
 
 def mid_kernel(
-    place_ref,
     got_ref,
     q_ref,
     k_ref,
@@ -180,7 +183,7 @@
     sems,
 ):
     copies = copies_in((q_ref, k_ref, v_ref), held, sems)
-    pick = far_rows(place_ref[0])
+    pick = far_rows(place()[0])
     block = 128
     for group in range(FOLD):
         q, kv = scaled_queries(got_ref, group), keys_values(got_ref, group)
@@ -205,8 +208,8 @@
     near_level(held.at[0], held.at[1], held.at[2], near_out_ref, near_lse_ref)
 
 
-def far_kernel(place_ref, q_ref, kv_ref, state_ref, base_ref, back_ref, fresh):
-    band, group = place_ref[0], place_ref[1]
+def far_kernel(q_ref, kv_ref, state_ref, base_ref, back_ref, fresh):
+    band, group = place()
     first = kv_ref[:, :FAR, :].reshape(HALF * FAR, LANES)
     second = kv_ref[:, FAR:, :].reshape(HALF * FAR, LANES)
     shape = (FAR, HALF * FAR)
@@ -263,7 +266,6 @@
 
 HBM = pl.BlockSpec(memory_space=pltpu.HBM)
 VMEM = pl.BlockSpec(memory_space=pltpu.VMEM)
-SMEM = pl.BlockSpec(memory_space=pltpu.SMEM)
 
 
 def call(kernel, ins, outs, flops=0, exps=0, scratch=(), mib=40):
@@ -282,8 +284,6 @@
 
 
 def on_device(queries, key_rows, value_rows):
-    group = lax.axis_index("outer") % HALF
-    place = jnp.stack([lax.axis_index("inner") // 8, group]).astype(jnp.int32)
     full = (TOK, PAIRS * LANES)
     tall = (FOLD * CLASS, LANES)
     spare = (FOLD * CLASS + ROWS, LANES)
@@ -300,7 +300,7 @@
     held = [pltpu.VMEM((3, *full), BF16), dma((3,))]
     (packed,) = call(
         pack_kernel,
-        [(place, SMEM), *own],
+        [*own],
         [((FOLD * INNER, CHUNK, LANES), BF16, VMEM)],
         scratch=held,
     )
@@ -309,14 +309,14 @@
     )
     (far_kv,) = call(
         pick_kernel,
-        [(place, SMEM), (got, VMEM)],
+        [(got, VMEM)],
         [((HALF, FOLD * FAR, LANES), BF16, HBM)],
         scratch=[pltpu.VMEM((FOLD * FAR, LANES), BF16), dma((FOLD * HALF,))],
     )
     all_kv = lax.all_to_all(far_kv, "outer", 0, 0, tiled=True, axis_index_groups=halves)
     far_q, state, base, near_out, near_lse = call(
         mid_kernel,
-        [(place, SMEM), (got, VMEM), *own],
+        [(got, VMEM), *own],
         [
             ((FOLD * FAR, LANES), BF16, VMEM),
             (spare, F32, VMEM),
@@ -330,7 +330,7 @@
     )
     (back,) = call(
         far_kernel,
-        [(place, SMEM), (far_q, VMEM), (all_kv, VMEM), (state, VMEM), (base, VMEM)],
+        [(far_q, VMEM), (all_kv, VMEM), (state, VMEM), (base, VMEM)],
         [((FOLD * INNER, ROWS, LANES), BF16, VMEM)],
         flops=4 * 3 * 128 * 1024 * 128,
         exps=3 * 128 * 1024,

time: 76.6 us -> 74.9 us (0.978)
  Pallas kernels: 9.86 us -> 7.69 us
    pallas_call x5, Pallas kernels: 9.86 us -> 7.69 us  [call(): pl.pallas_call(kernel, out_shape=shapes, in_specs=in_specs, out_specs=[s...]
where the time goes in v7:
time: 74.9 us; the launch traced here: 74.6 us
  blocking collectives  57.4 us (77%)
  Pallas kernels  7.69 us (10%)
  waiting for transfers between devices  5.44 us (7%)
  starting transfers between devices  4.03 us (5%)
    all_to_all x1, blocking collectives, on_device(): lax.all_to_all(packed, ('outer', 'inner'), 0, 0, tiled=True, axis_index_g...  34.9 us
    all_to_all x1, blocking collectives, on_device(): lax.all_to_all(back, ('outer', 'inner'), 0, 0, tiled=True, axis_index_gro...  22.5 us
    pallas_call x5, Pallas kernels, call(): pl.pallas_call(kernel, out_shape=shapes, in_specs=in_specs, out_specs=[s...  7.69 us
    all_to_all x1, waiting for transfers between devices, on_device(): lax.all_to_all(far_kv, 'outer', 0, 0, tiled=True, axis_index_groups=halves)  5.44 us
    all_to_all x1, starting transfers between devices, on_device(): lax.all_to_all(far_kv, 'outer', 0, 0, tiled=True, axis_index_groups=halves)  4.03 us
  transfers between devices with their start and end apart: 1, of which 1 were waited for; matrix products, arithmetic and copies ran while one was open for 0% of the time, Pallas kernels for 4%

profile of v7, /device:TPU:1, one launch (start us, length us, event | category | flops | bytes accessed | tf_op | source)
XLA Modules:
  0.0 74.6 jit_solution(4421099266751691976)
XLA Ops:
  0.0 1.5 %shard_map.37 = bf16[64,24,128]{2,1,0:T(8,128)(2,1)S(1)} custom-call(bf16[64,1024]{1,0:T(8,128)(2,1)} %q_ref.3, bf16[64,1024]{1,0:T(8,128)(2,1)} %k_ref.3, bf16[64,1024]{1,0:T(8,128)(2,1)} %v_ref.3), custom_call_target="tpu_custom_call" | custom-call | bytes 393216 | tf_op jit(solution)/shard_map/pallas_call | solution.py:275
  1.5 34.9 %all_to_all.15.got_ref = bf16[64,24,128]{2,1,0:T(8,128)(2,1)S(1)} all-to-all(bf16[64,24,128]{2,1,0:T(8,128)(2,1)S(1)} %shard_map.37), channel_id=1, replica_groups={{0,1,2,3,4,5,6,7,8,9,10,11,12,13,14,15,16,17,18,19,20,21,22,23,24,25,26..., dimensions={0} | all-to-all | bytes 786432 | tf_op jit(solution)/shard_map/all_to_all | solution.py:307
  36.5 1.1 %shard_map.39 = bf16[8,256,128]{2,1,0:T(8,128)(2,1)} custom-call(bf16[64,24,128]{2,1,0:T(8,128)(2,1)S(1)} %all_to_all.15.got_ref), custom_call_target="tpu_custom_call" | custom-call | bytes 393216 | tf_op jit(solution)/shard_map/pallas_call | solution.py:275
  37.6 4.0 %all-to-all-start.1 = ((bf16[8,256,128]{2,1,0:T(8,128)(2,1)}), bf16[8,256,128]{2,1,0:T(8,128)(2,1)S(1)}, u32[]{:S(2)}, u32[]{:S(2)}) async-start(bf16[8,256,128]{2,1,0:T(8,128)(2,1)} %shard_map.39), calls=%async_computation.1 | async-start | bytes 1048576 | tf_op jit(solution)/shard_map/all_to_all | solution.py:316
  41.6 2.8 %shard_map.38 = (bf16[256,128]{1,0:T(8,128)(2,1)S(1)}, f32[1040,128]{1,0:T(8,128)S(1)}, f32[1024,128]{1,0:T(8,128)S(1)}, f32[64,1024]{1,0:T(8,128)S(1)}, f32[64,1024]{1,0:T(8,128)S(1)}) custom-call(bf16[64,24,128]{2,1,0:T(8,128)(2,1)S(1)} %all_to_all.15.got_ref, bf16[64,1024]{1,0:T(8,128)(2,1)} %q_ref.3, bf16[64,1024]{1,0:T(8,128)(2,1)} %k_ref.3, ...), custom_call_target="tpu_custom_call" | custom-call | flops 268435456 | bytes 786432 | tf_op jit(solution)/shard_map/pallas_call | solution.py:275
  44.5 5.4 %all-to-all-done.1.kv_ref = bf16[8,256,128]{2,1,0:T(8,128)(2,1)S(1)} async-done(((bf16[8,256,128]{2,1,0:T(8,128)(2,1)}), bf16[8,256,128]{2,1,0:T(8,128)(2,1)S(1)}, u32[]{:S(2)}, u32[]{:S(2)}) %all-to-all-start.1) | async-done | bytes 524320 | tf_op jit(solution)/shard_map/all_to_all | solution.py:316
  49.9 1.1 %shard_map.40 = bf16[64,16,128]{2,1,0:T(8,128)(2,1)S(1)} custom-call(bf16[256,128]{1,0:T(8,128)(2,1)S(1)} %get-tuple-element.10.q_ref, bf16[8,256,128]{2,1,0:T(8,128)(2,1)S(1)} %all-to-all-done.1.kv_ref, f32[1040,128]{1,0:T(8,128)S(1)} %get-tuple-element.11.state_ref, f32[1024,128]{1,0:T(8,128)S(1)} %get-tuple-element.12.base_ref), custom_call_target="tpu_custom_call" | custom-call | flops 201326592 | bytes 1646592 | tf_op jit(solution)/shard_map/pallas_call | solution.py:275
  51.0 22.5 %all_to_all.16.got_ref = bf16[64,16,128]{2,1,0:T(8,128)(2,1)S(1)} all-to-all(bf16[64,16,128]{2,1,0:T(8,128)(2,1)S(1)} %shard_map.40), channel_id=1, replica_groups={{0,1,2,3,4,5,6,7,8,9,10,11,12,13,14,15,16,17,18,19,20,21,22,23,24,25,26..., dimensions={0} | all-to-all | bytes 524288 | tf_op jit(solution)/shard_map/all_to_all | solution.py:339
  73.5 1.2 %shard_map.41 = f32[64,1024]{1,0:T(8,128)} custom-call(bf16[64,16,128]{2,1,0:T(8,128)(2,1)S(1)} %all_to_all.16.got_ref, f32[64,1024]{1,0:T(8,128)S(1)} %get-tuple-element.13.near_out_ref, f32[64,1024]{1,0:T(8,128)S(1)} %get-tuple-element.14.near_lse_ref), custom_call_target="tpu_custom_call" | custom-call | bytes 786432 | tf_op jit(solution)/shard_map/pallas_call | solution.py:275
Async XLA Ops:
  37.6 12.3 %all-to-all-start.1 = ((bf16[8,256,128]{2,1,0:T(8,128)(2,1)}), bf16[8,256,128]{2,1,0:T(8,128)(2,1)S(1)}, u32[]{:S(2)}, u32[]{:S(2)}) async-start(bf16[8,256,128]{2,1,0:T(8,128)(2,1)} %shard_map.39), calls=%async_computation.1 | async-start | bytes 1048576 | tf_op jit(solution)/shard_map/all_to_all | solution.py:316

commit v8 on v7

--- a/solution.py
+++ b/solution.py
@@ -150,6 +150,19 @@
     which = iota(lse.shape, 1) % WIDTH // 16
     parts = jnp.where(which == 1, middle, jnp.where(which == 2, lse - high - middle, 0.0))
     return jnp.where(which == 0, high, parts)
+
+
+def own_column(parts):
+    keep = iota(parts.shape, 2) % 16 == 2 * iota(parts.shape, 1)
+    return jnp.where(keep, parts, 0.0)
+
+
+def open_chunks(chunks):
+    chunks = chunks.astype(F32)
+    rows = [chunks[:, at, :, :] for at in range(EIGHT // 2)]
+    lse = chunks[:, EIGHT // 2, :1, :]
+    rows.append(own_column(jnp.broadcast_to(lse, (lse.shape[0], EIGHT, LANES))))
+    return jnp.concatenate(rows, axis=1)
 
 
 def pick_kernel(got_ref, kv_ref, held, sems):
@@ -235,21 +248,24 @@
                 fresh[rows, :] = beside_right(upper, lower)
     shape = (FOLD * CLASS, LANES)
     back = jnp.where(iota(shape, 0) % 4 == band, fresh[: FOLD * CLASS, :], base_ref[...])
-    back_ref[...] = back.astype(BF16).reshape(FOLD * INNER, ROWS, LANES)
+    back = back.reshape(FOLD * INNER, ROWS, LANES)
+    for at in range(EIGHT // 2):
+        back_ref[:, at, :, :] = back[:, 2 * at : 2 * at + 2, :].astype(BF16)
+    lse = jnp.sum(own_column(back[:, EIGHT:, :]), axis=1, keepdims=True).astype(BF16)
+    back_ref[:, EIGHT // 2, :, :] = jnp.broadcast_to(lse, (FOLD * INNER, 2, LANES))
 
 
 def home_kernel(got_ref, near_out_ref, near_lse_ref, out_ref, held, sems):
     order = one_hot((TOK, TOK), lambda r: r, by_half)
     shape = (LANES, LANES)
     row, col = iota(shape, 0), iota(shape, 1)
-    gather = (row // WIDTH == col // WIDTH) & (row % 16 == 0)
-    gather = gather.astype(F32).astype(BF16)
+    gather = (row // WIDTH == col // WIDTH).astype(F32).astype(BF16)
     sends = []
     for pair in range(PAIRS):
         cols = slice(pair * LANES, (pair + 1) * LANES)
         rows = slice(pair * RES, (pair + 1) * RES)
-        a = got_ref[rows, :, :].astype(F32)
-        b = got_ref[INNER + pair * RES : INNER + (pair + 1) * RES, :, :].astype(F32)
+        a = open_chunks(got_ref[rows])
+        b = open_chunks(got_ref[INNER + pair * RES : INNER + (pair + 1) * RES])
         both = jnp.concatenate([beside(a, b), beside_right(a, b)], axis=0)
         tall = (TOK, LANES)
         out = dot(order, both[:, :EIGHT, :].reshape(tall).astype(BF16))
@@ -331,7 +347,7 @@
     (back,) = call(
         far_kernel,
         [(far_q, VMEM), (all_kv, VMEM), (state, VMEM), (base, VMEM)],
-        [((FOLD * INNER, ROWS, LANES), BF16, VMEM)],
+        [((FOLD * INNER, EIGHT // 2 + 1, 2, LANES), BF16, VMEM)],
         flops=4 * 3 * 128 * 1024 * 128,
         exps=3 * 128 * 1024,
         scratch=[pltpu.VMEM(spare, F32)],

time: 74.9 us -> 73.1 us (0.976)
  blocking collectives: 57.4 us -> 55.4 us
    all_to_all x1, blocking collectives: 22.5 us -> 20.5 us  [on_device(): lax.all_to_all(back, ('outer', 'inner'), 0, 0, tiled=True, axis_index_gro...]
where the time goes in v8:
time: 73.1 us; the launch traced here: 72.8 us
  blocking collectives  55.4 us (76%)
  Pallas kernels  7.9 us (11%)
  waiting for transfers between devices  5.44 us (7%)
  starting transfers between devices  4.03 us (6%)
    all_to_all x1, blocking collectives, on_device(): lax.all_to_all(packed, ('outer', 'inner'), 0, 0, tiled=True, axis_index_g...  34.9 us
    all_to_all x1, blocking collectives, on_device(): lax.all_to_all(back, ('outer', 'inner'), 0, 0, tiled=True, axis_index_gro...  20.5 us
    pallas_call x5, Pallas kernels, call(): pl.pallas_call(kernel, out_shape=shapes, in_specs=in_specs, out_specs=[s...  7.9 us
    all_to_all x1, waiting for transfers between devices, on_device(): lax.all_to_all(far_kv, 'outer', 0, 0, tiled=True, axis_index_groups=halves)  5.44 us
    all_to_all x1, starting transfers between devices, on_device(): lax.all_to_all(far_kv, 'outer', 0, 0, tiled=True, axis_index_groups=halves)  4.03 us
  transfers between devices with their start and end apart: 1, of which 1 were waited for; matrix products, arithmetic and copies ran while one was open for 0% of the time, Pallas kernels for 4%

profile of v8, /device:TPU:1, one launch (start us, length us, event | category | flops | bytes accessed | tf_op | source)
XLA Modules:
  0.0 72.8 jit_solution(9774556946130580001)
XLA Ops:
  0.0 1.5 %shard_map.37 = bf16[64,24,128]{2,1,0:T(8,128)(2,1)S(1)} custom-call(bf16[64,1024]{1,0:T(8,128)(2,1)} %q_ref.3, bf16[64,1024]{1,0:T(8,128)(2,1)} %k_ref.3, bf16[64,1024]{1,0:T(8,128)(2,1)} %v_ref.3), custom_call_target="tpu_custom_call" | custom-call | bytes 393216 | tf_op jit(solution)/shard_map/pallas_call | solution.py:291
  1.5 34.9 %all_to_all.15.got_ref = bf16[64,24,128]{2,1,0:T(8,128)(2,1)S(1)} all-to-all(bf16[64,24,128]{2,1,0:T(8,128)(2,1)S(1)} %shard_map.37), channel_id=1, replica_groups={{0,1,2,3,4,5,6,7,8,9,10,11,12,13,14,15,16,17,18,19,20,21,22,23,24,25,26..., dimensions={0} | all-to-all | bytes 786432 | tf_op jit(solution)/shard_map/all_to_all | solution.py:323
  36.5 1.1 %shard_map.39 = bf16[8,256,128]{2,1,0:T(8,128)(2,1)} custom-call(bf16[64,24,128]{2,1,0:T(8,128)(2,1)S(1)} %all_to_all.15.got_ref), custom_call_target="tpu_custom_call" | custom-call | bytes 393216 | tf_op jit(solution)/shard_map/pallas_call | solution.py:291
  37.6 4.0 %all-to-all-start.1 = ((bf16[8,256,128]{2,1,0:T(8,128)(2,1)}), bf16[8,256,128]{2,1,0:T(8,128)(2,1)S(1)}, u32[]{:S(2)}, u32[]{:S(2)}) async-start(bf16[8,256,128]{2,1,0:T(8,128)(2,1)} %shard_map.39), calls=%async_computation.1 | async-start | bytes 1048576 | tf_op jit(solution)/shard_map/all_to_all | solution.py:332
  41.6 2.8 %shard_map.38 = (bf16[256,128]{1,0:T(8,128)(2,1)S(1)}, f32[1040,128]{1,0:T(8,128)S(1)}, f32[1024,128]{1,0:T(8,128)S(1)}, f32[64,1024]{1,0:T(8,128)S(1)}, f32[64,1024]{1,0:T(8,128)S(1)}) custom-call(bf16[64,24,128]{2,1,0:T(8,128)(2,1)S(1)} %all_to_all.15.got_ref, bf16[64,1024]{1,0:T(8,128)(2,1)} %q_ref.3, bf16[64,1024]{1,0:T(8,128)(2,1)} %k_ref.3, ...), custom_call_target="tpu_custom_call" | custom-call | flops 268435456 | bytes 786432 | tf_op jit(solution)/shard_map/pallas_call | solution.py:291
  44.5 5.4 %all-to-all-done.1.kv_ref = bf16[8,256,128]{2,1,0:T(8,128)(2,1)S(1)} async-done(((bf16[8,256,128]{2,1,0:T(8,128)(2,1)}), bf16[8,256,128]{2,1,0:T(8,128)(2,1)S(1)}, u32[]{:S(2)}, u32[]{:S(2)}) %all-to-all-start.1) | async-done | bytes 524320 | tf_op jit(solution)/shard_map/all_to_all | solution.py:332
  49.9 1.2 %shard_map.40 = bf16[64,5,2,128]{3,2,1,0:T(2,128)(2,1)S(1)} custom-call(bf16[256,128]{1,0:T(8,128)(2,1)S(1)} %get-tuple-element.10.q_ref, bf16[8,256,128]{2,1,0:T(8,128)(2,1)S(1)} %all-to-all-done.1.kv_ref, f32[1040,128]{1,0:T(8,128)S(1)} %get-tuple-element.11.state_ref, f32[1024,128]{1,0:T(8,128)S(1)} %get-tuple-element.12.base_ref), custom_call_target="tpu_custom_call" | custom-call | flops 201326592 | bytes 1646592 | tf_op jit(solution)/shard_map/pallas_call | solution.py:291
  51.1 20.5 %all_to_all.16.got_ref = bf16[64,5,2,128]{3,2,1,0:T(2,128)(2,1)S(1)} all-to-all(bf16[64,5,2,128]{3,2,1,0:T(2,128)(2,1)S(1)} %shard_map.40), channel_id=1, replica_groups={{0,1,2,3,4,5,6,7,8,9,10,11,12,13,14,15,16,17,18,19,20,21,22,23,24,25,26..., dimensions={0} | all-to-all | bytes 327680 | tf_op jit(solution)/shard_map/all_to_all | solution.py:355
  71.6 1.2 %shard_map.41 = f32[64,1024]{1,0:T(8,128)} custom-call(bf16[64,5,2,128]{3,2,1,0:T(2,128)(2,1)S(1)} %all_to_all.16.got_ref, f32[64,1024]{1,0:T(8,128)S(1)} %get-tuple-element.13.near_out_ref, f32[64,1024]{1,0:T(8,128)S(1)} %get-tuple-element.14.near_lse_ref), custom_call_target="tpu_custom_call" | custom-call | bytes 688128 | tf_op jit(solution)/shard_map/pallas_call | solution.py:291
Async XLA Ops:
  37.6 12.3 %all-to-all-start.1 = ((bf16[8,256,128]{2,1,0:T(8,128)(2,1)}), bf16[8,256,128]{2,1,0:T(8,128)(2,1)S(1)}, u32[]{:S(2)}, u32[]{:S(2)}) async-start(bf16[8,256,128]{2,1,0:T(8,128)(2,1)} %shard_map.39), calls=%async_computation.1 | async-start | bytes 1048576 | tf_op jit(solution)/shard_map/all_to_all | solution.py:332

commit v9 on v8

--- a/solution.py
+++ b/solution.py
@@ -214,7 +214,7 @@
             for x in (out, lse_parts(lse)):
                 x = x.reshape(block // ROWS, ROWS, LANES)
                 packed.append(beside_right(x[:, :EIGHT], x[:, EIGHT:]))
-            packed = jnp.concatenate(packed, axis=1)
+            packed = jnp.concatenate([packed[0], own_column(packed[1])], axis=1)
             base_ref[at : at + block, :] = packed.reshape(block, LANES)
     for copy in copies:
         copy.wait()
@@ -222,6 +222,7 @@
 
 
 def far_kernel(q_ref, kv_ref, state_ref, base_ref, back_ref, fresh):
+    fresh[: FOLD * CLASS, :] = base_ref[...]
     band, group = place()
     first = kv_ref[:, :FAR, :].reshape(HALF * FAR, LANES)
     second = kv_ref[:, FAR:, :].reshape(HALF * FAR, LANES)
@@ -230,28 +231,33 @@
     over_first = dot_t(q_ref[...], first)
     over_second = jnp.where(allowed, dot_t(q_ref[FAR:, :], second), FLOOR)
     early = softmax_out(jnp.where(allowed, over_first[:FAR], FLOOR), first)
-    late = softmax_out(
-        jnp.concatenate([over_first[FAR:], over_second], axis=1),
-        jnp.concatenate([first, second], axis=0),
-    )
+    late_first = over_first[FAR:]
+    top = jnp.maximum(
+        jnp.max(late_first, axis=1, keepdims=True), jnp.max(over_second, axis=1, keepdims=True)
+    )
+    w_first, w_second = jnp.exp(late_first - top), jnp.exp(over_second - top)
+    total = jnp.sum(w_first, axis=1, keepdims=True) + jnp.sum(w_second, axis=1, keepdims=True)
+    summed = dot(w_first.astype(BF16), first) + dot(w_second.astype(BF16), second)
+    late = (summed / total, top + jnp.log(total))
     for at, (far_out, far_lse) in enumerate((early, late)):
         start = at * CLASS + band
         mid = jnp.concatenate(
             [state_ref[pl.ds(start + 4 * lot, INNER, stride=ROWS), :] for lot in range(4)], axis=0
         )
         out, lse = merge(mid, swap(mid), far_out, jnp.broadcast_to(far_lse, far_out.shape))
+        column = iota((INNER, LANES), 1) % 16
         for x, down in ((out, 0), (lse_parts(lse), EIGHT)):
             for lot in range(2):
                 upper = x[lot * INNER : (lot + 1) * INNER]
                 lower = x[(lot + 2) * INNER : (lot + 3) * INNER]
-                rows = pl.ds(start + down + 4 * lot, INNER, stride=ROWS)
-                fresh[rows, :] = beside_right(upper, lower)
-    shape = (FOLD * CLASS, LANES)
-    back = jnp.where(iota(shape, 0) % 4 == band, fresh[: FOLD * CLASS, :], base_ref[...])
-    back = back.reshape(FOLD * INNER, ROWS, LANES)
+                rows = beside_right(upper, lower)
+                if down:
+                    rows = jnp.where(column == 2 * (band + 4 * lot), rows, 0.0)
+                fresh[pl.ds(start + down + 4 * lot, INNER, stride=ROWS), :] = rows
+    back = fresh[: FOLD * CLASS, :].reshape(FOLD * INNER, ROWS, LANES)
     for at in range(EIGHT // 2):
         back_ref[:, at, :, :] = back[:, 2 * at : 2 * at + 2, :].astype(BF16)
-    lse = jnp.sum(own_column(back[:, EIGHT:, :]), axis=1, keepdims=True).astype(BF16)
+    lse = jnp.sum(back[:, EIGHT:, :], axis=1, keepdims=True).astype(BF16)
     back_ref[:, EIGHT // 2, :, :] = jnp.broadcast_to(lse, (FOLD * INNER, 2, LANES))
 
 

time: 73.1 us -> 73 us (level)
  no operation moved by 1% of the time
where the time goes in v9:
time: 73 us; the launch traced here: 72.7 us
  blocking collectives  55.4 us (76%)
  Pallas kernels  7.83 us (11%)
  waiting for transfers between devices  5.41 us (7%)
  starting transfers between devices  4.03 us (6%)
    all_to_all x1, blocking collectives, on_device(): lax.all_to_all(packed, ('outer', 'inner'), 0, 0, tiled=True, axis_index_g...  34.9 us
    all_to_all x1, blocking collectives, on_device(): lax.all_to_all(back, ('outer', 'inner'), 0, 0, tiled=True, axis_index_gro...  20.5 us
    pallas_call x5, Pallas kernels, call(): pl.pallas_call(kernel, out_shape=shapes, in_specs=in_specs, out_specs=[s...  7.83 us
    all_to_all x1, waiting for transfers between devices, on_device(): lax.all_to_all(far_kv, 'outer', 0, 0, tiled=True, axis_index_groups=halves)  5.41 us
    all_to_all x1, starting transfers between devices, on_device(): lax.all_to_all(far_kv, 'outer', 0, 0, tiled=True, axis_index_groups=halves)  4.03 us
  transfers between devices with their start and end apart: 1, of which 1 were waited for; matrix products, arithmetic and copies ran while one was open for 0% of the time, Pallas kernels for 4%

profile of v9, /device:TPU:1, one launch (start us, length us, event | category | flops | bytes accessed | tf_op | source)
XLA Modules:
  0.0 72.7 jit_solution(8439532699124257893)
XLA Ops:
  0.0 1.5 %shard_map.37 = bf16[64,24,128]{2,1,0:T(8,128)(2,1)S(1)} custom-call(bf16[64,1024]{1,0:T(8,128)(2,1)} %q_ref.3, bf16[64,1024]{1,0:T(8,128)(2,1)} %k_ref.3, bf16[64,1024]{1,0:T(8,128)(2,1)} %v_ref.3), custom_call_target="tpu_custom_call" | custom-call | bytes 393216 | tf_op jit(solution)/shard_map/pallas_call | solution.py:297
  1.5 34.9 %all_to_all.15.got_ref = bf16[64,24,128]{2,1,0:T(8,128)(2,1)S(1)} all-to-all(bf16[64,24,128]{2,1,0:T(8,128)(2,1)S(1)} %shard_map.37), channel_id=1, replica_groups={{0,1,2,3,4,5,6,7,8,9,10,11,12,13,14,15,16,17,18,19,20,21,22,23,24,25,26..., dimensions={0} | all-to-all | bytes 786432 | tf_op jit(solution)/shard_map/all_to_all | solution.py:329
  36.5 1.1 %shard_map.39 = bf16[8,256,128]{2,1,0:T(8,128)(2,1)} custom-call(bf16[64,24,128]{2,1,0:T(8,128)(2,1)S(1)} %all_to_all.15.got_ref), custom_call_target="tpu_custom_call" | custom-call | bytes 393216 | tf_op jit(solution)/shard_map/pallas_call | solution.py:297
  37.6 4.0 %all-to-all-start.1 = ((bf16[8,256,128]{2,1,0:T(8,128)(2,1)}), bf16[8,256,128]{2,1,0:T(8,128)(2,1)S(1)}, u32[]{:S(2)}, u32[]{:S(2)}) async-start(bf16[8,256,128]{2,1,0:T(8,128)(2,1)} %shard_map.39), calls=%async_computation.1 | async-start | bytes 1048576 | tf_op jit(solution)/shard_map/all_to_all | solution.py:338
  41.6 2.9 %shard_map.38 = (bf16[256,128]{1,0:T(8,128)(2,1)S(1)}, f32[1040,128]{1,0:T(8,128)S(1)}, f32[1024,128]{1,0:T(8,128)S(1)}, f32[64,1024]{1,0:T(8,128)S(1)}, f32[64,1024]{1,0:T(8,128)S(1)}) custom-call(bf16[64,24,128]{2,1,0:T(8,128)(2,1)S(1)} %all_to_all.15.got_ref, bf16[64,1024]{1,0:T(8,128)(2,1)} %q_ref.3, bf16[64,1024]{1,0:T(8,128)(2,1)} %k_ref.3, ...), custom_call_target="tpu_custom_call" | custom-call | flops 268435456 | bytes 786432 | tf_op jit(solution)/shard_map/pallas_call | solution.py:297
  44.5 5.4 %all-to-all-done.1.kv_ref = bf16[8,256,128]{2,1,0:T(8,128)(2,1)S(1)} async-done(((bf16[8,256,128]{2,1,0:T(8,128)(2,1)}), bf16[8,256,128]{2,1,0:T(8,128)(2,1)S(1)}, u32[]{:S(2)}, u32[]{:S(2)}) %all-to-all-start.1) | async-done | bytes 524320 | tf_op jit(solution)/shard_map/all_to_all | solution.py:338
  49.9 1.1 %shard_map.40 = bf16[64,5,2,128]{3,2,1,0:T(2,128)(2,1)S(1)} custom-call(bf16[256,128]{1,0:T(8,128)(2,1)S(1)} %get-tuple-element.10.q_ref, bf16[8,256,128]{2,1,0:T(8,128)(2,1)S(1)} %all-to-all-done.1.kv_ref, f32[1040,128]{1,0:T(8,128)S(1)} %get-tuple-element.11.state_ref, f32[1024,128]{1,0:T(8,128)S(1)} %get-tuple-element.12.base_ref), custom_call_target="tpu_custom_call" | custom-call | flops 201326592 | bytes 1646592 | tf_op jit(solution)/shard_map/pallas_call | solution.py:297
  51.0 20.5 %all_to_all.16.got_ref = bf16[64,5,2,128]{3,2,1,0:T(2,128)(2,1)S(1)} all-to-all(bf16[64,5,2,128]{3,2,1,0:T(2,128)(2,1)S(1)} %shard_map.40), channel_id=1, replica_groups={{0,1,2,3,4,5,6,7,8,9,10,11,12,13,14,15,16,17,18,19,20,21,22,23,24,25,26..., dimensions={0} | all-to-all | bytes 327680 | tf_op jit(solution)/shard_map/all_to_all | solution.py:361
  71.5 1.2 %shard_map.41 = f32[64,1024]{1,0:T(8,128)} custom-call(bf16[64,5,2,128]{3,2,1,0:T(2,128)(2,1)S(1)} %all_to_all.16.got_ref, f32[64,1024]{1,0:T(8,128)S(1)} %get-tuple-element.13.near_out_ref, f32[64,1024]{1,0:T(8,128)S(1)} %get-tuple-element.14.near_lse_ref), custom_call_target="tpu_custom_call" | custom-call | bytes 688128 | tf_op jit(solution)/shard_map/pallas_call | solution.py:297
Async XLA Ops:
  37.6 12.3 %all-to-all-start.1 = ((bf16[8,256,128]{2,1,0:T(8,128)(2,1)}), bf16[8,256,128]{2,1,0:T(8,128)(2,1)S(1)}, u32[]{:S(2)}, u32[]{:S(2)}) async-start(bf16[8,256,128]{2,1,0:T(8,128)(2,1)} %shard_map.39), calls=%async_computation.1 | async-start | bytes 1048576 | tf_op jit(solution)/shard_map/all_to_all | solution.py:338

commit v10 on v9

--- a/solution.py
+++ b/solution.py
@@ -130,8 +130,14 @@
     return q.reshape(CLASS, LANES).astype(BF16)
 
 
+def partner(group):
+    return group ^ (HALF + HALF // 2)
+
+
 def place():
-    return lax.axis_index("inner") // (INNER // 4), lax.axis_index("outer") % HALF
+    outer = lax.axis_index("outer")
+    group = jnp.where(outer < HALF, outer, partner(outer))
+    return lax.axis_index("inner") // (INNER // 4), group
 
 
 def far_rows(band):
@@ -229,7 +235,9 @@
     shape = (FAR, HALF * FAR)
     allowed = far_rank(iota(shape, 1)) <= group * FAR + far_rank(iota(shape, 0))
     over_first = dot_t(q_ref[...], first)
-    over_second = jnp.where(allowed, dot_t(q_ref[FAR:, :], second), FLOOR)
+    late_rank = far_rank(iota(shape, 1) ^ (HALF // 2 * FAR))
+    allowed_late = late_rank <= (group ^ (HALF // 2)) * FAR + far_rank(iota(shape, 0))
+    over_second = jnp.where(allowed_late, dot_t(q_ref[FAR:, :], second), FLOOR)
     early = softmax_out(jnp.where(allowed, over_first[:FAR], FLOOR), first)
     late_first = over_first[FAR:]
     top = jnp.maximum(
@@ -311,10 +319,10 @@
     spare = (FOLD * CLASS + ROWS, LANES)
     dma = pltpu.SemaphoreType.DMA
     folded = [
-        [(g + HALF * half) * INNER + i for half in range(FOLD) for i in range(INNER)]
+        [shared * INNER + i for shared in (g, partner(g)) for i in range(INNER)]
         for g in range(HALF)
     ]
-    halves = [list(range(half * HALF, (half + 1) * HALF)) for half in range(FOLD)]
+    halves = [list(range(HALF)), [partner(g) for g in range(HALF)]]
     own = [
         (pltpu.with_memory_space_constraint(x, pltpu.HBM), HBM)
         for x in (queries, key_rows, value_rows)

time: 73 us -> 72.1 us (0.988)
  blocking collectives: 55.4 us -> 52 us
  starting transfers between devices: 4.03 us -> 5.88 us
    all_to_all x1, blocking collectives: 20.5 us -> 18.4 us  [on_device(): lax.all_to_all(back, ('outer', 'inner'), 0, 0, tiled=True, axis_index_gro...]
    all_to_all x1, starting transfers between devices: 4.03 us -> 5.88 us  [on_device(): lax.all_to_all(far_kv, 'outer', 0, 0, tiled=True, axis_index_groups=halves)]
    all_to_all x1, blocking collectives: 34.9 us -> 33.6 us  [on_device(): lax.all_to_all(packed, ('outer', 'inner'), 0, 0, tiled=True, axis_index_g...]
where the time goes in v10:
time: 72.1 us; the launch traced here: 71.8 us
  blocking collectives  52 us (72%)
  Pallas kernels  7.83 us (11%)
  waiting for transfers between devices  6.11 us (8%)
  starting transfers between devices  5.88 us (8%)
    all_to_all x1, blocking collectives, on_device(): lax.all_to_all(packed, ('outer', 'inner'), 0, 0, tiled=True, axis_index_g...  33.6 us
    all_to_all x1, blocking collectives, on_device(): lax.all_to_all(back, ('outer', 'inner'), 0, 0, tiled=True, axis_index_gro...  18.4 us
    pallas_call x5, Pallas kernels, call(): pl.pallas_call(kernel, out_shape=shapes, in_specs=in_specs, out_specs=[s...  7.83 us
    all_to_all x1, waiting for transfers between devices, on_device(): lax.all_to_all(far_kv, 'outer', 0, 0, tiled=True, axis_index_groups=halves)  6.11 us
    all_to_all x1, starting transfers between devices, on_device(): lax.all_to_all(far_kv, 'outer', 0, 0, tiled=True, axis_index_groups=halves)  5.88 us
  transfers between devices with their start and end apart: 1, of which 1 were waited for; matrix products, arithmetic and copies ran while one was open for 0% of the time, Pallas kernels for 4%

profile of v10, /device:TPU:1, one launch (start us, length us, event | category | flops | bytes accessed | tf_op | source)
XLA Modules:
  0.0 71.8 jit_solution(5578944380808218198)
XLA Ops:
  0.0 1.5 %shard_map.37 = bf16[64,24,128]{2,1,0:T(8,128)(2,1)S(1)} custom-call(bf16[64,1024]{1,0:T(8,128)(2,1)} %q_ref.3, bf16[64,1024]{1,0:T(8,128)(2,1)} %k_ref.3, bf16[64,1024]{1,0:T(8,128)(2,1)} %v_ref.3), custom_call_target="tpu_custom_call" | custom-call | bytes 393216 | tf_op jit(solution)/shard_map/pallas_call | solution.py:305
  1.5 33.6 %all_to_all.15.got_ref = bf16[64,24,128]{2,1,0:T(8,128)(2,1)S(1)} all-to-all(bf16[64,24,128]{2,1,0:T(8,128)(2,1)S(1)} %shard_map.37), channel_id=1, replica_groups={{0,1,2,3,4,5,6,7,8,9,10,11,12,13,14,15,16,17,18,19,20,21,22,23,24,25,26..., dimensions={0} | all-to-all | bytes 786432 | tf_op jit(solution)/shard_map/all_to_all | solution.py:337
  35.1 1.1 %shard_map.39 = bf16[8,256,128]{2,1,0:T(8,128)(2,1)} custom-call(bf16[64,24,128]{2,1,0:T(8,128)(2,1)S(1)} %all_to_all.15.got_ref), custom_call_target="tpu_custom_call" | custom-call | bytes 393216 | tf_op jit(solution)/shard_map/pallas_call | solution.py:305
  36.2 5.9 %all-to-all-start.1 = ((bf16[8,256,128]{2,1,0:T(8,128)(2,1)}), bf16[8,256,128]{2,1,0:T(8,128)(2,1)S(1)}, u32[]{:S(2)}, u32[]{:S(2)}) async-start(bf16[8,256,128]{2,1,0:T(8,128)(2,1)} %shard_map.39), calls=%async_computation.1 | async-start | bytes 1048576 | tf_op jit(solution)/shard_map/all_to_all | solution.py:346
  42.1 2.9 %shard_map.38 = (bf16[256,128]{1,0:T(8,128)(2,1)S(1)}, f32[1040,128]{1,0:T(8,128)S(1)}, f32[1024,128]{1,0:T(8,128)S(1)}, f32[64,1024]{1,0:T(8,128)S(1)}, f32[64,1024]{1,0:T(8,128)S(1)}) custom-call(bf16[64,24,128]{2,1,0:T(8,128)(2,1)S(1)} %all_to_all.15.got_ref, bf16[64,1024]{1,0:T(8,128)(2,1)} %q_ref.3, bf16[64,1024]{1,0:T(8,128)(2,1)} %k_ref.3, ...), custom_call_target="tpu_custom_call" | custom-call | flops 268435456 | bytes 786432 | tf_op jit(solution)/shard_map/pallas_call | solution.py:305
  45.0 6.1 %all-to-all-done.1.kv_ref = bf16[8,256,128]{2,1,0:T(8,128)(2,1)S(1)} async-done(((bf16[8,256,128]{2,1,0:T(8,128)(2,1)}), bf16[8,256,128]{2,1,0:T(8,128)(2,1)S(1)}, u32[]{:S(2)}, u32[]{:S(2)}) %all-to-all-start.1) | async-done | bytes 524320 | tf_op jit(solution)/shard_map/all_to_all | solution.py:346
  51.1 1.1 %shard_map.40 = bf16[64,5,2,128]{3,2,1,0:T(2,128)(2,1)S(1)} custom-call(bf16[256,128]{1,0:T(8,128)(2,1)S(1)} %get-tuple-element.10.q_ref, bf16[8,256,128]{2,1,0:T(8,128)(2,1)S(1)} %all-to-all-done.1.kv_ref, f32[1040,128]{1,0:T(8,128)S(1)} %get-tuple-element.11.state_ref, f32[1024,128]{1,0:T(8,128)S(1)} %get-tuple-element.12.base_ref), custom_call_target="tpu_custom_call" | custom-call | flops 201326592 | bytes 1646592 | tf_op jit(solution)/shard_map/pallas_call | solution.py:305
  52.2 18.4 %all_to_all.16.got_ref = bf16[64,5,2,128]{3,2,1,0:T(2,128)(2,1)S(1)} all-to-all(bf16[64,5,2,128]{3,2,1,0:T(2,128)(2,1)S(1)} %shard_map.40), channel_id=1, replica_groups={{0,1,2,3,4,5,6,7,8,9,10,11,12,13,14,15,16,17,18,19,20,21,22,23,24,25,26..., dimensions={0} | all-to-all | bytes 327680 | tf_op jit(solution)/shard_map/all_to_all | solution.py:369
  70.6 1.2 %shard_map.41 = f32[64,1024]{1,0:T(8,128)} custom-call(bf16[64,5,2,128]{3,2,1,0:T(2,128)(2,1)S(1)} %all_to_all.16.got_ref, f32[64,1024]{1,0:T(8,128)S(1)} %get-tuple-element.13.near_out_ref, f32[64,1024]{1,0:T(8,128)S(1)} %get-tuple-element.14.near_lse_ref), custom_call_target="tpu_custom_call" | custom-call | bytes 688128 | tf_op jit(solution)/shard_map/pallas_call | solution.py:305
Async XLA Ops:
  36.2 14.8 %all-to-all-start.1 = ((bf16[8,256,128]{2,1,0:T(8,128)(2,1)}), bf16[8,256,128]{2,1,0:T(8,128)(2,1)S(1)}, u32[]{:S(2)}, u32[]{:S(2)}) async-start(bf16[8,256,128]{2,1,0:T(8,128)(2,1)} %shard_map.39), calls=%async_computation.1 | async-start | bytes 1048576 | tf_op jit(solution)/shard_map/all_to_all | solution.py:346

commit v11 on v10

--- a/solution.py
+++ b/solution.py
@@ -36,7 +36,8 @@
 
 
 def one_hot(shape, row_of, col_of):
-    return (row_of(iota(shape, 0)) == col_of(iota(shape, 1))).astype(F32).astype(BF16)
+    rows, cols = row_of(iota((shape[0], 1), 0)), col_of(iota((1, shape[1]), 1))
+    return (rows == cols).astype(F32).astype(BF16)
 
 
 def by_class(r):
@@ -232,11 +233,11 @@
     band, group = place()
     first = kv_ref[:, :FAR, :].reshape(HALF * FAR, LANES)
     second = kv_ref[:, FAR:, :].reshape(HALF * FAR, LANES)
-    shape = (FAR, HALF * FAR)
-    allowed = far_rank(iota(shape, 1)) <= group * FAR + far_rank(iota(shape, 0))
+    keys, mine = iota((1, HALF * FAR), 1), far_rank(iota((FAR, 1), 0))
+    allowed = far_rank(keys) <= group * FAR + mine
     over_first = dot_t(q_ref[...], first)
-    late_rank = far_rank(iota(shape, 1) ^ (HALF // 2 * FAR))
-    allowed_late = late_rank <= (group ^ (HALF // 2)) * FAR + far_rank(iota(shape, 0))
+    late_rank = far_rank(keys ^ (HALF // 2 * FAR))
+    allowed_late = late_rank <= (group ^ (HALF // 2)) * FAR + mine
     over_second = jnp.where(allowed_late, dot_t(q_ref[FAR:, :], second), FLOOR)
     early = softmax_out(jnp.where(allowed, over_first[:FAR], FLOOR), first)
     late_first = over_first[FAR:]

time: 72.1 us -> 72.1 us (level)
  no operation moved by 1% of the time
where the time goes in v11:
time: 72.1 us; the launch traced here: 71.8 us
  blocking collectives  51.9 us (72%)
  Pallas kernels  7.84 us (11%)
  waiting for transfers between devices  6.11 us (8%)
  starting transfers between devices  5.88 us (8%)
    all_to_all x1, blocking collectives, on_device(): lax.all_to_all(packed, ('outer', 'inner'), 0, 0, tiled=True, axis_index_g...  33.6 us
    all_to_all x1, blocking collectives, on_device(): lax.all_to_all(back, ('outer', 'inner'), 0, 0, tiled=True, axis_index_gro...  18.4 us
    pallas_call x5, Pallas kernels, call(): pl.pallas_call(kernel, out_shape=shapes, in_specs=in_specs, out_specs=[s...  7.84 us
    all_to_all x1, waiting for transfers between devices, on_device(): lax.all_to_all(far_kv, 'outer', 0, 0, tiled=True, axis_index_groups=halves)  6.11 us
    all_to_all x1, starting transfers between devices, on_device(): lax.all_to_all(far_kv, 'outer', 0, 0, tiled=True, axis_index_groups=halves)  5.88 us
  transfers between devices with their start and end apart: 1, of which 1 were waited for; matrix products, arithmetic and copies ran while one was open for 0% of the time, Pallas kernels for 4%

profile of v11, /device:TPU:1, one launch (start us, length us, event | category | flops | bytes accessed | tf_op | source)
XLA Modules:
  0.0 71.8 jit_solution(5085563040094097877)
XLA Ops:
  0.0 1.5 %shard_map.37 = bf16[64,24,128]{2,1,0:T(8,128)(2,1)S(1)} custom-call(bf16[64,1024]{1,0:T(8,128)(2,1)} %q_ref.3, bf16[64,1024]{1,0:T(8,128)(2,1)} %k_ref.3, bf16[64,1024]{1,0:T(8,128)(2,1)} %v_ref.3), custom_call_target="tpu_custom_call" | custom-call | bytes 393216 | tf_op jit(solution)/shard_map/pallas_call | solution.py:306
  1.5 33.6 %all_to_all.15.got_ref = bf16[64,24,128]{2,1,0:T(8,128)(2,1)S(1)} all-to-all(bf16[64,24,128]{2,1,0:T(8,128)(2,1)S(1)} %shard_map.37), channel_id=1, replica_groups={{0,1,2,3,4,5,6,7,8,9,10,11,12,13,14,15,16,17,18,19,20,21,22,23,24,25,26..., dimensions={0} | all-to-all | bytes 786432 | tf_op jit(solution)/shard_map/all_to_all | solution.py:338
  35.1 1.1 %shard_map.39 = bf16[8,256,128]{2,1,0:T(8,128)(2,1)} custom-call(bf16[64,24,128]{2,1,0:T(8,128)(2,1)S(1)} %all_to_all.15.got_ref), custom_call_target="tpu_custom_call" | custom-call | bytes 393216 | tf_op jit(solution)/shard_map/pallas_call | solution.py:306
  36.2 5.9 %all-to-all-start.1 = ((bf16[8,256,128]{2,1,0:T(8,128)(2,1)}), bf16[8,256,128]{2,1,0:T(8,128)(2,1)S(1)}, u32[]{:S(2)}, u32[]{:S(2)}) async-start(bf16[8,256,128]{2,1,0:T(8,128)(2,1)} %shard_map.39), calls=%async_computation.1 | async-start | bytes 1048576 | tf_op jit(solution)/shard_map/all_to_all | solution.py:347
  42.1 2.9 %shard_map.38 = (bf16[256,128]{1,0:T(8,128)(2,1)S(1)}, f32[1040,128]{1,0:T(8,128)S(1)}, f32[1024,128]{1,0:T(8,128)S(1)}, f32[64,1024]{1,0:T(8,128)S(1)}, f32[64,1024]{1,0:T(8,128)S(1)}) custom-call(bf16[64,24,128]{2,1,0:T(8,128)(2,1)S(1)} %all_to_all.15.got_ref, bf16[64,1024]{1,0:T(8,128)(2,1)} %q_ref.3, bf16[64,1024]{1,0:T(8,128)(2,1)} %k_ref.3, ...), custom_call_target="tpu_custom_call" | custom-call | flops 268435456 | bytes 786432 | tf_op jit(solution)/shard_map/pallas_call | solution.py:306
  45.0 6.1 %all-to-all-done.1.kv_ref = bf16[8,256,128]{2,1,0:T(8,128)(2,1)S(1)} async-done(((bf16[8,256,128]{2,1,0:T(8,128)(2,1)}), bf16[8,256,128]{2,1,0:T(8,128)(2,1)S(1)}, u32[]{:S(2)}, u32[]{:S(2)}) %all-to-all-start.1) | async-done | bytes 524320 | tf_op jit(solution)/shard_map/all_to_all | solution.py:347
  51.1 1.1 %shard_map.40 = bf16[64,5,2,128]{3,2,1,0:T(2,128)(2,1)S(1)} custom-call(bf16[256,128]{1,0:T(8,128)(2,1)S(1)} %get-tuple-element.10.q_ref, bf16[8,256,128]{2,1,0:T(8,128)(2,1)S(1)} %all-to-all-done.1.kv_ref, f32[1040,128]{1,0:T(8,128)S(1)} %get-tuple-element.11.state_ref, f32[1024,128]{1,0:T(8,128)S(1)} %get-tuple-element.12.base_ref), custom_call_target="tpu_custom_call" | custom-call | flops 201326592 | bytes 1646592 | tf_op jit(solution)/shard_map/pallas_call | solution.py:306
  52.2 18.4 %all_to_all.16.got_ref = bf16[64,5,2,128]{3,2,1,0:T(2,128)(2,1)S(1)} all-to-all(bf16[64,5,2,128]{3,2,1,0:T(2,128)(2,1)S(1)} %shard_map.40), channel_id=1, replica_groups={{0,1,2,3,4,5,6,7,8,9,10,11,12,13,14,15,16,17,18,19,20,21,22,23,24,25,26..., dimensions={0} | all-to-all | bytes 327680 | tf_op jit(solution)/shard_map/all_to_all | solution.py:370
  70.6 1.2 %shard_map.41 = f32[64,1024]{1,0:T(8,128)} custom-call(bf16[64,5,2,128]{3,2,1,0:T(2,128)(2,1)S(1)} %all_to_all.16.got_ref, f32[64,1024]{1,0:T(8,128)S(1)} %get-tuple-element.13.near_out_ref, f32[64,1024]{1,0:T(8,128)S(1)} %get-tuple-element.14.near_lse_ref), custom_call_target="tpu_custom_call" | custom-call | bytes 688128 | tf_op jit(solution)/shard_map/pallas_call | solution.py:306
Async XLA Ops:
  36.2 14.8 %all-to-all-start.1 = ((bf16[8,256,128]{2,1,0:T(8,128)(2,1)}), bf16[8,256,128]{2,1,0:T(8,128)(2,1)S(1)}, u32[]{:S(2)}, u32[]{:S(2)}) async-start(bf16[8,256,128]{2,1,0:T(8,128)(2,1)} %shard_map.39), calls=%async_computation.1 | async-start | bytes 1048576 | tf_op jit(solution)/shard_map/all_to_all | solution.py:347

commit v12 on v11

--- a/solution.py
+++ b/solution.py
@@ -195,12 +195,13 @@
     k_ref,
     v_ref,
     far_q_ref,
-    state_ref,
+    far_mid_ref,
     base_ref,
     near_out_ref,
     near_lse_ref,
     held,
     sems,
+    state_ref,
 ):
     copies = copies_in((q_ref, k_ref, v_ref), held, sems)
     pick = far_rows(place()[0])
@@ -223,12 +224,17 @@
                 packed.append(beside_right(x[:, :EIGHT], x[:, EIGHT:]))
             packed = jnp.concatenate([packed[0], own_column(packed[1])], axis=1)
             base_ref[at : at + block, :] = packed.reshape(block, LANES)
+    for at in range(FOLD):
+        for lot in range(4):
+            rows = pl.ds(at * CLASS + place()[0] + 4 * lot, INNER, stride=ROWS)
+            to = at * FAR + lot * INNER
+            far_mid_ref[to : to + INNER, :] = state_ref[rows, :]
     for copy in copies:
         copy.wait()
     near_level(held.at[0], held.at[1], held.at[2], near_out_ref, near_lse_ref)
 
 
-def far_kernel(q_ref, kv_ref, state_ref, base_ref, back_ref, fresh):
+def far_kernel(q_ref, kv_ref, far_mid_ref, base_ref, back_ref, fresh):
     fresh[: FOLD * CLASS, :] = base_ref[...]
     band, group = place()
     first = kv_ref[:, :FAR, :].reshape(HALF * FAR, LANES)
@@ -250,9 +256,7 @@
     late = (summed / total, top + jnp.log(total))
     for at, (far_out, far_lse) in enumerate((early, late)):
         start = at * CLASS + band
-        mid = jnp.concatenate(
-            [state_ref[pl.ds(start + 4 * lot, INNER, stride=ROWS), :] for lot in range(4)], axis=0
-        )
+        mid = far_mid_ref[at * FAR : (at + 1) * FAR, :]
         out, lse = merge(mid, swap(mid), far_out, jnp.broadcast_to(far_lse, far_out.shape))
         column = iota((INNER, LANES), 1) % 16
         for x, down in ((out, 0), (lse_parts(lse), EIGHT)):
@@ -350,14 +354,14 @@
         [(got, VMEM), *own],
         [
             ((FOLD * FAR, LANES), BF16, VMEM),
-            (spare, F32, VMEM),
+            ((FOLD * FAR, LANES), F32, VMEM),
             (tall, F32, VMEM),
             (full, F32, VMEM),
             (full, F32, VMEM),
         ],
         flops=4 * 2 * 512 * 512 * 128,
         exps=2 * 512 * 512,
-        scratch=held,
+        scratch=[*held, pltpu.VMEM(spare, F32)],
     )
     (back,) = call(
         far_kernel,

time: 72.1 us -> 72.1 us (level)
  waiting for transfers between devices: 6.11 us -> 5.12 us
  Pallas kernels: 7.84 us -> 8.79 us
    all_to_all x1, waiting for transfers between devices: 6.11 us -> 5.12 us  [on_device(): lax.all_to_all(far_kv, 'outer', 0, 0, tiled=True, axis_index_groups=halves)]
    pallas_call x5, Pallas kernels: 7.84 us -> 8.79 us  [call(): pl.pallas_call(kernel, out_shape=shapes, in_specs=in_specs, out_specs=[s...]
  transfers between devices with their start and end apart: 1 -> 1, of which waited for: 1 -> 1; matrix products, arithmetic and copies ran while one was open for 0% -> 0% of each run, Pallas kernels for 4% -> 5%
where the time goes in v12:
time: 72.1 us; the launch traced here: 71.8 us
  blocking collectives  52 us (72%)
  Pallas kernels  8.79 us (12%)
  starting transfers between devices  5.88 us (8%)
  waiting for transfers between devices  5.12 us (7%)
    all_to_all x1, blocking collectives, on_device(): lax.all_to_all(packed, ('outer', 'inner'), 0, 0, tiled=True, axis_index_g...  33.6 us
    all_to_all x1, blocking collectives, on_device(): lax.all_to_all(back, ('outer', 'inner'), 0, 0, tiled=True, axis_index_gro...  18.4 us
    pallas_call x5, Pallas kernels, call(): pl.pallas_call(kernel, out_shape=shapes, in_specs=in_specs, out_specs=[s...  8.79 us
    all_to_all x1, starting transfers between devices, on_device(): lax.all_to_all(far_kv, 'outer', 0, 0, tiled=True, axis_index_groups=halves)  5.88 us
    all_to_all x1, waiting for transfers between devices, on_device(): lax.all_to_all(far_kv, 'outer', 0, 0, tiled=True, axis_index_groups=halves)  5.12 us
  transfers between devices with their start and end apart: 1, of which 1 were waited for; matrix products, arithmetic and copies ran while one was open for 0% of the time, Pallas kernels for 5%

profile of v12, /device:TPU:1, one launch (start us, length us, event | category | flops | bytes accessed | tf_op | source)
XLA Modules:
  0.0 71.8 jit_solution(2393414360413172603)
XLA Ops:
  0.0 1.5 %shard_map.37 = bf16[64,24,128]{2,1,0:T(8,128)(2,1)S(1)} custom-call(bf16[64,1024]{1,0:T(8,128)(2,1)} %q_ref.3, bf16[64,1024]{1,0:T(8,128)(2,1)} %k_ref.3, bf16[64,1024]{1,0:T(8,128)(2,1)} %v_ref.3), custom_call_target="tpu_custom_call" | custom-call | bytes 393216 | tf_op jit(solution)/shard_map/pallas_call | solution.py:310
  1.5 33.6 %all_to_all.15.got_ref = bf16[64,24,128]{2,1,0:T(8,128)(2,1)S(1)} all-to-all(bf16[64,24,128]{2,1,0:T(8,128)(2,1)S(1)} %shard_map.37), channel_id=1, replica_groups={{0,1,2,3,4,5,6,7,8,9,10,11,12,13,14,15,16,17,18,19,20,21,22,23,24,25,26..., dimensions={0} | all-to-all | bytes 786432 | tf_op jit(solution)/shard_map/all_to_all | solution.py:342
  35.1 1.1 %shard_map.39 = bf16[8,256,128]{2,1,0:T(8,128)(2,1)} custom-call(bf16[64,24,128]{2,1,0:T(8,128)(2,1)S(1)} %all_to_all.15.got_ref), custom_call_target="tpu_custom_call" | custom-call | bytes 393216 | tf_op jit(solution)/shard_map/pallas_call | solution.py:310
  36.2 5.9 %all-to-all-start.1 = ((bf16[8,256,128]{2,1,0:T(8,128)(2,1)}), bf16[8,256,128]{2,1,0:T(8,128)(2,1)S(1)}, u32[]{:S(2)}, u32[]{:S(2)}) async-start(bf16[8,256,128]{2,1,0:T(8,128)(2,1)} %shard_map.39), calls=%async_computation.1 | async-start | bytes 1048576 | tf_op jit(solution)/shard_map/all_to_all | solution.py:351
  42.1 3.8 %shard_map.38 = (bf16[256,128]{1,0:T(8,128)(2,1)S(1)}, f32[256,128]{1,0:T(8,128)S(1)}, f32[1024,128]{1,0:T(8,128)S(1)}, f32[64,1024]{1,0:T(8,128)S(1)}, f32[64,1024]{1,0:T(8,128)S(1)}) custom-call(bf16[64,24,128]{2,1,0:T(8,128)(2,1)S(1)} %all_to_all.15.got_ref, bf16[64,1024]{1,0:T(8,128)(2,1)} %q_ref.3, bf16[64,1024]{1,0:T(8,128)(2,1)} %k_ref.3, ...), custom_call_target="tpu_custom_call" | custom-call | flops 268435456 | bytes 786432 | tf_op jit(solution)/shard_map/pallas_call | solution.py:310
  45.9 5.1 %all-to-all-done.1.kv_ref = bf16[8,256,128]{2,1,0:T(8,128)(2,1)S(1)} async-done(((bf16[8,256,128]{2,1,0:T(8,128)(2,1)}), bf16[8,256,128]{2,1,0:T(8,128)(2,1)S(1)}, u32[]{:S(2)}, u32[]{:S(2)}) %all-to-all-start.1) | async-done | bytes 524320 | tf_op jit(solution)/shard_map/all_to_all | solution.py:351
  51.1 1.1 %shard_map.40 = bf16[64,5,2,128]{3,2,1,0:T(2,128)(2,1)S(1)} custom-call(bf16[256,128]{1,0:T(8,128)(2,1)S(1)} %get-tuple-element.10.q_ref, bf16[8,256,128]{2,1,0:T(8,128)(2,1)S(1)} %all-to-all-done.1.kv_ref, f32[256,128]{1,0:T(8,128)S(1)} %get-tuple-element.11.far_mid_ref, f32[1024,128]{1,0:T(8,128)S(1)} %get-tuple-element.12.base_ref), custom_call_target="tpu_custom_call" | custom-call | flops 201326592 | bytes 1245184 | tf_op jit(solution)/shard_map/pallas_call | solution.py:310
  52.2 18.4 %all_to_all.16.got_ref = bf16[64,5,2,128]{3,2,1,0:T(2,128)(2,1)S(1)} all-to-all(bf16[64,5,2,128]{3,2,1,0:T(2,128)(2,1)S(1)} %shard_map.40), channel_id=1, replica_groups={{0,1,2,3,4,5,6,7,8,9,10,11,12,13,14,15,16,17,18,19,20,21,22,23,24,25,26..., dimensions={0} | all-to-all | bytes 327680 | tf_op jit(solution)/shard_map/all_to_all | solution.py:374
  70.6 1.2 %shard_map.41 = f32[64,1024]{1,0:T(8,128)} custom-call(bf16[64,5,2,128]{3,2,1,0:T(2,128)(2,1)S(1)} %all_to_all.16.got_ref, f32[64,1024]{1,0:T(8,128)S(1)} %get-tuple-element.13.near_out_ref, f32[64,1024]{1,0:T(8,128)S(1)} %get-tuple-element.14.near_lse_ref), custom_call_target="tpu_custom_call" | custom-call | bytes 688128 | tf_op jit(solution)/shard_map/pallas_call | solution.py:310
Async XLA Ops:
  36.2 14.8 %all-to-all-start.1 = ((bf16[8,256,128]{2,1,0:T(8,128)(2,1)}), bf16[8,256,128]{2,1,0:T(8,128)(2,1)S(1)}, u32[]{:S(2)}, u32[]{:S(2)}) async-start(bf16[8,256,128]{2,1,0:T(8,128)(2,1)} %shard_map.39), calls=%async_computation.1 | async-start | bytes 1048576 | tf_op jit(solution)/shard_map/all_to_all | solution.py:351
